TPU v7x, 32 devices: a whole 2x2x4 slice. The times are simulated.
32 devices in a mesh: dp: 8 (over y, x, core), shard: 4 (over z).
Axes of the slice: x: 2, y: 2, z: 4, core: 2. Of those that a mesh axis runs over, the one named last changes fastest.
Arguments:
- tokens: bfloat16 [4096, 2048], P(('dp', 'shard')), may hold values from -6 to 6
- cotangent: bfloat16 [4096, 2048], P(('dp', 'shard')), may hold values from -6 to 6
- gain_first: bfloat16 [2048], replicated, may hold values from 0.5 to 1.5
- gain_second: bfloat16 [2048], replicated, may hold values from 0.5 to 1.5
- router_attn: bfloat16 [2048, 8], replicated, may hold values from -0.09375 to 0.09375
- router_mlp: bfloat16 [2048, 8], replicated, may hold values from -0.09375 to 0.09375
- query_w: bfloat16 [8, 2048, 2048], P(None, None, 'shard'), may hold values from -0.125 to 0.125
- key_w: bfloat16 [2048, 2048], P(None, 'shard'), may hold values from -0.125 to 0.125
- value_w: bfloat16 [2048, 2048], P(None, 'shard'), may hold values from -0.125 to 0.125
- output_w: bfloat16 [8, 2048, 2048], P(None, 'shard'), may hold values from -0.75 to 0.75
- gate_w: bfloat16 [2048, 45056], P(None, 'dp'), may hold values from -0.125 to 0.125
- up_w: bfloat16 [2048, 45056], P(None, 'dp'), may hold values from -0.125 to 0.125
- down_w: bfloat16 [45056, 2048], P('dp'), may hold values from -0.078125 to 0.078125
- query_a: bfloat16 [8, 8, 2048, 16], replicated, may hold values from -0.125 to 0.125
- query_b: bfloat16 [8, 8, 16, 2048], P(None, None, None, 'shard'), may hold values from -0.75 to 0.75
- key_a: bfloat16 [8, 2048, 16], replicated, may hold values from -0.125 to 0.125
- key_b: bfloat16 [8, 16, 2048], P(None, None, 'shard'), may hold values from -0.75 to 0.75
- value_a: bfloat16 [8, 2048, 16], replicated, may hold values from -0.125 to 0.125
- value_b: bfloat16 [8, 16, 2048], P(None, None, 'shard'), may hold values from -0.75 to 0.75
- output_a: bfloat16 [8, 8, 2048, 16], P(None, None, 'shard'), may hold values from -0.75 to 0.75
- output_b: bfloat16 [8, 8, 16, 2048], replicated, may hold values from -0.75 to 0.75
- gate_a: bfloat16 [8, 8, 2048, 16], replicated, may hold values from -0.125 to 0.125
- gate_b: bfloat16 [8, 16, 45056], P(None, None, 'dp'), may hold values from -0.75 to 0.75
- up_a: bfloat16 [8, 8, 2048, 16], replicated, may hold values from -0.125 to 0.125
- up_b: bfloat16 [8, 16, 45056], P(None, None, 'dp'), may hold values from -0.75 to 0.75
- down_a: bfloat16 [8, 45056, 16], P(None, 'dp'), may hold values from -0.078125 to 0.078125
- down_b: bfloat16 [8, 8, 16, 2048], replicated, may hold values from -0.75 to 0.75
- adapter_ids: int32 [8], replicated, may hold values from 0 to 7
- attn_routes: int32 [4096, 2], P('dp'), may hold values from 0 to 7, all different within a row; in each aligned block of 512 rows (0 to 511, 512 to 1023, ...) at most 160 rows name the same one
- mlp_routes: int32 [4096, 2], P(('dp', 'shard')), may hold values from 0 to 7, all different within a row; in each aligned block of 128 rows (0 to 127, 128 to 255, ...) at most 40 rows name the same one
Outputs:
- layer_out: bfloat16 [4096, 2048], P(('dp', 'shard'))
- input_grad: float32 [4096, 2048], P(('dp', 'shard'))
- grad_query_a: float32 [8, 8, 2048, 16], P(None, None, ('dp', 'shard'))
- grad_query_b: float32 [8, 8, 16, 2048], P(None, None, 'dp', 'shard')
- grad_key_a: float32 [8, 2048, 16], P(None, ('dp', 'shard'))
- grad_key_b: float32 [8, 16, 2048], P(None, 'dp', 'shard')
- grad_value_a: float32 [8, 2048, 16], P(None, ('dp', 'shard'))
- grad_value_b: float32 [8, 16, 2048], P(None, 'dp', 'shard')
- grad_output_a: float32 [8, 8, 2048, 16], P(None, None, 'shard', 'dp')
- grad_output_b: float32 [8, 8, 16, 2048], P(None, None, None, ('dp', 'shard'))
- grad_gate_a: float32 [8, 8, 2048, 16], P(None, None, ('dp', 'shard'))
- grad_gate_b: float32 [8, 16, 45056], P(None, None, ('dp', 'shard'))
- grad_up_a: float32 [8, 8, 2048, 16], P(None, None, ('dp', 'shard'))
- grad_up_b: float32 [8, 16, 45056], P(None, None, ('dp', 'shard'))
- grad_down_a: float32 [8, 45056, 16], P(None, ('dp', 'shard'))
- grad_down_b: float32 [8, 8, 16, 2048], P(None, None, None, ('dp', 'shard'))
Inputs may be any that keep to these rules, and one draw needn't show every extreme that they name: `attn_routes`: each row names two different experts. In the 512 rows of one sequence no expert is named by more than 160 rows, and in some sequence one is named by exactly 160 rows. `mlp_routes`: each row names two different experts. In the 128 rows of one device no expert is named by more than 40 rows, and on some device one is named by exactly 40 rows.
All inputs are finite; a program needn't handle non-finite values.
Results may differ from a plain program's by a relative error of at most 0.024.
Values may be sent and summed in bfloat16 or wider, within the bound.
No kernel may reach another device: no remote copies, remote signals or barrier semaphores. Data moves between devices by JAX's collectives and lax.ppermute only.
A program may use at most 576 MiB of HBM per device.

v0:
```python
import math

import jax
import jax.numpy as jnp
from jax import lax
from jax.sharding import PartitionSpec as P

D = 2048
HD = 128
EXPERTS = 8
ATT_EXPERTS = 8
ADAPTERS = 8
RANK = 16


precise = lax.Precision.HIGHEST
eps = 1e-05


def inverse_rms(values):
    return lax.rsqrt(jnp.mean(values * values, axis=-1, keepdims=True) + eps)


def rotary_tables(positions, head_width):
    half_width = head_width // 2
    freq_table = jnp.exp(
        jnp.arange(half_width, dtype=jnp.float32) * (-2.0 * math.log(10000.0) / head_width)
    )
    angles = positions.astype(jnp.float32)[..., None] * freq_table
    return (jnp.cos(angles), jnp.sin(angles))


def rotate(values, cosine_table, sine_table):
    half_width = values.shape[-1] // 2
    first_half = values[..., :half_width]
    second_half = values[..., half_width:]
    return jnp.concatenate(
        [
            first_half * cosine_table - second_half * sine_table,
            second_half * cosine_table + first_half * sine_table,
        ],
        axis=-1,
    )


def unrotate(values, cosine_table, sine_table):
    half_width = values.shape[-1] // 2
    first_half = values[..., :half_width]
    second_half = values[..., half_width:]
    return jnp.concatenate(
        [
            first_half * cosine_table + second_half * sine_table,
            second_half * cosine_table - first_half * sine_table,
        ],
        axis=-1,
    )


def pair_gates(logits, routes):
    chosen = jnp.take_along_axis(logits, routes, axis=1)
    peak_logit = jnp.max(chosen, axis=1, keepdims=True)
    weights = jnp.exp(chosen - peak_logit)
    return weights / jnp.sum(weights, axis=1, keepdims=True)


def gate_backward(gate_values, grad_gates):
    return gate_values * (grad_gates - jnp.sum(gate_values * grad_gates, axis=1, keepdims=True))


def norm_backward(values, inverse, gain_vector, grad_normed):
    weighted = gain_vector.astype(jnp.float32) * grad_normed
    return inverse * weighted - values * inverse**3 * jnp.mean(
        values * weighted, axis=-1, keepdims=True
    )


def slot_table(routes, expert_count, capacity):
    choose = (routes[:, :, None] == jnp.arange(expert_count, dtype=jnp.int32)).astype(jnp.int32)
    member = jnp.sum(choose, axis=1)
    slot_numbers = jnp.cumsum(member, axis=0) - member
    target = jnp.where(member > 0, slot_numbers, capacity)
    token_ids = jnp.broadcast_to(
        jnp.arange(routes.shape[0], dtype=jnp.int32)[:, None], member.shape
    )
    expert_ids = jnp.broadcast_to(jnp.arange(expert_count, dtype=jnp.int32)[None, :], member.shape)
    token_table = (
        jnp.zeros((expert_count, capacity), jnp.int32)
        .at[expert_ids, target]
        .set(token_ids, mode="drop")
    )
    slot_valid = jnp.arange(capacity, dtype=jnp.int32)[None, :] < jnp.sum(member, axis=0)[:, None]
    pair_slots = jnp.take_along_axis(slot_numbers, routes, axis=1)
    return (token_table, slot_valid, pair_slots, choose.astype(jnp.float32))


def place_adapter(partial_grad, insert_axis, adapter_pick):
    expanded = jnp.expand_dims(partial_grad, insert_axis)
    pick_shape = [1] * expanded.ndim
    pick_shape[insert_axis] = adapter_pick.shape[0]
    return expanded * adapter_pick.reshape(pick_shape)


def on_device(
    tokens,
    cotangent,
    gain_first,
    gain_second,
    router_attn,
    router_mlp,
    query_w,
    key_w,
    value_w,
    output_w,
    gate_w,
    up_w,
    down_w,
    query_a,
    query_b,
    key_a,
    key_b,
    value_a,
    value_b,
    output_a,
    output_b,
    gate_a,
    gate_b,
    up_a,
    up_b,
    down_a,
    down_b,
    adapter_ids,
    attn_routes,
    mlp_routes,
):
    shard_count = lax.axis_size("shard")
    group_count = lax.axis_size("dp")
    tok_rows = tokens.shape[0]
    seq_len = tok_rows * shard_count
    cap_att = seq_len // 4 + seq_len // 16
    cap_mlp = tok_rows // 4 + tok_rows // 16
    slice_count = group_count // EXPERTS
    ff_local = gate_w.shape[1]
    width_local = key_w.shape[1]
    heads_local = width_local // HD
    adapter_now = adapter_ids[lax.axis_index("dp")]
    first_row = lax.axis_index("shard") * tok_rows
    score_scale = HD ** (-0.5)
    adapter_pick = (jnp.arange(ADAPTERS, dtype=jnp.int32) == adapter_now).astype(jnp.float32)
    key_w_heads = key_w.reshape(D, heads_local, HD)
    value_w_heads = value_w.reshape(D, heads_local, HD)
    query_w_heads = query_w.reshape(ATT_EXPERTS, D, heads_local, HD)
    output_w_heads = output_w.reshape(ATT_EXPERTS, heads_local, HD, D)
    inputs = tokens.astype(jnp.float32)
    inverse_first = inverse_rms(inputs)
    normed = (inputs * inverse_first * gain_first.astype(jnp.float32)).astype(jnp.bfloat16)
    normed_all = lax.all_gather(normed, "shard", axis=0, tiled=True)
    attn_gates = pair_gates(
        jnp.dot(normed_all, router_attn, preferred_element_type=jnp.float32), attn_routes
    )
    attn_table, attn_valid, attn_slots, attn_choose = slot_table(attn_routes, ATT_EXPERTS, cap_att)
    gate_by_expert = jnp.sum(attn_gates[:, :, None] * attn_choose, axis=1)
    expert_range = jnp.arange(ATT_EXPERTS, dtype=jnp.int32)[:, None]
    attn_weight = jnp.where(attn_valid, gate_by_expert[attn_table, expert_range], 0.0)
    positions = jnp.arange(seq_len, dtype=jnp.int32)
    key_cos, key_sin = rotary_tables(positions, HD)
    key_first = key_a[adapter_now]
    key_second = key_b[adapter_now]
    value_first = value_a[adapter_now]
    value_second = value_b[adapter_now]
    key_second_heads = key_second.reshape(RANK, heads_local, HD)
    value_second_heads = value_second.reshape(RANK, heads_local, HD)
    key_low = jnp.dot(normed_all, key_first, preferred_element_type=jnp.float32)
    key_pre = jnp.einsum(
        "sd,dhj->hsj", normed_all, key_w_heads, preferred_element_type=jnp.float32
    ) + jnp.einsum("sr,rhj->hsj", key_low, key_second_heads.astype(jnp.float32), precision=precise)
    key_rows = rotate(key_pre, key_cos, key_sin).astype(jnp.bfloat16)
    value_low = jnp.dot(normed_all, value_first, preferred_element_type=jnp.float32)
    value_pre = jnp.einsum(
        "sd,dhj->hsj", normed_all, value_w_heads, preferred_element_type=jnp.float32
    ) + jnp.einsum(
        "sr,rhj->hsj", value_low, value_second_heads.astype(jnp.float32), precision=precise
    )
    value_rows = value_pre.astype(jnp.bfloat16)
    query_rows = normed_all[attn_table]
    query_first = query_a[:, adapter_now]
    query_second = query_b[:, adapter_now]
    query_second_heads = query_second.reshape(ATT_EXPERTS, RANK, heads_local, HD)
    query_low = jnp.einsum(
        "ecd,edr->ecr", query_rows, query_first, preferred_element_type=jnp.float32
    )
    query_pre = jnp.einsum(
        "ecd,edhj->ehcj", query_rows, query_w_heads, preferred_element_type=jnp.float32
    ) + jnp.einsum(
        "ecr,erhj->ehcj", query_low, query_second_heads.astype(jnp.float32), precision=precise
    )
    query_cos, query_sin = rotary_tables(attn_table, HD)
    query_cos = query_cos[:, None]
    query_sin = query_sin[:, None]
    queries = rotate(query_pre, query_cos, query_sin).astype(jnp.bfloat16)

    def scores_for(query_block, query_pos):
        raw_scores = (
            jnp.einsum("hqd,hkd->hqk", query_block, key_rows, preferred_element_type=jnp.float32)
            * score_scale
        )
        allowed = positions[None, None, :] <= query_pos[None, :, None]
        return jnp.where(allowed, raw_scores, -1e30)

    def attend(block_items):
        query_block, query_pos = block_items
        scores = scores_for(query_block, query_pos)
        peak_score = jnp.max(scores, axis=-1, keepdims=True)
        exp_scores = jnp.exp(scores - peak_score)
        total_weight = jnp.sum(exp_scores, axis=-1, keepdims=True)
        probabilities = (exp_scores / total_weight).astype(jnp.bfloat16)
        mixed = jnp.einsum(
            "hqk,hkd->hqd", probabilities, value_rows, preferred_element_type=jnp.float32
        ).astype(jnp.bfloat16)
        return (mixed, peak_score[..., 0] + jnp.log(total_weight[..., 0]))

    mixed_heads, log_totals = lax.map(attend, (queries, attn_table))
    out_first = output_a[:, adapter_now]
    out_second = output_b[:, adapter_now]
    out_first_heads = out_first.reshape(ATT_EXPERTS, heads_local, HD, RANK)
    out_low = jnp.einsum(
        "ehcj,ehjr->ecr", mixed_heads, out_first_heads, preferred_element_type=jnp.float32
    )
    out_part = jnp.einsum(
        "ehcj,ehjd->ecd", mixed_heads, output_w_heads, preferred_element_type=jnp.float32
    ) + jnp.einsum("ecr,erd->ecd", out_low, out_second.astype(jnp.float32), precision=precise)
    attn_part = (
        jnp.zeros((seq_len, D), jnp.float32).at[attn_table].add(attn_weight[..., None] * out_part)
    )
    attn_local = lax.psum_scatter(
        attn_part.astype(jnp.bfloat16), "shard", scatter_dimension=0, tiled=True
    ).astype(jnp.float32)
    hidden_first = inputs + attn_local
    inverse_second = inverse_rms(hidden_first)
    mlp_in = (hidden_first * inverse_second * gain_second.astype(jnp.float32)).astype(jnp.bfloat16)
    mlp_gates = pair_gates(
        jnp.dot(mlp_in, router_mlp, preferred_element_type=jnp.float32), mlp_routes
    )
    mlp_table, mlp_valid, mlp_slots, mlp_choose = slot_table(mlp_routes, EXPERTS, cap_mlp)
    mlp_by_expert = jnp.sum(mlp_gates[:, :, None] * mlp_choose, axis=1)
    mlp_range = jnp.arange(EXPERTS, dtype=jnp.int32)[:, None]
    mlp_weight = jnp.where(mlp_valid, mlp_by_expert[mlp_table, mlp_range], 0.0)
    sent_rows = jnp.where(mlp_valid[..., None], mlp_in[mlp_table], jnp.zeros((), jnp.bfloat16))
    gate_first = gate_a[:, adapter_now]
    up_first = up_a[:, adapter_now]
    low_gate = jnp.einsum("td,edr->ter", mlp_in, gate_first, preferred_element_type=jnp.float32)
    low_up = jnp.einsum("td,edr->ter", mlp_in, up_first, preferred_element_type=jnp.float32)
    low_both = jnp.concatenate([low_gate, low_up], axis=-1)
    sent_low = jnp.where(mlp_valid[..., None], low_both[mlp_table, mlp_range], 0.0).astype(
        jnp.bfloat16
    )
    send_rows_all = jnp.repeat(sent_rows, slice_count, axis=0)
    send_low_all = jnp.repeat(sent_low, slice_count, axis=0)
    pick_source = (adapter_ids[:, None] == jnp.arange(ADAPTERS, dtype=jnp.int32)[None, :]).astype(
        jnp.float32
    )
    gate_table = gate_b.reshape(ADAPTERS * RANK, ff_local)
    up_table = up_b.reshape(ADAPTERS * RANK, ff_local)
    down_table = jnp.transpose(down_a, (1, 0, 2)).reshape(ff_local, ADAPTERS * RANK)

    def spread_low(low_part):
        expanded = pick_source[:, None, :, None] * low_part[:, :, None, :]
        return expanded.reshape(low_part.shape[0], low_part.shape[1], ADAPTERS * RANK).astype(
            jnp.bfloat16
        )

    def select_low(wide):
        split_wide = wide.reshape(wide.shape[0], wide.shape[1], ADAPTERS, RANK)
        return jnp.sum(split_wide * pick_source[:, None, :, None], axis=2)

    def expert_inner(recv_rows, recv_low):
        gate_wide = spread_low(recv_low[..., :RANK].astype(jnp.float32))
        up_wide = spread_low(recv_low[..., RANK:].astype(jnp.float32))
        gate_pre = jnp.einsum(
            "scd,df->scf", recv_rows, gate_w, preferred_element_type=jnp.float32
        ) + jnp.einsum("scq,qf->scf", gate_wide, gate_table, preferred_element_type=jnp.float32)
        up_pre = jnp.einsum(
            "scd,df->scf", recv_rows, up_w, preferred_element_type=jnp.float32
        ) + jnp.einsum("scq,qf->scf", up_wide, up_table, preferred_element_type=jnp.float32)
        return (gate_pre, up_pre, gate_wide, up_wide)

    recv_rows = lax.all_to_all(send_rows_all, "dp", split_axis=0, concat_axis=0, tiled=True)
    recv_low = lax.all_to_all(send_low_all, "dp", split_axis=0, concat_axis=0, tiled=True)
    gate_pre, up_pre, gate_wide, up_wide = expert_inner(recv_rows, recv_low)
    hidden_act = (jax.nn.silu(gate_pre) * up_pre).astype(jnp.bfloat16)
    main_out = jnp.einsum("scf,fd->scd", hidden_act, down_w, preferred_element_type=jnp.float32)
    down_low = select_low(
        jnp.einsum("scf,fq->scq", hidden_act, down_table, preferred_element_type=jnp.float32)
    )
    main_out, down_low, kept_rows, kept_low = (main_out, down_low, recv_rows, recv_low)
    returned = (
        lax.all_to_all(
            main_out.astype(jnp.bfloat16), "dp", split_axis=0, concat_axis=0, tiled=True
        ).astype(main_out.dtype),
        lax.all_to_all(
            down_low.astype(jnp.bfloat16), "dp", split_axis=0, concat_axis=0, tiled=True
        ).astype(down_low.dtype),
    )
    main_sum = jnp.sum(returned[0].reshape(EXPERTS, slice_count, cap_mlp, D), axis=1)
    low_sum = jnp.sum(returned[1].reshape(EXPERTS, slice_count, cap_mlp, RANK), axis=1)
    down_second = down_b[:, adapter_now].astype(jnp.float32)
    expert_out = main_sum + jnp.einsum("ecr,erd->ecd", low_sum, down_second, precision=precise)
    pair_out = expert_out[mlp_routes, mlp_slots]
    mlp_out = jnp.sum(mlp_gates[..., None] * pair_out, axis=1)
    layer_out = (hidden_first + mlp_out).astype(jnp.bfloat16)
    grad_out = cotangent.astype(jnp.float32)
    grad_pair_gate = jnp.sum(grad_out[:, None, :] * pair_out, axis=-1)
    grad_mlp_logits = gate_backward(mlp_gates, grad_pair_gate)
    grad_mlp_cols = jnp.sum(grad_mlp_logits[:, :, None] * mlp_choose, axis=1)
    grad_mlp_in = jnp.dot(grad_mlp_cols, router_mlp.astype(jnp.float32).T, precision=precise)
    grad_expert = mlp_weight[..., None] * grad_out[mlp_table]
    grad_main = grad_expert.astype(jnp.bfloat16)
    grad_down_low = jnp.einsum("ecd,erd->ecr", grad_expert, down_second, precision=precise).astype(
        jnp.bfloat16
    )
    grad_down_b_own = jnp.einsum("ecr,ecd->erd", low_sum, grad_expert, precision=precise)
    send_grad = jnp.repeat(grad_main, slice_count, axis=0)
    send_grad_low = jnp.repeat(grad_down_low, slice_count, axis=0)
    recv_grad, recv_grad_low, owner_rows, owner_low = (
        lax.all_to_all(send_grad, "dp", split_axis=0, concat_axis=0, tiled=True),
        lax.all_to_all(send_grad_low, "dp", split_axis=0, concat_axis=0, tiled=True),
        lax.all_to_all(send_rows_all, "dp", split_axis=0, concat_axis=0, tiled=True),
        lax.all_to_all(send_low_all, "dp", split_axis=0, concat_axis=0, tiled=True),
    )
    gate_pre, up_pre, gate_wide, up_wide = expert_inner(owner_rows, owner_low)
    sigmoid_gate = jax.nn.sigmoid(gate_pre)
    activated = gate_pre * sigmoid_gate
    hidden_act = (activated * up_pre).astype(jnp.bfloat16)
    grad_low_wide = spread_low(recv_grad_low.astype(jnp.float32))
    grad_hidden = jnp.einsum(
        "scd,fd->scf", recv_grad, down_w, preferred_element_type=jnp.float32
    ) + jnp.einsum("scq,fq->scf", grad_low_wide, down_table, preferred_element_type=jnp.float32)
    grad_down_table = jnp.einsum(
        "scf,scq->fq", hidden_act, grad_low_wide, preferred_element_type=jnp.float32
    )
    grad_gate_pre = (
        grad_hidden * up_pre * sigmoid_gate * (1.0 + gate_pre * (1.0 - sigmoid_gate))
    ).astype(jnp.bfloat16)
    grad_up_pre = (grad_hidden * activated).astype(jnp.bfloat16)
    grad_rows = jnp.einsum(
        "scf,df->scd", grad_gate_pre, gate_w, preferred_element_type=jnp.float32
    ) + jnp.einsum("scf,df->scd", grad_up_pre, up_w, preferred_element_type=jnp.float32)
    grad_gate_low = select_low(
        jnp.einsum("scf,qf->scq", grad_gate_pre, gate_table, preferred_element_type=jnp.float32)
    )
    grad_up_low = select_low(
        jnp.einsum("scf,qf->scq", grad_up_pre, up_table, preferred_element_type=jnp.float32)
    )
    grad_gate_table = jnp.einsum(
        "scq,scf->qf", gate_wide, grad_gate_pre, preferred_element_type=jnp.float32
    )
    grad_up_table = jnp.einsum(
        "scq,scf->qf", up_wide, grad_up_pre, preferred_element_type=jnp.float32
    )
    grad_back = (
        lax.all_to_all(
            grad_rows.astype(jnp.bfloat16), "dp", split_axis=0, concat_axis=0, tiled=True
        ).astype(grad_rows.dtype),
        lax.all_to_all(
            jnp.concatenate([grad_gate_low, grad_up_low], axis=-1).astype(jnp.bfloat16),
            "dp",
            split_axis=0,
            concat_axis=0,
            tiled=True,
        ).astype(jnp.float32),
    )
    rows_back = jnp.sum(grad_back[0].reshape(EXPERTS, slice_count, cap_mlp, D), axis=1)
    lows_back = jnp.sum(grad_back[1].reshape(EXPERTS, slice_count, cap_mlp, 2 * RANK), axis=1)
    grad_gate_lows = lows_back[..., :RANK]
    grad_up_lows = lows_back[..., RANK:]
    grad_buffer = (
        rows_back
        + jnp.einsum(
            "ecr,edr->ecd", grad_gate_lows, gate_first.astype(jnp.float32), precision=precise
        )
        + jnp.einsum("ecr,edr->ecd", grad_up_lows, up_first.astype(jnp.float32), precision=precise)
    )
    grad_mlp_in = grad_mlp_in + jnp.zeros((tok_rows, D), jnp.float32).at[mlp_table].add(
        jnp.where(mlp_valid[..., None], grad_buffer, 0.0)
    )
    sent_rows_wide = sent_rows.astype(jnp.float32)
    grad_gate_a_own = jnp.einsum("ecd,ecr->edr", sent_rows_wide, grad_gate_lows, precision=precise)
    grad_up_a_own = jnp.einsum("ecd,ecr->edr", sent_rows_wide, grad_up_lows, precision=precise)
    grad_first = grad_out + norm_backward(hidden_first, inverse_second, gain_second, grad_mlp_in)
    grad_all = lax.all_gather(grad_first.astype(jnp.bfloat16), "shard", axis=0, tiled=True)
    grad_at_pairs = grad_all[attn_table].astype(jnp.float32)
    grad_gate_part = jnp.where(attn_valid, jnp.sum(grad_at_pairs * out_part, axis=-1), 0.0)
    grad_result = (attn_weight[..., None] * grad_at_pairs).astype(jnp.bfloat16)
    grad_out_low = jnp.einsum(
        "ecd,erd->ecr", grad_result, out_second, preferred_element_type=jnp.float32
    )
    grad_output_b_own = jnp.einsum(
        "ecr,ecd->erd", out_low, grad_result.astype(jnp.float32), precision=precise
    )
    grad_output_a_own = jnp.einsum(
        "ehcj,ecr->ehjr", mixed_heads.astype(jnp.float32), grad_out_low, precision=precise
    ).reshape(ATT_EXPERTS, width_local, RANK)
    grad_mixed = jnp.einsum(
        "ecd,ehjd->ehcj", grad_result, output_w_heads, preferred_element_type=jnp.float32
    ) + jnp.einsum(
        "ecr,ehjr->ehcj", grad_out_low, out_first_heads.astype(jnp.float32), precision=precise
    )
    grad_mixed = grad_mixed.astype(jnp.bfloat16)

    def attend_back(running, block_items):
        key_sum, value_sum = running
        query_block, query_pos, grad_block, log_block = block_items
        scores = scores_for(query_block, query_pos)
        probabilities = jnp.exp(scores - log_block[..., None])
        grad_probs = jnp.einsum(
            "hqd,hkd->hqk", grad_block, value_rows, preferred_element_type=jnp.float32
        )
        centre = jnp.sum(probabilities * grad_probs, axis=-1, keepdims=True)
        grad_scores = (probabilities * (grad_probs - centre)).astype(jnp.bfloat16)
        grad_query = (
            jnp.einsum("hqk,hkd->hqd", grad_scores, key_rows, preferred_element_type=jnp.float32)
            * score_scale
        )
        key_sum = (
            key_sum
            + jnp.einsum(
                "hqk,hqd->hkd", grad_scores, query_block, preferred_element_type=jnp.float32
            )
            * score_scale
        )
        value_sum = value_sum + jnp.einsum(
            "hqk,hqd->hkd",
            probabilities.astype(jnp.bfloat16),
            grad_block,
            preferred_element_type=jnp.float32,
        )
        return ((key_sum, value_sum), grad_query)

    zero_rows = jnp.zeros((heads_local, seq_len, HD), jnp.float32)
    (grad_keys, grad_values), grad_queries = lax.scan(
        attend_back, (zero_rows, zero_rows), (queries, attn_table, grad_mixed, log_totals)
    )
    grad_query_pre = unrotate(grad_queries, query_cos, query_sin).astype(jnp.bfloat16)
    grad_key_pre = unrotate(grad_keys, key_cos, key_sin).astype(jnp.bfloat16)
    grad_value_pre = grad_values.astype(jnp.bfloat16)
    grad_query_low = jnp.einsum(
        "ehcj,erhj->ecr", grad_query_pre, query_second_heads, preferred_element_type=jnp.float32
    )
    grad_query_rows = jnp.einsum(
        "ehcj,edhj->ecd", grad_query_pre, query_w_heads, preferred_element_type=jnp.float32
    ) + jnp.einsum(
        "ecr,edr->ecd", grad_query_low, query_first.astype(jnp.float32), precision=precise
    )
    grad_query_b_own = jnp.einsum(
        "ecr,ehcj->erhj", query_low, grad_query_pre.astype(jnp.float32), precision=precise
    ).reshape(ATT_EXPERTS, RANK, width_local)
    grad_query_a_own = jnp.einsum(
        "ecd,ecr->edr", query_rows.astype(jnp.float32), grad_query_low, precision=precise
    )
    grad_normed = (
        jnp.zeros((seq_len, D), jnp.float32)
        .at[attn_table]
        .add(jnp.where(attn_valid[..., None], grad_query_rows, 0.0))
    )
    grad_key_low = jnp.einsum(
        "hsj,rhj->sr", grad_key_pre, key_second_heads, preferred_element_type=jnp.float32
    )
    grad_value_low = jnp.einsum(
        "hsj,rhj->sr", grad_value_pre, value_second_heads, preferred_element_type=jnp.float32
    )
    grad_normed = (
        grad_normed
        + jnp.einsum("hsj,dhj->sd", grad_key_pre, key_w_heads, preferred_element_type=jnp.float32)
        + jnp.einsum(
            "hsj,dhj->sd", grad_value_pre, value_w_heads, preferred_element_type=jnp.float32
        )
    )
    grad_normed = (
        grad_normed
        + jnp.dot(grad_key_low, key_first.astype(jnp.float32).T, precision=precise)
        + jnp.dot(grad_value_low, value_first.astype(jnp.float32).T, precision=precise)
    )
    grad_key_b_own = jnp.einsum(
        "sr,hsj->rhj", key_low, grad_key_pre.astype(jnp.float32), precision=precise
    ).reshape(RANK, width_local)
    grad_value_b_own = jnp.einsum(
        "sr,hsj->rhj", value_low, grad_value_pre.astype(jnp.float32), precision=precise
    ).reshape(RANK, width_local)
    grad_kv_first = jnp.dot(
        normed_all.astype(jnp.float32).T,
        jnp.concatenate([grad_key_low, grad_value_low], axis=1),
        precision=precise,
    )
    grad_key_a_own = grad_kv_first[:, :RANK]
    grad_value_a_own = grad_kv_first[:, RANK:]
    gate_rows_part = (
        jnp.zeros((seq_len, ATT_EXPERTS), jnp.float32)
        .at[attn_table, expert_range]
        .add(grad_gate_part)
    )
    grad_normed_local, grad_gate_local = (
        lax.psum_scatter(
            grad_normed.astype(jnp.bfloat16), "shard", scatter_dimension=0, tiled=True
        ).astype(jnp.float32),
        lax.psum_scatter(
            gate_rows_part.astype(jnp.bfloat16), "shard", scatter_dimension=0, tiled=True
        ).astype(jnp.float32),
    )
    local_gates = lax.dynamic_slice_in_dim(attn_gates, first_row, tok_rows, 0)
    local_routes = lax.dynamic_slice_in_dim(attn_routes, first_row, tok_rows, 0)
    local_choose = lax.dynamic_slice_in_dim(attn_choose, first_row, tok_rows, 0)
    grad_pair = jnp.take_along_axis(grad_gate_local, local_routes, axis=1)
    grad_attn_logits = gate_backward(local_gates, grad_pair)
    grad_attn_cols = jnp.sum(grad_attn_logits[:, :, None] * local_choose, axis=1)
    grad_normed_local = grad_normed_local + jnp.dot(
        grad_attn_cols, router_attn.astype(jnp.float32).T, precision=precise
    )
    input_grad = grad_first + norm_backward(inputs, inverse_first, gain_first, grad_normed_local)
    head_sums = (
        lax.psum_scatter(
            place_adapter(grad_query_b_own, 1, adapter_pick).astype(jnp.bfloat16),
            "dp",
            scatter_dimension=2,
            tiled=True,
        ).astype(jnp.float32),
        lax.psum_scatter(
            place_adapter(grad_key_b_own, 0, adapter_pick).astype(jnp.bfloat16),
            "dp",
            scatter_dimension=1,
            tiled=True,
        ).astype(jnp.float32),
        lax.psum_scatter(
            place_adapter(grad_value_b_own, 0, adapter_pick).astype(jnp.bfloat16),
            "dp",
            scatter_dimension=1,
            tiled=True,
        ).astype(jnp.float32),
        lax.psum_scatter(
            place_adapter(grad_output_a_own, 1, adapter_pick).astype(jnp.bfloat16),
            "dp",
            scatter_dimension=3,
            tiled=True,
        ).astype(jnp.float32),
    )
    grad_down_a_local = jnp.transpose(grad_down_table.reshape(ff_local, ADAPTERS, RANK), (1, 0, 2))
    slice_sums = (
        lax.psum_scatter(
            grad_gate_table.reshape(ADAPTERS, RANK, ff_local).astype(jnp.bfloat16),
            "shard",
            scatter_dimension=2,
            tiled=True,
        ).astype(jnp.float32),
        lax.psum_scatter(
            grad_up_table.reshape(ADAPTERS, RANK, ff_local).astype(jnp.bfloat16),
            "shard",
            scatter_dimension=2,
            tiled=True,
        ).astype(jnp.float32),
        lax.psum_scatter(
            grad_down_a_local.astype(jnp.bfloat16), "shard", scatter_dimension=1, tiled=True
        ).astype(jnp.float32),
    )
    shared_sums = (
        lax.psum_scatter(
            place_adapter(grad_query_a_own, 1, adapter_pick),
            ("dp", "shard"),
            scatter_dimension=2,
            tiled=True,
        ),
        lax.psum_scatter(
            place_adapter(grad_key_a_own, 0, adapter_pick),
            ("dp", "shard"),
            scatter_dimension=1,
            tiled=True,
        ),
        lax.psum_scatter(
            place_adapter(grad_value_a_own, 0, adapter_pick),
            ("dp", "shard"),
            scatter_dimension=1,
            tiled=True,
        ),
        lax.psum_scatter(
            place_adapter(grad_output_b_own, 1, adapter_pick),
            ("dp", "shard"),
            scatter_dimension=3,
            tiled=True,
        ),
        lax.psum_scatter(
            place_adapter(grad_gate_a_own, 1, adapter_pick),
            ("dp", "shard"),
            scatter_dimension=2,
            tiled=True,
        ),
        lax.psum_scatter(
            place_adapter(grad_up_a_own, 1, adapter_pick),
            ("dp", "shard"),
            scatter_dimension=2,
            tiled=True,
        ),
        lax.psum_scatter(
            place_adapter(grad_down_b_own, 1, adapter_pick),
            ("dp", "shard"),
            scatter_dimension=3,
            tiled=True,
        ),
    )
    return (
        layer_out,
        input_grad,
        shared_sums[0],
        head_sums[0],
        shared_sums[1],
        head_sums[1],
        shared_sums[2],
        head_sums[2],
        head_sums[3],
        shared_sums[3],
        shared_sums[4],
        slice_sums[0],
        shared_sums[5],
        slice_sums[1],
        slice_sums[2],
        shared_sums[6],
    )


def solution(mesh):
    placed = (
        P(("dp", "shard"), None),
        P(("dp", "shard"), None),
        P(),
        P(),
        P(),
        P(),
        P(None, None, "shard"),
        P(None, "shard"),
        P(None, "shard"),
        P(None, "shard", None),
        P(None, "dp"),
        P(None, "dp"),
        P("dp", None),
        P(),
        P(None, None, None, "shard"),
        P(),
        P(None, None, "shard"),
        P(),
        P(None, None, "shard"),
        P(None, None, "shard", None),
        P(),
        P(),
        P(None, None, "dp"),
        P(),
        P(None, None, "dp"),
        P(None, "dp", None),
        P(),
        P(),
        P("dp", None),
        P(("dp", "shard"), None),
    )
    return jax.shard_map(
        on_device,
        mesh=mesh,
        in_specs=placed,
        out_specs=(
            P(("dp", "shard"), None),
            P(("dp", "shard"), None),
            P(None, None, ("dp", "shard"), None),
            P(None, None, "dp", "shard"),
            P(None, ("dp", "shard"), None),
            P(None, "dp", "shard"),
            P(None, ("dp", "shard"), None),
            P(None, "dp", "shard"),
            P(None, None, "shard", "dp"),
            P(None, None, None, ("dp", "shard")),
            P(None, None, ("dp", "shard"), None),
            P(None, None, ("dp", "shard")),
            P(None, None, ("dp", "shard"), None),
            P(None, None, ("dp", "shard")),
            P(None, ("dp", "shard"), None),
            P(None, None, None, ("dp", "shard")),
        ),
        check_vma=False,
    )
```

profile of v0, /device:TPU:0, one launch (start us, length us, event | category | flops | bytes accessed | tf_op | source)
XLA Modules:
  0.0 2168.7 jit_solution(76881595376772790)
XLA Ops:
  22.6 15.7 scatter_custom_fusion.3
  47.9 13.5 all-gather.3.cloned.1.call-done
  89.2 12.9 gather_fusion.1
  106.1 9.2 fusion.46
  122.9 30.2 %while.28 = (s32[]{:T(128)}, bf16[8,4,160,128]{3,2,1,0:T(8,128)(2,1)}, f32[8,4,160]{2,1,0:T(4,128)}, s32[8,160]{1,0:T(8,128)S(1)}, bf16[8,4,160,128]{3,2,1,0:T(8...) while((s32[]{:T(128)}, ...), condition=%wide.region_12.13_spmd.clone, body=%wide.region_9.12_spmd.clone.sunk | while | flops 170556800 | bytes 5496301 | solution.py:221
  155.3 8.3 fusion.279
  163.7 13.4 broadcast_multiply_fusion
  177.1 23.3 %scatter_custom_fusion = f32[512,2048]{1,0:T(8,128)} fusion(s32[1280]{0:T(1024)} %copy-done.86, f32[1280,2048]{1,0:T(8,128)} %bitcast.563, f32[]{:T(128)} %constant.63.clone.1), kind=kCustom, calls=%fused_computation.159 | custom fusion | flops 2621440 | bytes 4194816 | tf_op jit(solution)/shard_map/scatter-add | solution.py:232
  212.3 35.1 %reduce-scatter.40.cloned.1.call-done = bf16[128,2048]{1,0:T(8,128)(2,1)} async-done(((bf16[512,2048]{1,0:T(8,128)(2,1)}), bf16[128,2048]{1,0:T(8,128)(2,1)}) %reduce-scatter.40.cloned.1.call-update) | async-done | bytes 524304 | tf_op jit(solution)/shard_map/reduce_scatter | solution.py:234
  271.2 18.0 all-to-all-done
  289.1 12.5 fusion.42
  303.0 15.0 fusion.38
  329.3 14.0 fusion.88
  410.2 11.8 all-to-all-done.4
  422.0 21.5 multiply_convert_fusion.2
  448.6 14.4 fusion.36
  471.8 14.5 fusion.85
  491.4 17.4 all-to-all-done.6
  529.7 9.3 copy.598
  539.0 13.4 reshape.820
  556.6 9.3 copy.596
  565.9 13.5 reshape.818
  585.6 9.3 copy.592
  594.9 13.4 reshape.814
  608.4 12.9 gather_fusion.7
  628.3 12.2 fusion.91
  640.5 75.3 %while.29 = (s32[]{:T(128)}, f32[4,512,128]{2,1,0:T(8,128)}, f32[4,512,128]{2,1,0:T(8,128)}, f32[8,4,160,128]{3,2,1,0:T(8,128)}, s32[8,160]{1,0:T(8,128)}, /*ind...) while((s32[]{:T(128)}, f32[4,512,128]{2,1,0:T(8,128)}, ...), condition=%wide.region_34.36_spmd.clone, body=%wide.region_32.35_spmd.clone.sunk | while | flops 423853440 | bytes 33536660 | solution.py:439
  723.2 9.7 scatter_custom_fusion.5
  804.4 9.3 fusion.66
  813.7 11.7 fusion.44
  825.3 13.0 fusion.52
  838.3 25.5 %scatter_fusion.1 = f32[512,2048]{1,0:T(8,128)} fusion(f32[512,2048]{1,0:T(8,128)} %fusion.66, s32[1280]{0:T(1024)S(1)} %copy-done.87, f32[1280,2048]{1,0:T(8,128)} %bitcast.551), kind=kCustom, calls=%fused_computation.14 | custom fusion | flops 2621440 | bytes 31462400 | tf_op jit(solution)/shard_map/scatter-add | solution.py:462
  874.9 9.8 broadcast_multiply_fusion.2
  884.7 50.3 %copy.594 = f32[8,8,2048,16]{3,1,0,2:T(8,128)} copy(f32[8,8,2048,16]{2,3,1,0:T(8,128)} %get-tuple-element.520) | data formatting | bytes 16777216
  935.0 54.6 %reshape.816 = f32[2048,1024]{1,0:T(8,128)} reshape(f32[2048,8,8,16]{3,2,1,0:T(8,128)} %bitcast.139) | data formatting | bytes 16777216
  997.7 8.1 broadcast_multiply_fusion.1
  1005.8 50.3 %copy.600 = f32[8,8,16,2048]{2,1,0,3:T(8,128)} copy(f32[8,8,16,2048]{3,2,1,0:T(8,128)} %get-tuple-element.518) | data formatting | bytes 16777216
  1056.1 54.6 %reshape.822 = f32[2048,1024]{1,0:T(8,128)} reshape(f32[2048,8,8,16]{3,2,1,0:T(8,128)} %bitcast.146) | data formatting | bytes 16777216
  1110.7 50.8 %copy.590 = f32[8,8,2048,16]{3,1,0,2:T(8,128)} copy(f32[8,8,2048,16]{2,3,1,0:T(8,128)} %get-tuple-element.521) | data formatting | bytes 16777216
  1161.5 54.9 %reshape.812 = f32[2048,1024]{1,0:T(8,128)} reshape(f32[2048,8,8,16]{3,2,1,0:T(8,128)} %bitcast.134) | data formatting | bytes 16777216
  1216.5 50.3 %copy.582 = f32[8,8,2048,16]{3,1,0,2:T(8,128)} copy(f32[8,8,2048,16]{2,3,1,0:T(8,128)} %get-tuple-element.522) | data formatting | bytes 16777216
  1266.8 54.7 %reshape.804 = f32[2048,1024]{1,0:T(8,128)} reshape(f32[2048,8,8,16]{3,2,1,0:T(8,128)} %bitcast.123) | data formatting | bytes 16777216
  1321.6 50.3 %copy.588 = f32[8,8,16,2048]{2,1,0,3:T(8,128)} copy(f32[8,8,16,2048]{3,2,1,0:T(8,128)} %get-tuple-element.519) | data formatting | bytes 16777216
  1371.9 54.7 %reshape.810 = f32[2048,1024]{1,0:T(8,128)} reshape(f32[2048,8,8,16]{3,2,1,0:T(8,128)} %bitcast.131) | data formatting | bytes 16777216
  1474.5 123.6 %reduce-scatter.72.cloned.1.call-done = f32[64,1024]{1,0:T(8,128)} async-done(((f32[2048,1024]{1,0:T(8,128)}), f32[64,1024]{1,0:T(8,128)}) %reduce-scatter.72.cloned.1.call-update) | async-done | bytes 262160
  1601.8 182.1 %reduce-scatter.62.cloned.1.call-done = f32[64,1024]{1,0:T(8,128)} async-done(((f32[2048,1024]{1,0:T(8,128)}), f32[64,1024]{1,0:T(8,128)}) %reduce-scatter.62.cloned.1.call-update) | async-done | bytes 262160
  1787.6 182.1 %reduce-scatter.54.cloned.1.call-done = f32[64,1024]{1,0:T(8,128)} async-done(((f32[2048,1024]{1,0:T(8,128)}), f32[64,1024]{1,0:T(8,128)}) %reduce-scatter.54.cloned.1.call-update) | async-done | bytes 262160
  1976.2 179.4 %reduce-scatter.60.cloned.1.call-done = f32[64,1024]{1,0:T(8,128)} async-done(((f32[2048,1024]{1,0:T(8,128)}), f32[64,1024]{1,0:T(8,128)}) %reduce-scatter.60.cloned.1.call-update) | async-done | bytes 262160
  (765 shorter events, 506.0 us)
Async XLA Ops:
  7.2 113.7 %copy-start = (bf16[2048,512]{1,0:T(8,128)(2,1)S(1)}, bf16[2048,512]{1,0:T(8,128)(2,1)}, u32[]{:S(2)}) copy-start(bf16[2048,512]{1,0:T(8,128)(2,1)} %param.44) | copy-start | bytes 6291460
  7.2 54.1 %all-gather.3.cloned.1.call-start = ((), (), s32[]{:S(2)}) async-start(), calls=%async_computation.25 | async-start | bytes 2621440 | tf_op jit(solution)/shard_map/all_gather | solution.py:156
  12.5 235.0 %reduce-scatter.40.cloned.1.call-start = ((), (), s32[]{:S(2)}) async-start(), calls=%async_computation.26 | async-start | bytes 2621440 | tf_op jit(solution)/shard_map/reduce_scatter | solution.py:234
  16.0 147.6 %copy-start.103 = (s32[8]{0:T(128)}, s32[8]{0:T(128)S(1)}, u32[]{:S(2)}) copy-start(s32[8]{0:T(128)S(1)} %get-tuple-element.442) | copy-start | bytes 100
  19.5 66.7 %copy-start.89 = (bf16[16,4,128]{2,1,0:T(4,128)(2,1)}, bf16[16,4,128]{2,1,0:T(4,128)(2,1)S(1)}, u32[]{:S(2)}) copy-start(bf16[16,4,128]{2,1,0:T(4,128)(2,1)S(1)} %reshape_squeeze.13) | copy-start | bytes 49156
  20.5 94.8 %copy-start.45 = (bf16[8,16,4,128]{3,2,1,0:T(4,128)(2,1)}, bf16[8,16,4,128]{3,2,1,0:T(4,128)(2,1)S(1)}, u32[]{:S(2)}) copy-start(bf16[8,16,4,128]{3,2,1,0:T(4,128)(2,1)S(1)} %reshape_squeeze.12) | copy-start | bytes 393220
  21.5 131.7 %copy-start.47 = (bf16[8,4,128,16]{2,1,3,0:T(4,128)(2,1)}, bf16[8,4,128,16]{2,1,3,0:T(4,128)(2,1)S(1)}, u32[]{:S(2)}) copy-start(bf16[8,4,128,16]{2,1,3,0:T(4,128)(2,1)S(1)} %reshape_squeeze.15) | copy-start | bytes 393220
  39.1 22.2 %copy-start.74 = (bf16[2048,8]{0,1:T(8,128)(2,1)S(1)}, bf16[2048,8]{0,1:T(8,128)(2,1)}, u32[]{:S(2)}) copy-start(bf16[2048,8]{0,1:T(8,128)(2,1)} %param.40) | copy-start | bytes 98308
  44.2 42.6 %copy-start.39 = (f32[512,64]{0,1:T(8,128)}, f32[512,64]{0,1:T(8,128)S(1)}, u32[]{:S(2)}) copy-start(f32[512,64]{0,1:T(8,128)S(1)} %get-tuple-element.516) | copy-start | bytes 393220
  44.2 42.6 %copy-start.41 = (f32[512,64]{0,1:T(8,128)}, f32[512,64]{0,1:T(8,128)S(1)}, u32[]{:S(2)}) copy-start(f32[512,64]{0,1:T(8,128)S(1)} %get-tuple-element.517) | copy-start | bytes 393220
  47.9 68.7 %copy-start.25 = (f32[8,160,64]{2,1,0:T(8,128)}, f32[8,160,64]{2,1,0:T(8,128)S(1)}, u32[]{:S(2)}) copy-start(f32[8,160,64]{2,1,0:T(8,128)S(1)} %get-tuple-element.508) | copy-start | bytes 983044
  204.4 43.1 %copy-start.13 = (bf16[128,2048]{1,0:T(8,128)(2,1)S(1)}, bf16[128,2048]{1,0:T(8,128)(2,1)}, u32[]{:S(2)}) copy-start(bf16[128,2048]{1,0:T(8,128)(2,1)} %param.36) | copy-start | bytes 1572868
  204.4 46.3 %copy-start.66 = (f32[2048]{0:T(1024)}, f32[2048]{0:T(1024)S(1)}, u32[]{:S(2)}) copy-start(f32[2048]{0:T(1024)S(1)} %convert_element_type.273) | copy-start | bytes 24580
  209.9 41.1 %copy-start.93 = (s32[320]{0:T(512)}, s32[320]{0:T(512)S(1)}, u32[]{:S(2)}) copy-start(s32[320]{0:T(512)S(1)} %reshape.610) | copy-start | bytes 3844
  210.0 54.0 %copy-start.101 = (pred[8,40]{1,0:T(8,128)(4,1)}, pred[8,40]{1,0:T(8,128)(4,1)S(1)}, u32[]{:S(2)}) copy-start(pred[8,40]{1,0:T(8,128)(4,1)S(1)} %iota_compare_fusion.6) | copy-start | bytes 964
  257.4 9.2 all-to-all-start.1
  266.6 22.5 %all-to-all-start = ((bf16[8,40,2048]{2,1,0:T(8,128)(2,1)}), bf16[8,40,2048]{2,1,0:T(8,128)(2,1)}, u32[]{:S(2)}, u32[]{:S(2)}) async-start(bf16[8,40,2048]{2,1,0:T(8,128)(2,1)} %broadcast_select_fusion), calls=%async_computation.1 | async-start | bytes 2621440 | tf_op jit(solution)/shard_map/all_to_all | solution.py:286
  271.2 30.5 %copy-start.55 = (f32[8,40,16]{1,2,0:T(8,128)}, f32[8,40,16]{1,2,0:T(8,128)S(1)}, u32[]{:S(2)}) copy-start(f32[8,40,16]{1,2,0:T(8,128)S(1)} %get-tuple-element.506) | copy-start | bytes 61444
  271.2 46.9 %copy-start.64 = (f32[8,40,16]{1,2,0:T(8,128)}, f32[8,40,16]{1,2,0:T(8,128)S(1)}, u32[]{:S(2)}) copy-start(f32[8,40,16]{1,2,0:T(8,128)S(1)} %get-tuple-element.507) | copy-start | bytes 61444
  325.9 17.3 all-to-all-start.3
  343.3 22.9 %all-to-all-start.2 = ((bf16[8,40,2048]{2,1,0:T(8,128)(2,1)}), bf16[8,40,2048]{2,1,0:T(8,128)(2,1)}, u32[]{:S(2)}, u32[]{:S(2)}) async-start(bf16[8,40,2048]{2,1,0:T(8,128)(2,1)} %fusion.88), calls=%async_computation.3 | async-start | bytes 2621440 | tf_op jit(solution)/shard_map/all_to_all | solution.py:296
  390.6 8.7 all-to-all-start.5
  399.3 22.7 %all-to-all-start.4 = ((bf16[8,40,2048]{2,1,0:T(8,128)(2,1)}), bf16[8,40,2048]{2,1,0:T(8,128)(2,1)}, u32[]{:S(2)}, u32[]{:S(2)}) async-start(bf16[8,40,2048]{2,1,0:T(8,128)(2,1)} %multiply_convert_fusion.4), calls=%async_computation.5 | async-start | bytes 2621440 | tf_op jit(solution)/shard_map/all_to_all | solution.py:324
  422.0 21.5 copy-start.126
  468.2 18.0 all-to-all-start.7
  486.2 22.5 %all-to-all-start.6 = ((bf16[8,40,2048]{2,1,0:T(8,128)(2,1)}), bf16[8,40,2048]{2,1,0:T(8,128)(2,1)}, u32[]{:S(2)}, u32[]{:S(2)}) async-start(bf16[8,40,2048]{2,1,0:T(8,128)(2,1)} %fusion.85), calls=%async_computation.7 | async-start | bytes 2621440 | tf_op jit(solution)/shard_map/all_to_all | solution.py:360
  490.5 117.9 %all-gather.5.cloned.1.call-start = ((), (), s32[]{:S(2)}) async-start(), calls=%async_computation.27 | async-start | bytes 2621440 | tf_op jit(solution)/shard_map/all_gather | solution.py:389
  490.6 20.2 copy-start.102
  491.4 21.5 copy-start.53
  523.6 904.0 %reduce-scatter.70.cloned.1.call-start = ((), (), s32[]{:S(2)}) async-start(), calls=%async_computation.42 | async-start | bytes 1802240
  552.5 884.0 %reduce-scatter.68.cloned.1.call-start = ((), (), s32[]{:S(2)}) async-start(), calls=%async_computation.41 | async-start | bytes 1802240
  579.4 865.9 %reduce-scatter.64.cloned.1.call-start = ((), (), s32[]{:S(2)}) async-start(), calls=%async_computation.39 | async-start | bytes 1802240
  608.3 845.9 %reduce-scatter.52.cloned.1.call-start = ((), (), s32[]{:S(2)}) async-start(), calls=%async_computation.33 | async-start | bytes 163840
  715.8 19.3 copy-start.10
  722.4 16.9 copy-start.40
  742.7 714.3 %reduce-scatter.46.cloned.1.call-start = ((), (), s32[]{:S(2)}) async-start(), calls=%async_computation.30 | async-start | bytes 147456 | tf_op jit(solution)/shard_map/reduce_scatter | solution.py:525
  744.3 714.3 %reduce-scatter.48.cloned.1.call-start = ((), (), s32[]{:S(2)}) async-start(), calls=%async_computation.31 | async-start | bytes 147456 | tf_op jit(solution)/shard_map/reduce_scatter | solution.py:531
  748.2 711.7 %reduce-scatter.50.cloned.1.call-start = ((), (), s32[]{:S(2)}) async-start(), calls=%async_computation.32 | async-start | bytes 1179648 | tf_op jit(solution)/shard_map/reduce_scatter | solution.py:537
  749.5 712.2 %reduce-scatter.44.cloned.1.call-start = ((), (), s32[]{:S(2)}) async-start(), calls=%async_computation.29 | async-start | bytes 1179648 | tf_op jit(solution)/shard_map/reduce_scatter | solution.py:519
  758.8 704.7 %reduce-scatter.58.cloned.1.call-start = ((), (), s32[]{:S(2)}) async-start(), calls=%async_computation.36 | async-start | bytes 1081344
  777.2 687.9 %reduce-scatter.56.cloned.1.call-start = ((), (), s32[]{:S(2)}) async-start(), calls=%async_computation.35 | async-start | bytes 1081344
  803.9 662.9 %reduce-scatter.42.cloned.1.call-start = ((), (), s32[]{:S(2)}) async-start(), calls=%async_computation.28 | async-start | bytes 2621440 | tf_op jit(solution)/shard_map/reduce_scatter | solution.py:501
  867.7 603.2 %reduce-scatter.66.cloned.1.call-start = ((), (), s32[]{:S(2)}) async-start(), calls=%async_computation.40 | async-start | bytes 8650752
  989.7 608.5 %reduce-scatter.72.cloned.1.call-start = ((), (), s32[]{:S(2)}) async-start(), calls=%async_computation.43 | async-start | bytes 8650752
  1110.7 673.2 %reduce-scatter.62.cloned.1.call-start = ((), (), s32[]{:S(2)}) async-start(), calls=%async_computation.38 | async-start | bytes 8650752
  1216.5 753.2 %reduce-scatter.54.cloned.1.call-start = ((), (), s32[]{:S(2)}) async-start(), calls=%async_computation.34 | async-start | bytes 8650752
  1321.6 834.0 %reduce-scatter.60.cloned.1.call-start = ((), (), s32[]{:S(2)}) async-start(), calls=%async_computation.37 | async-start | bytes 8650752
  1972.7 189.3 %copy-start.1 = (bf16[2048,512]{1,0:T(8,128)(2,1)S(1)}, bf16[2048,512]{1,0:T(8,128)(2,1)}, u32[]{:S(2)}) copy-start(bf16[2048,512]{1,0:T(8,128)(2,1)} %param.44) | copy-start | bytes 6291460
  (135 other events, 828.7 us)
Sparse Core Ops, SparseCore 0:
  12.6 48.6 all-gather.2
  204.5 42.9 reduce-scatter.39
  523.7 43.4 all-gather.4
  569.5 31.9 reduce-scatter.69
  603.8 32.1 reduce-scatter.67
  638.2 32.1 reduce-scatter.63
  742.8 16.4 reduce-scatter.51
  762.9 31.6 reduce-scatter.45
  798.4 33.3 reduce-scatter.47
  834.9 36.0 reduce-scatter.49
  874.2 36.0 reduce-scatter.43
  912.3 135.3 reduce-scatter.57
  1050.0 132.0 reduce-scatter.55
  1184.3 40.6 reduce-scatter.41
  1227.2 185.1 reduce-scatter.65
  1414.7 183.4 reduce-scatter.71
  1600.4 183.4 reduce-scatter.61
  1786.1 183.4 reduce-scatter.53
  1972.1 183.4 reduce-scatter.59
where the time goes:
time: 2180 us; the launch traced here: 2170 us
  local copies, waits for them, and re-layouts  816 us (37%)
  waiting for transfers between devices  773 us (35%)
  matrix products  360 us (17%)
  other arithmetic  167 us (8%)
  starting transfers between devices  33.8 us (2%)
    unnamed x310, local copies, waits for them, and re-layouts  711 us
    unnamed x30, waiting for transfers between devices  668 us
  transfers between devices with their start and end apart: 27, of which 11 were waited for; matrix products, arithmetic and copies ran while one was open for 49% of the time, Pallas kernels for 0%

commit v1 on v0

--- a/solution.py
+++ b/solution.py
@@ -91,13 +91,6 @@
     slot_valid = jnp.arange(capacity, dtype=jnp.int32)[None, :] < jnp.sum(member, axis=0)[:, None]
     pair_slots = jnp.take_along_axis(slot_numbers, routes, axis=1)
     return (token_table, slot_valid, pair_slots, choose.astype(jnp.float32))
-
-
-def place_adapter(partial_grad, insert_axis, adapter_pick):
-    expanded = jnp.expand_dims(partial_grad, insert_axis)
-    pick_shape = [1] * expanded.ndim
-    pick_shape[insert_axis] = adapter_pick.shape[0]
-    return expanded * adapter_pick.reshape(pick_shape)
 
 
 def on_device(
@@ -145,7 +138,6 @@
     adapter_now = adapter_ids[lax.axis_index("dp")]
     first_row = lax.axis_index("shard") * tok_rows
     score_scale = HD ** (-0.5)
-    adapter_pick = (jnp.arange(ADAPTERS, dtype=jnp.int32) == adapter_now).astype(jnp.float32)
     key_w_heads = key_w.reshape(D, heads_local, HD)
     value_w_heads = value_w.reshape(D, heads_local, HD)
     query_w_heads = query_w.reshape(ATT_EXPERTS, D, heads_local, HD)
@@ -335,7 +327,7 @@
         "scd,fd->scf", recv_grad, down_w, preferred_element_type=jnp.float32
     ) + jnp.einsum("scq,fq->scf", grad_low_wide, down_table, preferred_element_type=jnp.float32)
     grad_down_table = jnp.einsum(
-        "scf,scq->fq", hidden_act, grad_low_wide, preferred_element_type=jnp.float32
+        "scq,scf->qf", grad_low_wide, hidden_act, preferred_element_type=jnp.float32
     )
     grad_gate_pre = (
         grad_hidden * up_pre * sigmoid_gate * (1.0 + gate_pre * (1.0 - sigmoid_gate))
@@ -383,8 +375,8 @@
         jnp.where(mlp_valid[..., None], grad_buffer, 0.0)
     )
     sent_rows_wide = sent_rows.astype(jnp.float32)
-    grad_gate_a_own = jnp.einsum("ecd,ecr->edr", sent_rows_wide, grad_gate_lows, precision=precise)
-    grad_up_a_own = jnp.einsum("ecd,ecr->edr", sent_rows_wide, grad_up_lows, precision=precise)
+    grad_gate_a_own = jnp.einsum("ecd,ecr->erd", sent_rows_wide, grad_gate_lows, precision=precise)
+    grad_up_a_own = jnp.einsum("ecd,ecr->erd", sent_rows_wide, grad_up_lows, precision=precise)
     grad_first = grad_out + norm_backward(hidden_first, inverse_second, gain_second, grad_mlp_in)
     grad_all = lax.all_gather(grad_first.astype(jnp.bfloat16), "shard", axis=0, tiled=True)
     grad_at_pairs = grad_all[attn_table].astype(jnp.float32)
@@ -393,12 +385,9 @@
     grad_out_low = jnp.einsum(
         "ecd,erd->ecr", grad_result, out_second, preferred_element_type=jnp.float32
     )
-    grad_output_b_own = jnp.einsum(
-        "ecr,ecd->erd", out_low, grad_result.astype(jnp.float32), precision=precise
-    )
     grad_output_a_own = jnp.einsum(
-        "ehcj,ecr->ehjr", mixed_heads.astype(jnp.float32), grad_out_low, precision=precise
-    ).reshape(ATT_EXPERTS, width_local, RANK)
+        "ecr,ehcj->erhj", grad_out_low, mixed_heads.astype(jnp.float32), precision=precise
+    ).reshape(ATT_EXPERTS, RANK, width_local)
     grad_mixed = jnp.einsum(
         "ecd,ehjd->ehcj", grad_result, output_w_heads, preferred_element_type=jnp.float32
     ) + jnp.einsum(
@@ -453,9 +442,6 @@
     grad_query_b_own = jnp.einsum(
         "ecr,ehcj->erhj", query_low, grad_query_pre.astype(jnp.float32), precision=precise
     ).reshape(ATT_EXPERTS, RANK, width_local)
-    grad_query_a_own = jnp.einsum(
-        "ecd,ecr->edr", query_rows.astype(jnp.float32), grad_query_low, precision=precise
-    )
     grad_normed = (
         jnp.zeros((seq_len, D), jnp.float32)
         .at[attn_table]
@@ -485,13 +471,6 @@
     grad_value_b_own = jnp.einsum(
         "sr,hsj->rhj", value_low, grad_value_pre.astype(jnp.float32), precision=precise
     ).reshape(RANK, width_local)
-    grad_kv_first = jnp.dot(
-        normed_all.astype(jnp.float32).T,
-        jnp.concatenate([grad_key_low, grad_value_low], axis=1),
-        precision=precise,
-    )
-    grad_key_a_own = grad_kv_first[:, :RANK]
-    grad_value_a_own = grad_kv_first[:, RANK:]
     gate_rows_part = (
         jnp.zeros((seq_len, ATT_EXPERTS), jnp.float32)
         .at[attn_table, expert_range]
@@ -515,111 +494,128 @@
         grad_attn_cols, router_attn.astype(jnp.float32).T, precision=precise
     )
     input_grad = grad_first + norm_backward(inputs, inverse_first, gain_first, grad_normed_local)
-    head_sums = (
-        lax.psum_scatter(
-            place_adapter(grad_query_b_own, 1, adapter_pick).astype(jnp.bfloat16),
-            "dp",
-            scatter_dimension=2,
-            tiled=True,
-        ).astype(jnp.float32),
-        lax.psum_scatter(
-            place_adapter(grad_key_b_own, 0, adapter_pick).astype(jnp.bfloat16),
-            "dp",
-            scatter_dimension=1,
-            tiled=True,
-        ).astype(jnp.float32),
-        lax.psum_scatter(
-            place_adapter(grad_value_b_own, 0, adapter_pick).astype(jnp.bfloat16),
-            "dp",
-            scatter_dimension=1,
-            tiled=True,
-        ).astype(jnp.float32),
-        lax.psum_scatter(
-            place_adapter(grad_output_a_own, 1, adapter_pick).astype(jnp.bfloat16),
-            "dp",
-            scatter_dimension=3,
-            tiled=True,
-        ).astype(jnp.float32),
-    )
-    grad_down_a_local = jnp.transpose(grad_down_table.reshape(ff_local, ADAPTERS, RANK), (1, 0, 2))
-    slice_sums = (
-        lax.psum_scatter(
-            grad_gate_table.reshape(ADAPTERS, RANK, ff_local).astype(jnp.bfloat16),
-            "shard",
-            scatter_dimension=2,
-            tiled=True,
-        ).astype(jnp.float32),
-        lax.psum_scatter(
-            grad_up_table.reshape(ADAPTERS, RANK, ff_local).astype(jnp.bfloat16),
-            "shard",
-            scatter_dimension=2,
-            tiled=True,
-        ).astype(jnp.float32),
-        lax.psum_scatter(
-            grad_down_a_local.astype(jnp.bfloat16), "shard", scatter_dimension=1, tiled=True
-        ).astype(jnp.float32),
-    )
-    shared_sums = (
-        lax.psum_scatter(
-            place_adapter(grad_query_a_own, 1, adapter_pick),
-            ("dp", "shard"),
-            scatter_dimension=2,
-            tiled=True,
-        ),
-        lax.psum_scatter(
-            place_adapter(grad_key_a_own, 0, adapter_pick),
-            ("dp", "shard"),
-            scatter_dimension=1,
-            tiled=True,
-        ),
-        lax.psum_scatter(
-            place_adapter(grad_value_a_own, 0, adapter_pick),
-            ("dp", "shard"),
-            scatter_dimension=1,
-            tiled=True,
-        ),
-        lax.psum_scatter(
-            place_adapter(grad_output_b_own, 1, adapter_pick),
-            ("dp", "shard"),
-            scatter_dimension=3,
-            tiled=True,
-        ),
-        lax.psum_scatter(
-            place_adapter(grad_gate_a_own, 1, adapter_pick),
-            ("dp", "shard"),
-            scatter_dimension=2,
-            tiled=True,
-        ),
-        lax.psum_scatter(
-            place_adapter(grad_up_a_own, 1, adapter_pick),
-            ("dp", "shard"),
-            scatter_dimension=2,
-            tiled=True,
-        ),
-        lax.psum_scatter(
-            place_adapter(grad_down_b_own, 1, adapter_pick),
-            ("dp", "shard"),
-            scatter_dimension=3,
-            tiled=True,
-        ),
-    )
+    block = D // (group_count * shard_count)
+    lows = jnp.concatenate(
+        [
+            out_low.reshape(-1, RANK),
+            grad_query_low.reshape(-1, RANK),
+            grad_key_low,
+            grad_value_low,
+        ],
+        axis=0,
+    )
+    lows = lax.psum(lows, "shard")
+    pair_count = ATT_EXPERTS * cap_att
+    out_low_full = lows[:pair_count].reshape(ATT_EXPERTS, cap_att, RANK)
+    query_low_full = lows[pair_count : 2 * pair_count].reshape(ATT_EXPERTS, cap_att, RANK)
+    kv_low_full = jnp.concatenate(
+        [lows[2 * pair_count : 2 * pair_count + seq_len], lows[2 * pair_count + seq_len :]], axis=1
+    )
+
+    def own_columns(rows):
+        split = rows.reshape(rows.shape[:-1] + (group_count, shard_count, block))
+        own = lax.dynamic_index_in_dim(
+            split, lax.axis_index("shard"), axis=split.ndim - 2, keepdims=False
+        )
+        return own.reshape(rows.shape[:-1] + (group_count * block,))
+
+    grad_query_a_own = jnp.einsum(
+        "ecr,ecd->erd",
+        query_low_full,
+        own_columns(query_rows).astype(jnp.float32),
+        preferred_element_type=jnp.float32,
+    )
+    grad_output_b_own = jnp.einsum(
+        "ecr,ecd->erd",
+        out_low_full,
+        own_columns(grad_result).astype(jnp.float32),
+        preferred_element_type=jnp.float32,
+    )
+    grad_kv_a_own = jnp.einsum(
+        "sr,sd->rd",
+        kv_low_full,
+        own_columns(normed_all).astype(jnp.float32),
+        preferred_element_type=jnp.float32,
+    ).reshape(2, RANK, group_count * block)
+    mlp_parts = jnp.concatenate([grad_gate_a_own, grad_up_a_own, grad_down_b_own], axis=0)
+    mlp_parts = (
+        mlp_parts.reshape(3 * EXPERTS * RANK, group_count, shard_count, block)
+        .transpose(2, 0, 1, 3)
+        .reshape(shard_count, 3 * EXPERTS * RANK, group_count * block)
+        .astype(jnp.bfloat16)
+    )
+    mlp_parts = lax.psum_scatter(mlp_parts, "shard", scatter_dimension=0, tiled=True)[0]
+
+    def to_owner_columns(part):
+        return part.reshape(-1, group_count, block).transpose(1, 0, 2).reshape(group_count, -1)
+
+    def to_owner_ranks(part):
+        rows = part.reshape(-1, group_count, RANK // group_count, width_local)
+        return rows.transpose(1, 0, 2, 3).reshape(group_count, -1)
+
+    pieces = [
+        to_owner_columns(grad_query_a_own.astype(jnp.bfloat16)),
+        to_owner_columns(grad_output_b_own.astype(jnp.bfloat16)),
+        to_owner_columns(grad_kv_a_own.astype(jnp.bfloat16)),
+        to_owner_columns(mlp_parts),
+        to_owner_ranks(grad_query_b_own.astype(jnp.bfloat16)),
+        to_owner_ranks(grad_output_a_own.astype(jnp.bfloat16)),
+        to_owner_ranks(jnp.stack([grad_key_b_own, grad_value_b_own]).astype(jnp.bfloat16)),
+    ]
+    sizes = [piece.shape[1] for piece in pieces]
+    sent = jnp.concatenate(pieces, axis=1).reshape(group_count, -1, 128)
+    got = lax.all_to_all(sent, "dp", split_axis=0, concat_axis=0, tiled=True)
+    got = got.reshape(group_count, -1).astype(jnp.float32)
+    placed_sums = jnp.einsum("sa,sn->an", pick_source, got, precision=precise)
+    parts = []
+    start = 0
+    for size in sizes:
+        parts.append(placed_sums[:, start : start + size])
+        start += size
+    ranks_own = RANK // group_count
+
+    def columns_out(part, count):
+        return part.reshape(ADAPTERS, count, RANK, block)
+
+    def ranks_out(part, count):
+        return part.reshape(ADAPTERS, count, ranks_own, width_local)
+
+    query_a_sum = columns_out(parts[0], ATT_EXPERTS).transpose(1, 0, 3, 2)
+    output_b_sum = columns_out(parts[1], ATT_EXPERTS).transpose(1, 0, 2, 3)
+    kv_a_sum = columns_out(parts[2], 2).transpose(1, 0, 3, 2)
+    mlp_sum = columns_out(parts[3], 3 * EXPERTS).transpose(1, 0, 2, 3)
+    gate_a_sum = mlp_sum[:EXPERTS].transpose(0, 1, 3, 2)
+    up_a_sum = mlp_sum[EXPERTS : 2 * EXPERTS].transpose(0, 1, 3, 2)
+    down_b_sum = mlp_sum[2 * EXPERTS :]
+    query_b_sum = ranks_out(parts[4], ATT_EXPERTS).transpose(1, 0, 2, 3)
+    output_a_sum = ranks_out(parts[5], ATT_EXPERTS).transpose(1, 0, 3, 2)
+    kv_b_sum = ranks_out(parts[6], 2).transpose(1, 0, 2, 3)
+
+    def slice_sum(table):
+        return lax.psum_scatter(
+            table.astype(jnp.bfloat16), "shard", scatter_dimension=1, tiled=True
+        ).astype(jnp.float32)
+
+    gate_b_sum = slice_sum(grad_gate_table).reshape(ADAPTERS, RANK, -1)
+    up_b_sum = slice_sum(grad_up_table).reshape(ADAPTERS, RANK, -1)
+    down_a_sum = slice_sum(grad_down_table).reshape(ADAPTERS, RANK, -1).transpose(0, 2, 1)
     return (
         layer_out,
         input_grad,
-        shared_sums[0],
-        head_sums[0],
-        shared_sums[1],
-        head_sums[1],
-        shared_sums[2],
-        head_sums[2],
-        head_sums[3],
-        shared_sums[3],
-        shared_sums[4],
-        slice_sums[0],
-        shared_sums[5],
-        slice_sums[1],
-        slice_sums[2],
-        shared_sums[6],
+        query_a_sum,
+        query_b_sum,
+        kv_a_sum[0],
+        kv_b_sum[0],
+        kv_a_sum[1],
+        kv_b_sum[1],
+        output_a_sum,
+        output_b_sum,
+        gate_a_sum,
+        gate_b_sum,
+        up_a_sum,
+        up_b_sum,
+        down_a_sum,
+        down_b_sum,
     )
 
 

time: 2180 us -> 993 us (0.46)
  waiting for transfers between devices: 773 us -> 111 us
  local copies, waits for them, and re-layouts: 816 us -> 284 us
  blocking collectives: 0 us -> 22.7 us
    unnamed x30 -> x13, waiting for transfers between devices: 668 us -> 0.17 us
    unnamed x310 -> x262, local copies, waits for them, and re-layouts: 711 us -> 52.3 us
    reshape x0 -> x25, local copies, waits for them, and re-layouts: none -> 46.4 us  [the longest x1 15.2 us: own_columns(): split = rows.reshape(rows.shape[:-1] + (group_count, shard_count, block))]
    convert_element_type x0 -> x8, local copies, waits for them, and re-layouts: none -> 44.6 us  [the longest x2 25.6 us: on_device(): grad_at_pairs = grad_all[attn_table].astype(jnp.float32)]
    psum x0 -> x1, blocking collectives: none -> 22.7 us  [on_device(): lows = lax.psum(lows, 'shard')]
  transfers between devices with their start and end apart: 27 -> 18, of which waited for: 11 -> 8; matrix products, arithmetic and copies ran while one was open for 49% -> 57% of each run, Pallas kernels for 0% -> 0%
where the time goes in v1:
time: 993 us; the launch traced here: 983 us
  matrix products  352 us (35%)
  local copies, waits for them, and re-layouts  284 us (29%)
  other arithmetic  158 us (16%)
  waiting for transfers between devices  111 us (11%)
  starting transfers between devices  36.6 us (4%)
  blocking collectives  22.7 us (2%)
  between operations  18 us (2%)
    unnamed x262, local copies, waits for them, and re-layouts  52.3 us
    reduce_scatter x1, waiting for transfers between devices, on_device(): lax.psum_scatter(attn_part.astype(jnp.bfloat16), 'shard', scatter_dimensi...  35 us
    convert_element_type x2, local copies, waits for them, and re-layouts, on_device(): grad_at_pairs = grad_all[attn_table].astype(jnp.float32)  25.6 us
    scatter-add x1, other arithmetic, on_device(): grad_normed = jnp.zeros((seq_len, D), jnp.float32).at[attn_table].add(jnp...  25.3 us
    dot_general x16, matrix products, scores_for(): jnp.einsum('hqd,hkd->hqk', query_block, key_rows, preferred_element_type=...  24.5 us
    scatter-add x1, other arithmetic, on_device(): jnp.zeros((seq_len, D), jnp.float32).at[attn_table]  23.3 us
    psum x1, blocking collectives, on_device(): lows = lax.psum(lows, 'shard')  22.7 us
    dot_general x1, matrix products, on_device(): jnp.einsum('scd,fd->scf', recv_grad, down_w, preferred_element_type=jnp.f...  21.6 us
  transfers between devices with their start and end apart: 18, of which 8 were waited for; matrix products, arithmetic and copies ran while one was open for 57% of the time, Pallas kernels for 0%

profile of v1, /device:TPU:0, one launch (start us, length us, event | category | flops | bytes accessed | tf_op | source)
XLA Modules:
  0.0 983.4 jit_solution(10216399503525249434)
XLA Ops:
  22.5 16.0 %scatter_custom_fusion.3 = s32[1280]{0:T(1024)S(1)} fusion(s32[4096]{0:T(1024)S(1)} %reshape.815, s32[4096]{0:T(1024)S(1)} %reshape.817, s32[]{:T(128)} %constant.77.clone.1), kind=kCustom, calls=%fused_computation.374 | custom fusion | bytes 5124
  48.1 13.0 %all-gather.3.cloned.1.call-done = bf16[512,2048]{1,0:T(8,128)(2,1)} async-done(((bf16[128,2048]{1,0:T(8,128)(2,1)}), bf16[512,2048]{1,0:T(8,128)(2,1)}) %all-gather.3.cloned.1.call-update) | async-done | bytes 2097168 | tf_op jit(solution)/shard_map/all_gather | solution.py:148
  63.3 6.5 gather_fusion.8
  71.9 7.5 gather_fusion
  89.0 12.9 %gather_fusion.1 = bf16[1280,2048]{1,0:T(8,128)(2,1)} fusion(bf16[512,2048]{1,0:T(8,128)(2,1)} %all-gather.3.cloned.1.call-done, s32[2048]{0:T(1024)} %pad_clamp_fusion), kind=kCustom, calls=%fused_computation.3 | custom fusion | bytes 10490880 | tf_op jit(solution)/shard_map/gather | solution.py:176
  105.9 9.1 fusion.46
  122.6 30.2 %while.28 = (s32[]{:T(128)}, bf16[8,4,160,128]{3,2,1,0:T(8,128)(2,1)}, f32[8,4,160]{2,1,0:T(4,128)}, s32[8,160]{1,0:T(8,128)S(1)}, bf16[8,4,160,128]{3,2,1,0:T(8...) while((s32[]{:T(128)}, ...), condition=%wide.region_12.13_spmd.clone, body=%wide.region_9.12_spmd.clone.sunk | while | flops 170556800 | bytes 5496301 | solution.py:213
  154.9 8.2 fusion.273
  163.3 13.1 %broadcast_multiply_fusion = (f32[8,160,2048]{2,1,0:T(8,128)}, f32[8,160,2048]{2,1,0:T(8,128)}) fusion(f32[8,160]{1,0:T(8,128)S(1)} %fusion.232, f32[8,160,16]{1,2,0:T(8,128)S(1)} %convolution_bitcast_fusion.9, bf16[8,8,16,2048]{3,2,1,0:T(8,128)(2,1)} %param.56, s32[]{:T(128)S(6)} %select_n.165, f32[8,160,2048,1]{2,1,3,0:T(8,128)S(1)} %fusion.273), kind=kOutput, calls=%fused_computation.106 | convolution fusion | flops 508559360 | bytes 32068612 | tf_op jit(solution)/shard_map/ecr,erd->ecd/dot_general | solution.py:222
  176.4 23.3 %scatter_custom_fusion = f32[512,2048]{1,0:T(8,128)} fusion(s32[1280]{0:T(1024)} %copy-done.86, f32[1280,2048]{1,0:T(8,128)} %bitcast.576, f32[]{:T(128)} %constant.76.clone.1), kind=kCustom, calls=%fused_computation.152 | custom fusion | flops 2621440 | bytes 4194816 | tf_op jit(solution)/shard_map/scatter-add | solution.py:224
  204.6 4.3 scatter_custom_fusion.4
  211.5 35.0 %reduce-scatter.16.cloned.1.call-done = bf16[128,2048]{1,0:T(8,128)(2,1)} async-done(((bf16[512,2048]{1,0:T(8,128)(2,1)}), bf16[128,2048]{1,0:T(8,128)(2,1)}) %reduce-scatter.16.cloned.1.call-update) | async-done | bytes 524304 | tf_op jit(solution)/shard_map/reduce_scatter | solution.py:226
  250.7 4.9 gather_fusion.3
  270.3 18.0 %all-to-all-done = bf16[8,40,2048]{2,1,0:T(8,128)(2,1)} async-done(((bf16[8,40,2048]{2,1,0:T(8,128)(2,1)}), bf16[8,40,2048]{2,1,0:T(8,128)(2,1)}, u32[]{:S(2)}, u32[]{:S(2)}) %all-to-all-start) | async-done | bytes 1310752 | tf_op jit(solution)/shard_map/all_to_all | solution.py:278
  288.3 12.5 %fusion.42 = f32[8,40,5632]{2,1,0:T(8,128)S(1)} fusion(bf16[8,40,2048]{2,1,0:T(8,128)(2,1)} %all-to-all-done, bf16[2048,5632]{1,0:T(8,128)(2,1)} %param.46), kind=kOutput, calls=%fused_computation.74 | convolution fusion | flops 7381975040 | bytes 31588352 | tf_op jit(solution)/shard_map/scd,df->scf/dot_general | solution.py:270
  302.1 15.0 %fusion.38 = f32[8,40,5632]{2,1,0:T(8,128)S(1)} fusion(bf16[8,40,2048]{2,1,0:T(8,128)(2,1)} %all-to-all-done, bf16[2048,5632]{1,0:T(8,128)(2,1)} %param.47), kind=kOutput, calls=%fused_computation.70 | convolution fusion | flops 7381975040 | bytes 31588352 | tf_op jit(solution)/shard_map/scd,df->scf/dot_general | solution.py:273
  317.2 4.6 multiply_convert_fusion.4
  328.4 14.0 %fusion.78 = bf16[8,40,2048]{2,1,0:T(8,128)(2,1)} fusion(bf16[8,40,5632]{2,1,0:T(8,128)(2,1)} %copy-done.35, bf16[5632,2048]{1,0:T(8,128)(2,1)} %param.48), kind=kOutput, calls=%fused_computation.124 | convolution fusion | flops 7382630400 | bytes 27983872 | tf_op jit(solution)/shard_map/scf,fd->scd/dot_general | solution.py:282
  342.4 4.7 all-to-all-start.2
  357.2 8.1 all-to-all-done.2
  368.8 5.2 gather_fusion.4
  377.5 6.3 multiply_reduce_fusion.2
  413.1 5.6 convolution_bitcast_fusion
  420.3 21.6 %multiply_convert_fusion.3 = (bf16[8,40,5632]{2,1,0:T(8,128)(2,1)}, bf16[8,40,5632]{2,1,0:T(8,128)(2,1)}) fusion(f32[8,40,5632]{2,1,0:T(8,128)} %copy-done.27, f32[8,40,5632]{2,1,0:T(8,128)} %get-tuple-element.425, f32[8,40,5632]{2,1,0:T(8,128)} %convolution_bitcast_fusion, bf16[8,40,2048]{2,1,0:T(8,128)(2,1)} %all-to-all-done.4, bf16[5632,2048]{1,0:T(8,128)(2,1)} %param.48), kind=kOutput, calls=%fused_computation.100 | convolution fusion | flops 7407206400 | bytes 53215232 | tf_op jit(solution)/shard_map/scd,fd->scf/dot_general | solution.py:326
  441.9 4.6 fusion.136
  453.6 14.3 %fusion.36 = f32[8,40,2048]{2,1,0:T(8,128)} fusion(bf16[8,40,5632]{2,1,0:T(8,128)(2,1)} %get-tuple-element.381, bf16[2048,5632]{1,0:T(8,128)(2,1)} %param.47), kind=kOutput, calls=%fused_computation.68 | convolution fusion | flops 7381975040 | bytes 29294592 | tf_op jit(solution)/shard_map/scf,df->scd/dot_general | solution.py:338
  470.4 6.6 convert_element_type.313
  477.0 6.0 copy.675
  483.0 14.4 %fusion.75 = bf16[8,40,2048]{2,1,0:T(8,128)(2,1)} fusion(f32[8,40,2048]{2,1,0:T(8,128)} %fusion.36, bf16[8,40,5632]{2,1,0:T(8,128)(2,1)} %get-tuple-element.380, bf16[2048,5632]{1,0:T(8,128)(2,1)} %param.46), kind=kOutput, calls=%fused_computation.123 | convolution fusion | flops 7383285760 | bytes 30605312 | tf_op jit(solution)/shard_map/scf,df->scd/dot_general | solution.py:336
  497.5 4.4 all-to-all-start.6
  502.6 17.5 %all-to-all-done.6 = bf16[8,40,2048]{2,1,0:T(8,128)(2,1)} async-done(((bf16[8,40,2048]{2,1,0:T(8,128)(2,1)}), bf16[8,40,2048]{2,1,0:T(8,128)(2,1)}, u32[]{:S(2)}, u32[]{:S(2)}) %all-to-all-start.6) | async-done | bytes 1310752 | tf_op jit(solution)/shard_map/all_to_all | solution.py:352
  524.4 6.1 scatter_fusion
  547.5 7.9 copy.664
  556.2 15.2 %reshape.661 = bf16[8,160,8,4,64]{1,0,4,3,2:T(8,128)(2,1)} reshape(bf16[1280,2048]{0,1:T(8,128)(2,1)} %copy.664) | data formatting | bytes 10485760 | tf_op jit(solution)/shard_map/reshape | solution.py:516
  589.7 12.7 %gather_fusion.7 = bf16[1280,2048]{1,0:T(8,128)(2,1)} fusion(bf16[512,2048]{1,0:T(8,128)(2,1)} %all-gather.5.cloned.1.call-done, s32[2048]{0:T(1024)S(1)} %copy-done.85), kind=kCustom, calls=%fused_computation.9 | custom fusion | bytes 10490880 | tf_op jit(solution)/shard_map/gather | solution.py:382
  602.4 8.6 copy.668
  621.5 12.5 %fusion.60 = f32[8,160,4,128]{3,1,2,0:T(8,128)S(1)} fusion(bf16[8,4,128,2048]{3,2,1,0:T(8,128)(2,1)} %bitcast.567, f32[8,160,2048]{2,1,0:T(8,128)} %bitcast.564, f32[8,160]{1,0:T(8,128)S(1)} %copy-done.59), kind=kOutput, calls=%fused_computation.104 | convolution fusion | flops 2689597440 | bytes 29889536 | tf_op jit(solution)/shard_map/ecd,ehjd->ehcj/dot_general | solution.py:391
  639.3 75.2 %while.29 = (s32[]{:T(128)}, f32[4,512,128]{2,1,0:T(8,128)}, f32[4,512,128]{2,1,0:T(8,128)}, f32[8,4,160,128]{3,2,1,0:T(8,128)}, s32[8,160]{1,0:T(8,128)}, /*ind...) while((s32[]{:T(128)}, f32[4,512,128]{2,1,0:T(8,128)}, ...), condition=%wide.region_34.36_spmd.clone, body=%wide.region_32.35_spmd.clone.sunk | while | flops 423853440 | bytes 33536660 | solution.py:428
  735.1 22.7 %all-reduce.1 = bf16[3584,16]{0,1:T(8,128)(2,1)} all-reduce(f32[3584,16]{0,1:T(8,128)} %pad_maximum_fusion.5), channel_id=1, replica_groups=mesh['dp'=8,'shard'=4] {'shard'}, use_global_device_ids=true, to_apply=%region_43.45 | all-reduce | flops 57344 | bytes 344064 | tf_op jit(solution)/shard_map/psum | solution.py:507
  760.6 7.9 multiply_reduce_fusion.1
  805.2 17.0 %reshape.704 = f32[8,160,8,4,64]{1,0,4,3,2:T(8,128)} reshape(f32[1280,2048]{0,1:T(8,128)} %copy.668) | data formatting | bytes 20971520 | tf_op jit(solution)/shard_map/convert_element_type | solution.py:382
  839.8 9.5 scatter_custom_fusion.5
  856.9 4.9 fusion.198
  868.4 11.8 %fusion.44 = f32[8,160,2048,1]{2,1,3,0:T(8,128)} fusion(bf16[8,4,160,64]{3,2,1,0:T(8,128)(2,1)S(1)} %copy-done.17, bf16[8,4,160,64]{3,2,1,0:T(8,128)(2,1)S(1)} %copy-done.15, bf16[8,2048,512]{2,1,0:T(8,128)(2,1)} %param.42), kind=kOutput, calls=%fused_computation.76 | convolution fusion | flops 2686976000 | bytes 28573696 | tf_op jit(solution)/shard_map/ehcj,edhj->ecd/dot_general | solution.py:437
  880.3 13.0 %fusion.50 = f32[8,160,2048]{2,1,0:T(8,128)} fusion(f32[8,160,2048,1]{2,1,3,0:T(8,128)} %fusion.44, pred[8,160]{1,0:T(8,128)(4,1)S(1)} %copy-done.98, f32[8,160,16]{1,2,0:T(8,128)S(1)} %copy-done.43, bf16[8,8,2048,16]{2,3,1,0:T(8,128)(2,1)} %param.49, s32[]{:T(128)S(6)} %select_n.165), kind=kOutput, calls=%fused_computation.83 | convolution fusion | flops 508559360 | bytes 21579012 | tf_op jit(solution)/shard_map/ecr,edr->ecd/dot_general | solution.py:439
  893.4 5.5 fusion.64
  898.9 25.3 %scatter_fusion.1 = f32[512,2048]{1,0:T(8,128)} fusion(f32[512,2048]{1,0:T(8,128)} %fusion.64, s32[1280]{0:T(1024)S(1)} %copy-done.87, f32[1280,2048]{1,0:T(8,128)} %bitcast.570), kind=kCustom, calls=%fused_computation.14 | custom fusion | flops 2621440 | bytes 31462400 | tf_op jit(solution)/shard_map/scatter-add | solution.py:448
  955.1 16.0 %reduce-scatter.18.cloned.1.call-done = bf16[128,2048]{1,0:T(8,128)(2,1)} async-done(((bf16[512,2048]{1,0:T(8,128)(2,1)}), bf16[128,2048]{1,0:T(8,128)(2,1)}) %reduce-scatter.18.cloned.1.call-update) | async-done | bytes 524304 | tf_op jit(solution)/shard_map/reduce_scatter | solution.py:480
  (738 shorter events, 430.4 us)
Async XLA Ops:
  7.2 113.4 %copy-start = (bf16[2048,512]{1,0:T(8,128)(2,1)S(1)}, bf16[2048,512]{1,0:T(8,128)(2,1)}, u32[]{:S(2)}) copy-start(bf16[2048,512]{1,0:T(8,128)(2,1)} %param.44) | copy-start | bytes 6291460
  7.2 53.9 %all-gather.3.cloned.1.call-start = ((), (), s32[]{:S(2)}) async-start(), calls=%async_computation.16 | async-start | bytes 2621440 | tf_op jit(solution)/shard_map/all_gather | solution.py:148
  12.5 234.1 %reduce-scatter.16.cloned.1.call-start = ((), (), s32[]{:S(2)}) async-start(), calls=%async_computation.17 | async-start | bytes 2621440 | tf_op jit(solution)/shard_map/reduce_scatter | solution.py:226
  15.9 147.2 %copy-start.99 = (s32[8]{0:T(128)}, s32[8]{0:T(128)S(1)}, u32[]{:S(2)}) copy-start(s32[8]{0:T(128)S(1)} %get-tuple-element.330) | copy-start | bytes 100
  19.4 66.6 %copy-start.89 = (bf16[16,4,128]{2,1,0:T(4,128)(2,1)}, bf16[16,4,128]{2,1,0:T(4,128)(2,1)S(1)}, u32[]{:S(2)}) copy-start(bf16[16,4,128]{2,1,0:T(4,128)(2,1)S(1)} %reshape_squeeze.16) | copy-start | bytes 49156
  20.4 94.7 %copy-start.48 = (bf16[8,16,4,128]{3,2,1,0:T(4,128)(2,1)}, bf16[8,16,4,128]{3,2,1,0:T(4,128)(2,1)S(1)}, u32[]{:S(2)}) copy-start(bf16[8,16,4,128]{3,2,1,0:T(4,128)(2,1)S(1)} %reshape_squeeze.15) | copy-start | bytes 393220
  21.4 131.4 %copy-start.50 = (bf16[8,4,128,16]{2,1,3,0:T(4,128)(2,1)}, bf16[8,4,128,16]{2,1,3,0:T(4,128)(2,1)S(1)}, u32[]{:S(2)}) copy-start(bf16[8,4,128,16]{2,1,3,0:T(4,128)(2,1)S(1)} %reshape_squeeze.18) | copy-start | bytes 393220
  39.3 21.8 %copy-start.77 = (bf16[2048,8]{0,1:T(8,128)(2,1)S(1)}, bf16[2048,8]{0,1:T(8,128)(2,1)}, u32[]{:S(2)}) copy-start(bf16[2048,8]{0,1:T(8,128)(2,1)} %param.40) | copy-start | bytes 98308
  44.5 42.2 %copy-start.44 = (f32[512,64]{0,1:T(8,128)}, f32[512,64]{0,1:T(8,128)S(1)}, u32[]{:S(2)}) copy-start(f32[512,64]{0,1:T(8,128)S(1)} %get-tuple-element.416) | copy-start | bytes 393220
  44.5 42.2 %copy-start.45 = (f32[512,64]{0,1:T(8,128)}, f32[512,64]{0,1:T(8,128)S(1)}, u32[]{:S(2)}) copy-start(f32[512,64]{0,1:T(8,128)S(1)} %get-tuple-element.417) | copy-start | bytes 393220
  48.1 68.2 %copy-start.28 = (f32[8,160,64]{2,1,0:T(8,128)}, f32[8,160,64]{2,1,0:T(8,128)S(1)}, u32[]{:S(2)}) copy-start(f32[8,160,64]{2,1,0:T(8,128)S(1)} %get-tuple-element.411) | copy-start | bytes 983044
  203.6 43.0 %copy-start.13 = (bf16[128,2048]{1,0:T(8,128)(2,1)S(1)}, bf16[128,2048]{1,0:T(8,128)(2,1)}, u32[]{:S(2)}) copy-start(bf16[128,2048]{1,0:T(8,128)(2,1)} %param.36) | copy-start | bytes 1572868
  203.6 46.2 %copy-start.68 = (f32[2048]{0:T(1024)}, f32[2048]{0:T(1024)S(1)}, u32[]{:S(2)}) copy-start(f32[2048]{0:T(1024)S(1)} %convert_element_type.274) | copy-start | bytes 24580
  209.2 41.0 %copy-start.90 = (s32[320]{0:T(512)}, s32[320]{0:T(512)S(1)}, u32[]{:S(2)}) copy-start(s32[320]{0:T(512)S(1)} %reshape.739) | copy-start | bytes 3844
  209.3 53.9 %copy-start.96 = (pred[8,40]{1,0:T(8,128)(4,1)}, pred[8,40]{1,0:T(8,128)(4,1)S(1)}, u32[]{:S(2)}) copy-start(pred[8,40]{1,0:T(8,128)(4,1)S(1)} %iota_compare_fusion.7) | copy-start | bytes 964
  256.5 9.3 all-to-all-start.1
  265.8 22.5 %all-to-all-start = ((bf16[8,40,2048]{2,1,0:T(8,128)(2,1)}), bf16[8,40,2048]{2,1,0:T(8,128)(2,1)}, u32[]{:S(2)}, u32[]{:S(2)}) async-start(bf16[8,40,2048]{2,1,0:T(8,128)(2,1)} %broadcast_select_fusion), calls=%async_computation.1 | async-start | bytes 2621440 | tf_op jit(solution)/shard_map/all_to_all | solution.py:278
  270.3 30.5 %copy-start.56 = (f32[8,40,16]{1,2,0:T(8,128)}, f32[8,40,16]{1,2,0:T(8,128)S(1)}, u32[]{:S(2)}) copy-start(f32[8,40,16]{1,2,0:T(8,128)S(1)} %get-tuple-element.409) | copy-start | bytes 61444
  270.3 46.9 %copy-start.64 = (f32[8,40,16]{1,2,0:T(8,128)}, f32[8,40,16]{1,2,0:T(8,128)S(1)}, u32[]{:S(2)}) copy-start(f32[8,40,16]{1,2,0:T(8,128)S(1)} %get-tuple-element.410) | copy-start | bytes 61444
  302.1 15.1 %copy-start.27 = (f32[8,40,5632]{2,1,0:T(8,128)}, f32[8,40,5632]{2,1,0:T(8,128)S(1)}, u32[]{:S(2)}) copy-start(f32[8,40,5632]{2,1,0:T(8,128)S(1)} %fusion.54) | copy-start | bytes 21626884
  302.1 15.1 %copy-start.118 = (bf16[8,16,5632]{2,1,0:T(8,128)(2,1)S(1)}, bf16[8,16,5632]{2,1,0:T(8,128)(2,1)}, u32[]{:S(2)}) copy-start(bf16[8,16,5632]{2,1,0:T(8,128)(2,1)} %param.60) | copy-start | bytes 4325380
  325.0 17.3 %all-to-all-start.3 = ((bf16[8,2,320]{2,1,0:T(2,128)(2,1)}), bf16[8,2,320]{2,1,0:T(2,128)(2,1)S(1)}, u32[]{:S(2)}, u32[]{:S(2)}) async-start(bf16[8,2,320]{2,1,0:T(2,128)(2,1)} %reshape.951), calls=%async_computation.4 | async-start | bytes 24576 | tf_op jit(solution)/shard_map/all_to_all | solution.py:291
  342.4 22.9 %all-to-all-start.2 = ((bf16[8,40,2048]{2,1,0:T(8,128)(2,1)}), bf16[8,40,2048]{2,1,0:T(8,128)(2,1)}, u32[]{:S(2)}, u32[]{:S(2)}) async-start(bf16[8,40,2048]{2,1,0:T(8,128)(2,1)} %fusion.78), calls=%async_computation.3 | async-start | bytes 2621440 | tf_op jit(solution)/shard_map/all_to_all | solution.py:288
  389.8 8.0 all-to-all-start.5
  397.8 22.5 %all-to-all-start.4 = ((bf16[8,40,2048]{2,1,0:T(8,128)(2,1)}), bf16[8,40,2048]{2,1,0:T(8,128)(2,1)}, u32[]{:S(2)}, u32[]{:S(2)}) async-start(bf16[8,40,2048]{2,1,0:T(8,128)(2,1)} %multiply_convert_fusion.5), calls=%async_computation.5 | async-start | bytes 2621440 | tf_op jit(solution)/shard_map/all_to_all | solution.py:316
  402.1 183.7 %reduce-scatter.28.cloned.1.call-start = ((), (), s32[]{:S(2)}) async-start(), calls=%async_computation.24 | async-start | bytes 1802240
  420.3 21.6 %copy-start.40 = (bf16[8,16,5632]{2,1,0:T(8,128)(2,1)S(1)}, bf16[8,16,5632]{2,1,0:T(8,128)(2,1)}, u32[]{:S(2)}) copy-start(bf16[8,16,5632]{2,1,0:T(8,128)(2,1)} %param.58) | copy-start | bytes 4325380
  449.8 18.1 %all-to-all-start.7 = ((bf16[8,2,640]{2,1,0:T(2,128)(2,1)}), bf16[8,2,640]{2,1,0:T(2,128)(2,1)S(1)}, u32[]{:S(2)}, u32[]{:S(2)}) async-start(bf16[8,2,640]{2,1,0:T(2,128)(2,1)} %reshape.955), calls=%async_computation.8 | async-start | bytes 40960 | tf_op jit(solution)/shard_map/all_to_all | solution.py:355
  453.1 134.5 %reduce-scatter.20.cloned.1.call-start = ((), (), s32[]{:S(2)}) async-start(), calls=%async_computation.20 | async-start | bytes 1966080 | tf_op jit(solution)/shard_map/reduce_scatter | solution.py:547
  497.5 22.6 %all-to-all-start.6 = ((bf16[8,40,2048]{2,1,0:T(8,128)(2,1)}), bf16[8,40,2048]{2,1,0:T(8,128)(2,1)}, u32[]{:S(2)}, u32[]{:S(2)}) async-start(bf16[8,40,2048]{2,1,0:T(8,128)(2,1)} %fusion.75), calls=%async_computation.7 | async-start | bytes 2621440 | tf_op jit(solution)/shard_map/all_to_all | solution.py:352
  501.9 87.8 %all-gather.5.cloned.1.call-start = ((), (), s32[]{:S(2)}) async-start(), calls=%async_computation.18 | async-start | bytes 2621440 | tf_op jit(solution)/shard_map/all_gather | solution.py:381
  502.0 20.2 %copy-start.97 = (pred[8,40]{1,0:T(8,128)(4,1)S(1)}, pred[8,40]{1,0:T(8,128)(4,1)}, u32[]{:S(2)}) copy-start(pred[8,40]{1,0:T(8,128)(4,1)} %copy-done.96) | copy-start | bytes 964
  535.1 393.9 %reduce-scatter.24.cloned.1.call-start = ((), (), s32[]{:S(2)}) async-start(), calls=%async_computation.22 | async-start | bytes 1802240
  540.7 390.4 %reduce-scatter.26.cloned.1.call-start = ((), (), s32[]{:S(2)}) async-start(), calls=%async_computation.23 | async-start | bytes 1802240
  621.5 15.3 %copy-start.51 = (bf16[8,4,128,16]{2,1,3,0:T(4,128)(2,1)S(1)}, bf16[8,4,128,16]{2,1,3,0:T(4,128)(2,1)}, u32[]{:S(2)}) copy-start(bf16[8,4,128,16]{2,1,3,0:T(4,128)(2,1)} %copy-done.50) | copy-start | bytes 393220
  835.2 21.6 %copy-start.80 = (f32[512,16]{0,1:T(8,128)S(1)}, f32[512,16]{0,1:T(8,128)}, u32[]{:S(2)}) copy-start(f32[512,16]{0,1:T(8,128)} %convolution_bitcast_fusion.13) | copy-start | bytes 98308
  852.5 83.9 %all-to-all-start.8 = ((bf16[8,480,128]{2,1,0:T(8,128)(2,1)}), bf16[8,480,128]{2,1,0:T(8,128)(2,1)}, u32[]{:S(2)}, u32[]{:S(2)}) async-start(bf16[8,480,128]{2,1,0:T(8,128)(2,1)} %copy.685), calls=%async_computation.11 | async-start | bytes 1966080 | tf_op jit(solution)/shard_map/all_to_all | solution.py:567
  856.8 76.4 %reduce-scatter.22.cloned.1.call-start = ((), (), s32[]{:S(2)}) async-start(), calls=%async_computation.21 | async-start | bytes 163840
  880.2 90.9 %reduce-scatter.18.cloned.1.call-start = ((), (), s32[]{:S(2)}) async-start(), calls=%async_computation.19 | async-start | bytes 2621440 | tf_op jit(solution)/shard_map/reduce_scatter | solution.py:480
  950.9 20.2 %copy-start.78 = (bf16[2048,8]{0,1:T(8,128)(2,1)S(1)}, bf16[2048,8]{0,1:T(8,128)(2,1)}, u32[]{:S(2)}) copy-start(bf16[2048,8]{0,1:T(8,128)(2,1)} %param.40) | copy-start | bytes 98308
  950.9 20.2 %copy-start.84 = (f32[2048]{0:T(1024)S(1)}, f32[2048]{0:T(1024)}, u32[]{:S(2)}) copy-start(f32[2048]{0:T(1024)} %copy-done.83) | copy-start | bytes 24580
  953.8 19.4 %copy-start.3 = (f32[128,2048]{1,0:T(8,128)S(1)}, f32[128,2048]{1,0:T(8,128)}, u32[]{:S(2)}) copy-start(f32[128,2048]{1,0:T(8,128)} %copy-done.2) | copy-start | bytes 3145732
  953.8 19.4 %copy-start.70 = (f32[2048]{0:T(1024)S(1)}, f32[2048]{0:T(1024)}, u32[]{:S(2)}) copy-start(f32[2048]{0:T(1024)} %copy-done.68) | copy-start | bytes 24580
  953.8 19.4 %copy-start.103 = (f32[128]{0:T(128)S(1)}, f32[128]{0:T(128)}, u32[]{:S(2)}) copy-start(f32[128]{0:T(128)} %copy-done.101) | copy-start | bytes 1540
  953.8 19.4 %copy-start.106 = (f32[128]{0:T(128)S(1)}, f32[128]{0:T(128)}, u32[]{:S(2)}) copy-start(f32[128]{0:T(128)} %copy-done.105) | copy-start | bytes 1540
  953.9 19.4 %copy-start.108 = (f32[128]{0:T(128)S(1)}, f32[128]{0:T(128)}, u32[]{:S(2)}) copy-start(f32[128]{0:T(128)} %get-tuple-element.420) | copy-start | bytes 1540
  953.9 19.4 %copy-start.110 = (f32[128]{0:T(128)S(1)}, f32[128]{0:T(128)}, u32[]{:S(2)}) copy-start(f32[128]{0:T(128)} %copy-done.109) | copy-start | bytes 1540
  953.9 19.4 %copy-start.113 = (f32[128]{0:T(128)S(1)}, f32[128]{0:T(128)}, u32[]{:S(2)}) copy-start(f32[128]{0:T(128)} %get-tuple-element.418) | copy-start | bytes 1540
  (119 other events, 569.2 us)
Sparse Core Ops, SparseCore 0:
  12.6 48.4 all-gather.2
  203.7 42.8 reduce-scatter.15
  412.5 33.0 reduce-scatter.27
  483.2 35.1 reduce-scatter.19
  535.2 43.5 all-gather.4
  581.1 31.9 reduce-scatter.23
  615.4 32.1 reduce-scatter.25
  880.3 18.1 reduce-scatter.21
  928.2 42.8 reduce-scatter.17

commit v2 on v1

v2 whole, which is shorter than its diff:
```python
import math

import jax
import jax.numpy as jnp
from jax import lax
from jax.experimental import pallas as pl
from jax.experimental.pallas import tpu as pltpu
from jax.sharding import PartitionSpec as P

D = 2048
HD = 128
EXPERTS = 8
ATT_EXPERTS = 8
ADAPTERS = 8
RANK = 16
LOW = 128
CHUNK = 128
GATE_LANE = 64
ROUTE_LANE = 96
ROUTER_ROW = 32


f32 = jnp.float32
bf16 = jnp.bfloat16
precise = lax.Precision.HIGHEST
eps = 1e-05
score_scale = HD ** (-0.5)


def nn(a, b):
    return lax.dot_general(a, b, (((1,), (0,)), ((), ())), preferred_element_type=f32)


def nt(a, b):
    return lax.dot_general(a, b, (((1,), (1,)), ((), ())), preferred_element_type=f32)


def tn(a, b):
    return lax.dot_general(a, b, (((0,), (0,)), ((), ())), preferred_element_type=f32)


def iota(shape, axis):
    return lax.broadcasted_iota(jnp.int32, shape, axis)


def ones_where(condition):
    return jnp.where(condition, 1.0, 0.0).astype(bf16)


def inverse_rms(values):
    return lax.rsqrt(jnp.mean(values * values, axis=-1, keepdims=True) + eps)


def norm_backward(values, inverse, gain_vector, grad_normed):
    weighted = gain_vector * grad_normed
    return inverse * weighted - values * (inverse * inverse * inverse) * jnp.mean(
        values * weighted, axis=-1, keepdims=True
    )


def softmax_pair(first, second):
    peak = jnp.maximum(first, second)
    one, two = jnp.exp(first - peak), jnp.exp(second - peak)
    total = one + two
    return one / total, two / total


def in_lane(column, lane, width=LOW):
    shape = (column.shape[0], width)
    return jnp.where(iota(shape, 1) == lane, column, 0.0)


def lane_of(values, lane):
    return jnp.sum(jnp.where(iota(values.shape, 1) == lane, values, 0.0), axis=1, keepdims=True)


def expert_lanes(dest, capacity, shape, group):
    lane = iota(shape, 1)
    low = (lane // group) * capacity
    return (dest >= low) & (dest < low + capacity)


def whole():
    return pl.BlockSpec(memory_space=pltpu.VMEM)


def sds(shape, dtype):
    return jax.ShapeDtypeStruct(shape, dtype)


def call(kernel, grid, in_specs, out_specs, out_shape, scratch, flops, moved):
    return pl.pallas_call(
        kernel,
        grid=grid,
        in_specs=in_specs,
        out_specs=out_specs,
        out_shape=out_shape,
        scratch_shapes=scratch,
        compiler_params=pltpu.CompilerParams(
            vmem_limit_bytes=60 * 1024 * 1024,
            dimension_semantics=("arbitrary",) * len(grid) if grid else None,
        ),
        cost_estimate=pl.CostEstimate(
            flops=4 * flops, bytes_accessed=4 * moved, transcendentals=0
        ),
    )


def rope(values, cosine, sine):
    return values * cosine + pltpu.roll(values, HD // 2, 1) * sine


def unrope(values, cosine, sine):
    return values * cosine - pltpu.roll(values, HD // 2, 1) * sine


def routed(route, shape):
    return (iota(shape, 1) // RANK) == route


def qkv_kernel(
    xn, wq, wk, wv, aq, amisc, bcat, kb, vb, routes, cosf, sinf,
    q_out, k_out, v_out, ga_out, low_out, misc_out, qsum,
):
    e = pl.program_id(0)
    s, width = k_out.shape
    heads = width // HD

    @pl.when(e == 0)
    def _():
        x = xn[...]
        low_out[...] = nt(x, aq[...]).astype(bf16)
        misc = nt(x, amisc[...])
        misc_out[...] = misc.astype(bf16)
        lane = iota((s, LOW), 1) - ROUTER_ROW
        gates = [
            jnp.sum(jnp.where(lane == routes[:, k : k + 1], misc, 0.0), axis=1, keepdims=True)
            for k in range(2)
        ]
        one, two = softmax_pair(*gates)
        ga_out[...] = in_lane(one, 0) + in_lane(two, 1)
        keys = nn(x, wk[...]) + nn(misc_out[...], kb[...])
        for h in range(heads):
            hs = slice(h * HD, (h + 1) * HD)
            k_out[:, hs] = rope(keys[:, hs], cosf[...], sinf[...]).astype(bf16)
        v_out[...] = (nn(x, wv[...]) + nn(misc_out[...], vb[...])).astype(bf16)
        for k in range(2):
            mine = routed(routes[:, k : k + 1], (s, LOW))
            low = jnp.where(mine, low_out[...], jnp.zeros((), bf16))
            qsum[k * s : (k + 1) * s, :] = nn(low, bcat[...])

    part = nn(xn[...], wq[0])
    for k in range(2):
        qsum[k * s : (k + 1) * s, :] += jnp.where(routes[:, k : k + 1] == e, part, 0.0)

    @pl.when(e == pl.num_programs(0) - 1)
    def _():
        for k in range(2):
            for h in range(heads):
                hs = slice(h * HD, (h + 1) * HD)
                at = slice(k * s, (k + 1) * s)
                q_out[at, hs] = rope(qsum[at, hs], cosf[...], sinf[...]).astype(bf16)


def causal(i, shape):
    row = (iota(shape, 0) & (CHUNK - 1)) + i * CHUNK
    return iota(shape, 1) <= row


def attend_kernel(q, k, v, ga, o_out, og_out, lse_out):
    s, width = k.shape
    for i in range(s // CHUNK):
        end = (i + 1) * CHUNK
        first, second = slice(i * CHUNK, end), slice(s + i * CHUNK, s + end)
        gates = [lane_of(ga[first, :], 0), lane_of(ga[first, :], 1)]
        log_totals = jnp.zeros((2 * CHUNK, LOW), f32)
        for h in range(width // HD):
            hs = slice(h * HD, (h + 1) * HD)
            queries = jnp.concatenate([q[first, hs], q[second, hs]], axis=0)
            scores = nt(queries, k[0:end, hs]) * score_scale
            scores = jnp.where(causal(i, scores.shape), scores, -1e30)
            peak = jnp.max(scores, axis=1, keepdims=True)
            weights = jnp.exp(scores - peak)
            total = jnp.sum(weights, axis=1, keepdims=True)
            mixed = nn(weights.astype(bf16), v[0:end, hs]) / total
            o_out[first, hs] = mixed[:CHUNK].astype(bf16)
            o_out[second, hs] = mixed[CHUNK:].astype(bf16)
            og_out[first, hs] = (mixed[:CHUNK] * gates[0]).astype(bf16)
            og_out[second, hs] = (mixed[CHUNK:] * gates[1]).astype(bf16)
            log_totals = log_totals + in_lane(peak + jnp.log(total), h)
        lse_out[first, :] = log_totals[:CHUNK]
        lse_out[second, :] = log_totals[CHUNK:]


def of_expert_rows(rows, routes, expert, s):
    return rows[0:s, :] * ones_where(routes[:, 0:1] == expert) + rows[s : 2 * s, :] * ones_where(
        routes[:, 1:2] == expert
    )


def out_kernel(og, wo, oa, ob, routes, attn_out, low_out, total):
    step = pl.program_id(0)
    s = attn_out.shape[0]
    batch = wo.shape[0]

    @pl.when(step == 0)
    def _():
        low = jnp.zeros((s, LOW), f32)
        for k in range(2):
            part = nt(og[k * s : (k + 1) * s, :], oa[...])
            low = low + jnp.where(routed(routes[:, k : k + 1], (s, LOW)), part, 0.0)
        low_out[...] = low.astype(bf16)
        total[...] = nn(low_out[...], ob[...])

    part = None
    for j in range(batch):
        new = nn(of_expert_rows(og, routes, step * batch + j, s), wo[j])
        part = new if part is None else part + new
    total[...] += part

    @pl.when(step == pl.num_programs(0) - 1)
    def _():
        attn_out[...] = total[...].astype(bf16)


def second_norm(attn, tokens, gain):
    hidden = tokens[...].astype(f32) + attn[...].astype(f32)
    inverse = inverse_rms(hidden)
    return hidden, inverse, gain[...].astype(f32)


def dispatch_kernel(cap, attn, tokens, cot, gain, router, mrow, mcol, rows_out, grads_out, gm_out, m_out):
    hidden, inverse, scale = second_norm(attn, tokens, gain)
    m = (hidden * inverse * scale).astype(bf16)
    m_out[...] = m
    logits = nt(m, router[...])
    gates = softmax_pair(
        *[
            jnp.sum(
                jnp.where(
                    expert_lanes(mcol[:, k : k + 1], cap, logits.shape, 1),
                    logits,
                    0.0,
                ),
                axis=1,
                keepdims=True,
            )
            for k in range(2)
        ]
    )
    gm_out[...] = in_lane(gates[0], 0) + in_lane(gates[1], 1)
    slot = iota((rows_out.shape[0], mrow.shape[1]), 0)
    picks = [ones_where(mrow[k : k + 1, :] == slot) for k in range(2)]
    rows_out[...] = nn(picks[0] + picks[1], m).astype(bf16)
    grad = cot[...].astype(f32)
    grads_out[...] = (
        nn(picks[0], (gates[0] * grad).astype(bf16)) + nn(picks[1], (gates[1] * grad).astype(bf16))
    ).astype(bf16)


def fold(first_lane):
    row, column = iota((LOW, LOW), 0), iota((LOW, LOW), 1)
    return ones_where(column == (row & (RANK - 1)) + first_lane)


def spread(first_lane):
    row, column = iota((LOW, LOW), 0), iota((LOW, LOW), 1)
    return ones_where(row == (column & (RANK - 1)) + first_lane)


def combine_kernel(cap, ze, attn, tokens, cot, gm, mcol, layer_out, dlm_out, low_out):
    hidden = tokens[...].astype(f32) + attn[...].astype(f32)
    grad = cot[...].astype(f32)
    lane = iota((mcol.shape[0], ze.shape[0]), 1)
    gates, slopes, lows = [], [], []
    for k in range(2):
        gates.append(lane_of(gm[...], k))
        pick = ones_where(mcol[:, k : k + 1] == lane)
        expert_out = nn(pick, ze[:, 0:D])
        lows.append(gates[k] * nn(pick, ze[:, D : D + LOW]))
        slopes.append(jnp.sum(grad * expert_out, axis=1, keepdims=True))
        hidden = hidden + gates[k] * expert_out
    layer_out[...] = hidden.astype(bf16)
    low_out[...] = lows[0] + pltpu.roll(lows[1], 3 * RANK, 1)
    mean = gates[0] * slopes[0] + gates[1] * slopes[1]
    total = jnp.zeros(dlm_out.shape, f32)
    for k in range(2):
        mine = expert_lanes(mcol[:, k : k + 1], cap, dlm_out.shape, 1)
        total = total + jnp.where(mine, gates[k] * (slopes[k] - mean), 0.0)
    dlm_out[...] = total.astype(bf16)


def hidden_grad_kernel(
    rows, dlm, low, attn, tokens, cot, gain, router, mcol, routes, dh1_out, da_out, low_out
):
    hidden, inverse, scale = second_norm(attn, tokens, gain)
    lane = iota((mcol.shape[0], rows.shape[0]), 1)
    picks = [ones_where(mcol[:, k : k + 1] == lane) for k in range(2)]
    grad_m = nn(picks[0] + picks[1], rows[:, 0:D]) + nn(dlm[...], router[...])
    lows = [nn(pick, rows[:, D : D + LOW]) for pick in picks]
    total = low[...] + lows[0] + pltpu.roll(lows[1], 3 * RANK, 1)
    for k in range(2):
        total = total + in_lane(routes[:, k : k + 1].astype(f32), ROUTE_LANE + k)
    low_out[...] = total.astype(bf16)
    grad = cot[...].astype(f32) + norm_backward(hidden, inverse, scale, grad_m)
    dh1_out[...] = grad
    da_out[...] = grad.astype(bf16)


def factor_kernel(low, columns, out):
    own = columns.shape[1] // 2
    count = low.shape[0]
    lane = (iota((count, LOW), 1) // RANK).astype(f32)
    lows = low[...]
    mine = [lane_of(lows.astype(f32), ROUTE_LANE + k) == lane for k in range(2)]
    for part in range(3):
        dense = jnp.zeros((count, LOW), f32)
        for k in range(2):
            wide = nn(lows, spread((3 * k + part) * RANK))
            dense = dense + jnp.where(mine[k], wide, 0.0)
        at = slice(own, 2 * own) if part == 2 else slice(0, own)
        out[part * LOW : (part + 1) * LOW, :] = tn(dense.astype(bf16), columns[:, at]).astype(bf16)


def expert_kernel(
    x, mask, ga, ua, db, gate_w, up_w, down_w, gate_b, up_b, down_a,
    ze_out, g_out, u_out, h_out, lg_out, lu_out, pd_out, total, pd,
):
    f = pl.program_id(0)

    @pl.when(f == 0)
    def _():
        lg_out[...] = nt(x[...], ga[...]).astype(bf16) * mask[...]
        lu_out[...] = nt(x[...], ua[...]).astype(bf16) * mask[...]
        total[...] = jnp.zeros_like(total)
        pd[...] = jnp.zeros_like(pd)

    gate = nn(x[...], gate_w[...]) + nn(lg_out[...], gate_b[...])
    up = nn(x[...], up_w[...]) + nn(lu_out[...], up_b[...])
    g_out[...] = gate.astype(bf16)
    u_out[...] = up.astype(bf16)
    hidden = (gate * jax.nn.sigmoid(gate) * up).astype(bf16)
    h_out[...] = hidden
    total[...] += nn(hidden, down_w[...])
    pd[...] += nt(hidden, down_a[...])

    @pl.when(f == pl.num_programs(0) - 1)
    def _():
        pd_out[...] = pd[...].astype(bf16) * mask[...]
        ze_out[:, 0:D] = (total[...] + nn(pd_out[...], db[...])).astype(bf16)
        ze_out[:, D : D + LOW] = nn(pd_out[...], fold(2 * RANK)).astype(bf16)


def identity():
    return ones_where(iota((LOW, LOW), 0) == iota((LOW, LOW), 1))


def down_grads_kernel(dy, mask, db, h, dpd_out, table_out, dpd_t):
    @pl.when(pl.program_id(0) == 0)
    def _():
        dpd_out[...] = nt(dy[...], db[...]).astype(bf16) * mask[...]
        dpd_t[...] = nt(identity(), dpd_out[...]).astype(bf16)

    table_out[0] = nn(dpd_t[...], h[...]).astype(bf16)


def expert_back_kernel(
    first, last,
    dy, mask, ga, ua, dpd, lg, lu, total_in, dlg_in, dlu_in,
    g, u, gate_w, up_w, down_w, gate_b, up_b, down_a,
    total, dlg, dlu, dm_out, tables_out, lg_t, lu_t,
):
    f = pl.program_id(0)

    @pl.when(f == 0)
    def _():
        lg_t[...] = nt(identity(), lg[...]).astype(bf16)
        lu_t[...] = nt(identity(), lu[...]).astype(bf16)
        if first:
            total[...] = jnp.zeros_like(total)
            dlg[...] = jnp.zeros_like(dlg)
            dlu[...] = jnp.zeros_like(dlu)
        else:
            total[...] = total_in[...]
            dlg[...] = dlg_in[...]
            dlu[...] = dlu_in[...]

    dh = nt(dy[...], down_w[...]) + nn(dpd[...], down_a[...])
    gate = g[...].astype(f32)
    up = u[...].astype(f32)
    sig = jax.nn.sigmoid(gate)
    act = gate * sig
    dgate = (dh * up * (sig + act * (1.0 - sig))).astype(bf16)
    dup = (dh * act).astype(bf16)
    total[...] += nt(dgate, gate_w[...]) + nt(dup, up_w[...])
    dlg[...] += nt(dgate, gate_b[...])
    dlu[...] += nt(dup, up_b[...])
    tables_out[0, 0:LOW, :] = nn(lg_t[...], dgate).astype(bf16)
    tables_out[0, LOW : 2 * LOW, :] = nn(lu_t[...], dup).astype(bf16)

    if last:

        @pl.when(f == pl.num_programs(0) - 1)
        def _():
            dlg_m = dlg[...].astype(bf16) * mask[...]
            dlu_m = dlu[...].astype(bf16) * mask[...]
            total_grad = total[...] + nn(dlg_m, ga[...]) + nn(dlu_m, ua[...])
            dm_out[:, 0:D] = total_grad.astype(bf16)
            dm_out[:, D : D + LOW] = (nn(dlg_m, fold(0)) + nn(dlu_m, fold(RANK))).astype(bf16)


def out_back_kernel(
    da, wo, oa, ob, routes, ga, o, do_out, stats_out, grad_oa_out, dzl, dosum
):
    e = pl.program_id(0)
    s = da.shape[0]
    width = o.shape[1]

    @pl.when(e == 0)
    def _():
        dzl[...] = nt(da[...], ob[...])
        for k in range(2):
            mine = routed(routes[:, k : k + 1], (s, LOW))
            low = jnp.where(mine, dzl[...], 0.0).astype(bf16)
            dosum[k * s : (k + 1) * s, :] = nn(low, oa[...])

    part = nt(da[...], wo[0])
    for k in range(2):
        dosum[k * s : (k + 1) * s, :] += jnp.where(routes[:, k : k + 1] == e, part, 0.0)

    @pl.when(e == pl.num_programs(0) - 1)
    def _():
        grad_oa = jnp.zeros((LOW, width), f32)
        for k in range(2):
            at = slice(k * s, (k + 1) * s)
            gate = lane_of(ga[...], k)
            mine = routed(routes[:, k : k + 1], (s, LOW))
            low = jnp.where(mine, gate * dzl[...], 0.0).astype(bf16)
            grad_oa = grad_oa + tn(low, o[at, :])
            stats = jnp.zeros((s, LOW), f32)
            slope = jnp.zeros((s, 1), f32)
            for h in range(width // HD):
                hs = slice(h * HD, (h + 1) * HD)
                before = dosum[at, hs]
                part = jnp.sum(o[at, hs].astype(f32) * before, axis=1, keepdims=True)
                slope = slope + part
                stats = stats + in_lane(gate * part, h)
                do_out[at, hs] = (gate * before).astype(bf16)
            stats_out[at, :] = stats + in_lane(slope, GATE_LANE)
        grad_oa_out[...] = grad_oa.astype(bf16)


def attend_back_kernel(
    q, k, v, do, lse, stats, cosf, sinf, bcat, kb, vb, low, misc, routes,
    dq_out, dk_out, dv_out, lows_out, misc_back_out, grad_qb_out, grad_kv_out, dk_sum, dv_sum,
):
    s, width = k.shape
    for h in range(width // HD):
        hs = slice(h * HD, (h + 1) * HD)
        dk_sum[...] = jnp.zeros_like(dk_sum)
        dv_sum[...] = jnp.zeros_like(dv_sum)
        for i in range(s // CHUNK):
            end = (i + 1) * CHUNK
            first, second = slice(i * CHUNK, end), slice(s + i * CHUNK, s + end)
            queries = jnp.concatenate([q[first, hs], q[second, hs]], axis=0)
            grads = jnp.concatenate([do[first, hs], do[second, hs]], axis=0)
            logs = jnp.concatenate(
                [lane_of(lse[first, :], h), lane_of(lse[second, :], h)], axis=0
            )
            centre = jnp.concatenate(
                [lane_of(stats[first, :], h), lane_of(stats[second, :], h)], axis=0
            )
            scores = nt(queries, k[0:end, hs]) * score_scale
            weights = jnp.where(causal(i, scores.shape), jnp.exp(scores - logs), 0.0)
            dscores = (weights * (nt(grads, v[0:end, hs]) - centre)).astype(bf16)
            dq = nn(dscores, k[0:end, hs]) * score_scale
            cosine, sine = cosf[first, :], sinf[first, :]
            dq_out[first, hs] = unrope(dq[:CHUNK], cosine, sine).astype(bf16)
            dq_out[second, hs] = unrope(dq[CHUNK:], cosine, sine).astype(bf16)
            dk_sum[0:end, :] += tn(dscores, queries)
            dv_sum[0:end, :] += tn(weights.astype(bf16), grads)
        dk_out[:, hs] = unrope(dk_sum[...] * score_scale, cosf[...], sinf[...]).astype(bf16)
        dv_out[:, hs] = dv_sum[...].astype(bf16)
    row, column = iota((LOW, LOW), 0), iota((LOW, LOW), 1)
    grad_qb = jnp.zeros((LOW, width), f32)
    for i in range(s // CHUNK):
        rs = slice(i * CHUNK, (i + 1) * CHUNK)
        misc_back = (nt(dk_out[rs, :], kb[...]) + nt(dv_out[rs, :], vb[...])).astype(bf16)
        lows = nn(misc_back, ones_where((column == row + 2 * RANK) & (row < 2 * RANK)))
        dense = jnp.zeros((CHUNK, LOW), f32)
        for j in range(2):
            at = slice(j * s + i * CHUNK, j * s + (i + 1) * CHUNK)
            mine = routed(routes[rs, j : j + 1], (CHUNK, LOW))
            part = jnp.where(mine, nt(dq_out[at, :], bcat[...]), 0.0).astype(bf16)
            dense = dense + part.astype(f32)
            fold = ones_where((column == (row & (RANK - 1)) + j * RANK) & (column < 2 * RANK))
            lows = lows + nn(part, fold)
            lows = lows + in_lane(lane_of(stats[at, :], GATE_LANE), GATE_LANE + j)
            grad_qb = grad_qb + tn(
                jnp.where(mine, low[rs, :], jnp.zeros((), bf16)), dq_out[at, :]
            )
        lows_out[rs, :] = lows.astype(bf16)
        misc_back_out[rs, 0:LOW] = dense.astype(bf16)
        misc_back_out[rs, LOW : 2 * LOW] = misc_back
    grad_qb_out[...] = grad_qb.astype(bf16)
    grad_kv_out[0:LOW, :] = tn(misc[...], dk_out[...]).astype(bf16)
    grad_kv_out[LOW : 2 * LOW, :] = tn(misc[...], dv_out[...]).astype(bf16)


def rows_back_kernel(dq, wq, dk, dv, wk, wv, aq, amisc, lows, routes, dx_out, total):
    step = pl.program_id(0)
    s = dk.shape[0]
    batch = wq.shape[0]

    @pl.when(step == 0)
    def _():
        total[...] = (
            nn(lows[:, 0:LOW], aq[...])
            + nn(lows[:, LOW : 2 * LOW], amisc[...])
            + nt(dk[...], wk[...])
            + nt(dv[...], wv[...])
        )

    part = None
    for j in range(batch):
        new = nt(of_expert_rows(dq, routes, step * batch + j, s), wq[j])
        part = new if part is None else part + new
    total[...] += part

    @pl.when(step == pl.num_programs(0) - 1)
    def _():
        dx_out[...] = total[...].astype(bf16)


def input_grad_kernel(dx, slopes, ga, tokens, gain, amisc, dh1, routes, out):
    x = tokens[...].astype(f32)
    gates = [lane_of(ga[...], k) for k in range(2)]
    slope = [lane_of(slopes[...].astype(f32), GATE_LANE + k) for k in range(2)]
    mean = gates[0] * slope[0] + gates[1] * slope[1]
    total = jnp.zeros(ga.shape, f32)
    lane = iota(ga.shape, 1) - ROUTER_ROW
    for k in range(2):
        mine = lane == routes[:, k : k + 1]
        total = total + jnp.where(mine, gates[k] * (slope[k] - mean), 0.0)
    grad = dx[...].astype(f32) + nn(total.astype(bf16), amisc[...])
    out[...] = dh1[...] + norm_backward(x, inverse_rms(x), gain[...].astype(f32), grad)


def after(value, *earlier):
    return lax.optimization_barrier((value, *earlier))[0]


def slot_places(routes, expert_count, capacity):
    choose = (routes[:, :, None] == jnp.arange(expert_count, dtype=jnp.int32)).astype(bf16)
    member = choose[:, 0] + choose[:, 1]
    count = routes.shape[0]
    before = (iota((count, count), 1) < iota((count, count), 0)).astype(bf16)
    slots = nn(before, member)
    mine = jnp.sum(slots[:, None, :] * choose.astype(f32), axis=2)
    return routes * capacity + mine.astype(jnp.int32)


def rotary_tables(count):
    half = HD // 2
    freq = jnp.exp(jnp.arange(half, dtype=f32) * (-2.0 * math.log(10000.0) / HD))
    angles = jnp.arange(count, dtype=jnp.int32).astype(f32)[:, None] * freq
    cosine, sine = jnp.cos(angles), jnp.sin(angles)
    return (
        jnp.concatenate([cosine, cosine], axis=1),
        jnp.concatenate([-sine, sine], axis=1),
    )


def on_device(
    tokens, cotangent, gain_first, gain_second, router_attn, router_mlp, query_w, key_w, value_w,
    output_w, gate_w, up_w, down_w, query_a, query_b, key_a, key_b, value_a, value_b, output_a,
    output_b, gate_a, gate_b, up_a, up_b, down_a, down_b, adapter_ids, attn_routes, mlp_routes,
):
    shards = lax.axis_size("shard")
    groups = lax.axis_size("dp")
    shard_at = lax.axis_index("shard")
    group_at = lax.axis_index("dp")
    rows = tokens.shape[0]
    seq = rows * shards
    cap_mlp = rows // 4 + rows // 16
    slices = groups // EXPERTS
    ff = gate_w.shape[1]
    width = key_w.shape[1]
    block = D // (groups * shards)
    own = groups * block
    adapter = adapter_ids[group_at]
    expert = group_at // slices

    x = tokens.astype(f32)
    normed = (x * inverse_rms(x) * gain_first.astype(f32)).astype(bf16)
    xn = lax.all_gather(normed, "shard", axis=0, tiled=True)

    mcol = slot_places(mlp_routes, EXPERTS, cap_mlp)
    mrow = mcol.T
    cosf, sinf = rotary_tables(seq)

    def ranks_first(factor):
        return jnp.swapaxes(factor, -1, -2)

    def of_adapter(factor, axis):
        return lax.dynamic_index_in_dim(factor, adapter, axis, keepdims=False)

    def pad_rows(parts, count=LOW):
        have = sum(p.shape[0] for p in parts)
        fill = jnp.zeros((count - have, parts[0].shape[1]), bf16)
        return jnp.concatenate(list(parts) + [fill], axis=0)

    aq = of_adapter(ranks_first(query_a), 1).reshape(LOW, D)
    amisc = pad_rows(
        [of_adapter(ranks_first(key_a), 0), of_adapter(ranks_first(value_a), 0), router_attn.T]
    )
    bcat = of_adapter(query_b, 1).reshape(LOW, width)
    key_second, value_second = of_adapter(key_b, 0), of_adapter(value_b, 0)
    kb = pad_rows([key_second])
    vb = pad_rows([jnp.zeros_like(value_second), value_second])
    oa = of_adapter(ranks_first(output_a), 1).reshape(LOW, width)
    ob = of_adapter(output_b, 1).reshape(LOW, D)
    router = pad_rows([router_mlp.T])
    gain1, gain2 = gain_first.reshape(1, D), gain_second.reshape(1, D)

    def of_expert(factor):
        return lax.dynamic_index_in_dim(factor, expert, 0, keepdims=False).reshape(LOW, D)

    gate_first = of_expert(ranks_first(gate_a))
    up_first = of_expert(ranks_first(up_a))
    down_second = of_expert(down_b)
    gate_table = gate_b.reshape(LOW, ff)
    up_table = up_b.reshape(LOW, ff)
    down_table = ranks_first(down_a).reshape(LOW, ff)
    expert_rows = groups * cap_mlp
    source_adapter = jnp.repeat(adapter_ids, cap_mlp)
    mask = (
        source_adapter[:, None] == (jnp.arange(LOW, dtype=jnp.int32) // RANK)[None, :]
    ).astype(bf16)

    experts = (ATT_EXPERTS,)
    batch = 2
    batches = (ATT_EXPERTS // batch,)
    projection = pl.BlockSpec((1, D, width), lambda e: (e, 0, 0))
    projections = pl.BlockSpec((batch, D, width), lambda e: (e, 0, 0))
    out_projection = pl.BlockSpec((1, width, D), lambda e: (e, 0, 0))
    out_projections = pl.BlockSpec((batch, width, D), lambda e: (e, 0, 0))
    project_flops = 2 * ATT_EXPERTS * seq * D * width
    weight_bytes = 2 * ATT_EXPERTS * D * width

    q, k, v, ga, low, misc = call(
        qkv_kernel,
        experts,
        [whole(), projection] + [whole()] * 10,
        [whole()] * 6,
        [
            sds((2 * seq, width), bf16),
            sds((seq, width), bf16),
            sds((seq, width), bf16),
            sds((seq, LOW), f32),
            sds((seq, LOW), bf16),
            sds((seq, LOW), bf16),
        ],
        [pltpu.VMEM((2 * seq, width), f32)],
        project_flops,
        weight_bytes,
    )(xn, query_w, key_w, value_w, aq, amisc, bcat, kb, vb, attn_routes, cosf, sinf)

    o, og, lse = call(
        attend_kernel,
        (),
        [whole()] * 4,
        [whole()] * 3,
        [
            sds((2 * seq, width), bf16),
            sds((2 * seq, width), bf16),
            sds((2 * seq, LOW), f32),
        ],
        [],
        8 * seq * seq * width,
        16 * seq * width,
    )(q, k, v, ga)

    attn_part, low_part = call(
        out_kernel,
        batches,
        [whole(), out_projections] + [whole()] * 3,
        [whole()] * 2,
        [sds((seq, D), bf16), sds((seq, LOW), bf16)],
        [pltpu.VMEM((seq, D), f32)],
        project_flops,
        weight_bytes,
    )(og, output_w, oa, ob, attn_routes)

    attn = lax.psum_scatter(attn_part, "shard", scatter_dimension=0, tiled=True)

    sent_rows = EXPERTS * cap_mlp
    rows_sent, grads_sent, gm, m = call(
        lambda *refs: dispatch_kernel(cap_mlp, *refs),
        (),
        [whole()] * 7,
        [whole()] * 4,
        [
            sds((sent_rows, D), bf16),
            sds((sent_rows, D), bf16),
            sds((rows, LOW), f32),
            sds((rows, D), bf16),
        ],
        [],
        6 * sent_rows * rows * D,
        8 * sent_rows * D,
    )(attn, tokens, cotangent, gain2, router, mrow, mcol)

    def to_experts(sent):
        sent = jnp.repeat(sent.reshape(EXPERTS, cap_mlp, D), slices, axis=0)
        got = lax.all_to_all(sent, "dp", split_axis=0, concat_axis=0, tiled=True)
        return got.reshape(expert_rows, D)

    def from_experts(made):
        got = lax.all_to_all(
            made.reshape(groups, cap_mlp, D + LOW), "dp", split_axis=0, concat_axis=0, tiled=True
        )
        if slices > 1:
            parts = got.reshape(EXPERTS, slices, cap_mlp, D + LOW).astype(f32)
            got = jnp.sum(parts, axis=1).astype(bf16)
        return got.reshape(sent_rows, D + LOW)

    def shifted(part, step):
        pairs = [(i, (i + step) % shards) for i in range(shards)]
        return lax.ppermute(part, "shard", pairs)

    def by_column_owner(part):
        split = part.reshape(rows, groups, shards, block)
        return split.transpose(2, 0, 1, 3).reshape(shards, rows, own)

    columns_sent = jnp.concatenate([by_column_owner(m), by_column_owner(cotangent)], axis=2)
    low_lanes = low_part.reshape(shards, rows, LOW).transpose(1, 0, 2).reshape(rows, shards * LOW)
    arrived = []
    for step in range(shards):
        piece = lax.dynamic_index_in_dim(
            columns_sent, lax.rem(shard_at + step, shards), 0, keepdims=False
        )
        piece = jnp.concatenate([piece, low_lanes], axis=1)
        arrived.append(shifted(piece, step) if step else piece)

    rows_in = to_experts(rows_sent)
    grads_in = to_experts(grads_sent)

    steps = 11
    each = ff // shards
    aligned = each % LOW == 0

    def spans(offset, span):
        if aligned:
            count, span = shards, span
            at = lambda f: pl.multiple_of(f * each + offset, LOW)
        else:
            count, span = steps, ff // steps
            at = lambda f: pl.multiple_of(f * (ff // steps), LOW)
        columns = pl.BlockSpec((pl.Element(D), pl.Element(span)), lambda f: (0, at(f)))
        weight_rows = pl.BlockSpec((pl.Element(span), pl.Element(D)), lambda f: (at(f), 0))
        table = pl.BlockSpec((pl.Element(LOW), pl.Element(span)), lambda f: (0, at(f)))
        kept = pl.BlockSpec((pl.Element(expert_rows), pl.Element(span)), lambda f: (0, at(f)))
        return count, span, columns, weight_rows, table, kept

    def by_shard(table):
        if aligned:
            return table
        return table.transpose(1, 0, 2).reshape(-1, shards, each).transpose(1, 0, 2)

    fb = ff // steps
    columns = pl.BlockSpec((D, fb), lambda f: (0, f))
    weight_rows = pl.BlockSpec((fb, D), lambda f: (f, 0))
    table = pl.BlockSpec((LOW, fb), lambda f: (0, f))
    kept = pl.BlockSpec((expert_rows, fb), lambda f: (0, f))
    expert_flops = 6 * expert_rows * D * ff
    expert_bytes = 6 * D * ff

    low_shape = sds((expert_rows, LOW), bf16)
    ze, g, u, hid, lg, lu, _ = call(
        expert_kernel,
        (steps,),
        [whole()] * 5 + [columns, columns, weight_rows, table, table, table],
        [whole(), kept, kept, kept, whole(), whole(), whole()],
        [sds((expert_rows, D + LOW), bf16)]
        + [sds((expert_rows, ff), bf16)] * 3
        + [low_shape, low_shape, low_shape],
        [pltpu.VMEM((expert_rows, D), f32), pltpu.VMEM((expert_rows, LOW), f32)],
        expert_flops,
        expert_bytes,
    )(rows_in, mask, gate_first, up_first, down_second, gate_w, up_w, down_w, gate_table, up_table, down_table)

    ze_back = from_experts(ze)

    hid, *arrived = lax.optimization_barrier((hid, *arrived))
    arrived = jnp.concatenate(arrived, axis=0)
    mlp_columns = arrived[:, : 2 * own]
    out_lows = jnp.sum(
        arrived[:, 2 * own :].reshape(shards, rows, shards, LOW).astype(f32), axis=0
    )
    out_lows = out_lows.astype(bf16).transpose(1, 0, 2).reshape(seq, LOW)

    count, span, _, _, _, kept = spans(0, each)
    dpd, down_part = call(
        down_grads_kernel,
        (count,),
        [whole()] * 3 + [kept],
        [whole(), pl.BlockSpec((1, LOW, span), lambda f: (f, 0, 0))],
        [low_shape, sds((count, LOW, span), bf16)],
        [pltpu.VMEM((LOW, expert_rows), bf16)],
        2 * expert_rows * LOW * ff,
        2 * expert_rows * ff,
    )(grads_in, mask, down_second, hid)

    def table_sum(part):
        part = by_shard(part)
        part = part.reshape(-1, part.shape[-1])
        return lax.psum_scatter(part, "shard", scatter_dimension=0, tiled=True)

    down_sum = table_sum(down_part)

    head = ((each // LOW + 1) // 2) * LOW
    pieces = [(0, head), (head, each - head)] if aligned else [(0, each)]
    low_sum = sds((expert_rows, LOW), f32)
    running = (jnp.zeros((8, LOW), f32),) * 3
    pair_parts = []
    for at, size in pieces:
        first, last = at == 0, at + size == each
        if not first:
            running = after(running, down_sum, ze_back)
        count, span, columns, weight_rows, table, kept = spans(at, size)
        made = call(
            lambda *refs, first=first, last=last: expert_back_kernel(first, last, *refs),
            (count,),
            [whole()] * 10
            + [kept, kept, columns, columns, weight_rows, table, table, table],
            [whole()] * 4 + [pl.BlockSpec((1, 2 * LOW, span), lambda f: (f, 0, 0))],
            [
                sds((expert_rows, D), f32),
                low_sum,
                low_sum,
                sds((expert_rows, D + LOW) if last else (16, LOW), bf16),
                sds((count, 2 * LOW, span), bf16),
            ],
            [pltpu.VMEM((LOW, expert_rows), bf16), pltpu.VMEM((LOW, expert_rows), bf16)],
            expert_flops * size // each,
            expert_bytes * size // each,
        )(grads_in, mask, gate_first, up_first, dpd, lg, lu, *running, g, u, gate_w, up_w, down_w, gate_table, up_table, down_table)
        running = made[:3]
        dm = made[3]
        pair_parts.append(made[4])

    dm_back = from_experts(dm)
    head_tables = table_sum(pair_parts[0])

    layer_out, dlm, low_down = call(
        lambda *refs: combine_kernel(cap_mlp, *refs),
        (),
        [whole()] * 6,
        [whole()] * 3,
        [sds((rows, D), bf16), sds((rows, LOW), bf16), sds((rows, LOW), f32)],
        [],
        4 * sent_rows * rows * D,
        4 * sent_rows * D,
    )(ze_back, attn, tokens, cotangent, gm, mcol)

    dm_back = after(dm_back, head_tables)
    dh1, da_own, low_mlp = call(
        hidden_grad_kernel,
        (),
        [whole()] * 10,
        [whole()] * 3,
        [sds((rows, D), f32), sds((rows, D), bf16), sds((rows, LOW), bf16)],
        [],
        2 * sent_rows * rows * D,
        4 * sent_rows * D,
    )(dm_back, dlm, low_down, attn, tokens, cotangent, gain2, router, mcol, mlp_routes)

    da = lax.all_gather(da_own, "shard", axis=0, tiled=True)
    mlp_lows = jnp.concatenate(
        [low_mlp] + [shifted(low_mlp, step) for step in range(1, shards)], axis=0
    )
    mlp_lows = after(mlp_lows, da)
    pair_tables = [head_tables] + [table_sum(after(part, da)) for part in pair_parts[1:]]
    factors = call(
        factor_kernel,
        (),
        [whole()] * 2,
        whole(),
        sds((3 * LOW, own), bf16),
        [],
        6 * seq * LOW * own,
        4 * seq * own,
    )(mlp_lows, mlp_columns)

    do, stats, grad_oa = call(
        out_back_kernel,
        experts,
        [whole(), out_projection] + [whole()] * 5,
        [whole()] * 3,
        [
            sds((2 * seq, width), bf16),
            sds((2 * seq, LOW), f32),
            sds((LOW, width), bf16),
        ],
        [pltpu.VMEM((seq, LOW), f32), pltpu.VMEM((2 * seq, width), f32)],
        project_flops,
        weight_bytes,
    )(da, output_w, oa, ob, attn_routes, ga, o)

    dq, dk, dv, lows, lows_dense, grad_qb, grad_kv = call(
        attend_back_kernel,
        (),
        [whole()] * 14,
        [whole()] * 7,
        [
            sds((2 * seq, width), bf16),
            sds((seq, width), bf16),
            sds((seq, width), bf16),
            sds((seq, LOW), bf16),
            sds((seq, 2 * LOW), bf16),
            sds((LOW, width), bf16),
            sds((2 * LOW, width), bf16),
        ],
        [pltpu.VMEM((seq, HD), f32), pltpu.VMEM((seq, HD), f32)],
        20 * seq * seq * width,
        16 * seq * width,
    )(q, k, v, do, lse, stats, cosf, sinf, bcat, kb, vb, low, misc, attn_routes)

    dx_part = call(
        rows_back_kernel,
        batches,
        [whole(), projections] + [whole()] * 8,
        whole(),
        sds((seq, D), bf16),
        [pltpu.VMEM((seq, D), f32)],
        project_flops,
        weight_bytes,
    )(dq, query_w, dk, dv, key_w, value_w, aq, amisc, lows_dense, attn_routes)

    column = jnp.arange(own, dtype=jnp.int32)
    own_at = (column // block) * (shards * block) + column % block
    dx_part, *pair_tables, grad_qb = lax.optimization_barrier((dx_part, *pair_tables, grad_qb))
    lows_parts = [lows] + [shifted(lows, step) for step in range(1, shards)]
    dx_part, *lows_parts = lax.optimization_barrier((dx_part, *lows_parts))
    lows_all = sum(part.astype(f32) for part in lows_parts).astype(bf16)
    dx = lax.psum_scatter(dx_part, "shard", scatter_dimension=0, tiled=True)

    own_rows = lambda array: lax.dynamic_slice_in_dim(array, shard_at * rows, rows, 0)

    input_grad = call(
        input_grad_kernel,
        (),
        [whole()] * 8,
        whole(),
        sds((rows, D), f32),
        [],
        2 * rows * LOW * D,
        24 * rows * D,
    )(dx, own_rows(lows_all), own_rows(ga), tokens, gain1, amisc, dh1, own_rows(attn_routes))

    select_own = (iota((D, own), 0) == (own_at + shard_at * block)[None, :]).astype(bf16)
    xn_own = nn(xn, select_own).astype(bf16)
    da_cols = nn(da, select_own).astype(bf16)
    lane = jnp.arange(LOW, dtype=jnp.int32)
    dense = jnp.zeros((seq, LOW), f32)
    for j in range(2):
        spread = (iota((LOW, LOW), 0) == (lane % RANK + j * RANK)[None, :]).astype(bf16)
        chosen = attn_routes[:, j : j + 1] == (lane // RANK)[None, :]
        dense = dense + jnp.where(chosen, nn(lows_all, spread), 0.0)
    grad_qa_own = tn(dense.astype(bf16), xn_own)
    grad_ob_own = tn(out_lows, da_cols)
    grad_kva_own = tn(lows_all[:, 2 * RANK : 4 * RANK], xn_own)

    def to_owner_columns(part):
        return part.reshape(-1, groups, block).transpose(1, 0, 2).reshape(groups, -1)

    def to_owner_ranks(part):
        parts = part.reshape(-1, groups, RANK // groups, width)
        return parts.transpose(1, 0, 2, 3).reshape(groups, -1)

    sending = [
        to_owner_columns(grad_qa_own.astype(bf16)),
        to_owner_columns(grad_ob_own.astype(bf16)),
        to_owner_columns(grad_kva_own.astype(bf16)),
        to_owner_ranks(grad_qb),
        to_owner_ranks(grad_oa),
        to_owner_ranks(jnp.concatenate([grad_kv[:RANK], grad_kv[LOW + RANK : LOW + 2 * RANK]])),
        to_owner_columns(factors),
    ]
    sizes = [piece.shape[1] for piece in sending]
    sent = jnp.concatenate(sending, axis=1).reshape(groups, -1, LOW)
    got = lax.all_to_all(sent, "dp", split_axis=0, concat_axis=0, tiled=True)
    got = got.reshape(groups, -1).astype(f32)
    pick_source = (adapter_ids[:, None] == jnp.arange(ADAPTERS, dtype=jnp.int32)[None, :]).astype(
        f32
    )
    placed_sums = jnp.einsum("sa,sn->an", pick_source, got, precision=precise)
    parts = []
    start = 0
    for size in sizes:
        parts.append(placed_sums[:, start : start + size])
        start += size
    ranks_own = RANK // groups

    def columns_out(part, count):
        return part.reshape(ADAPTERS, count, RANK, block)

    def ranks_out(part, count):
        return part.reshape(ADAPTERS, count, ranks_own, width)

    query_a_sum = columns_out(parts[0], ATT_EXPERTS).transpose(1, 0, 3, 2)
    output_b_sum = columns_out(parts[1], ATT_EXPERTS).transpose(1, 0, 2, 3)
    kv_a_sum = columns_out(parts[2], 2).transpose(1, 0, 3, 2)
    query_b_sum = ranks_out(parts[3], ATT_EXPERTS).transpose(1, 0, 2, 3)
    output_a_sum = ranks_out(parts[4], ATT_EXPERTS).transpose(1, 0, 3, 2)
    kv_b_sum = ranks_out(parts[5], 2).transpose(1, 0, 2, 3)
    factor_sum = columns_out(parts[6], 3 * EXPERTS).transpose(1, 0, 2, 3)
    gate_a_sum = factor_sum[:EXPERTS].transpose(0, 1, 3, 2)
    up_a_sum = factor_sum[EXPERTS : 2 * EXPERTS].transpose(0, 1, 3, 2)
    down_b_sum = factor_sum[2 * EXPERTS :]

    def widen(*parts):
        table = jnp.concatenate(parts, axis=1) if len(parts) > 1 else parts[0]
        return table.astype(f32).reshape(ADAPTERS, RANK, each)

    return (
        layer_out,
        input_grad,
        query_a_sum,
        query_b_sum,
        kv_a_sum[0],
        kv_b_sum[0],
        kv_a_sum[1],
        kv_b_sum[1],
        output_a_sum,
        output_b_sum,
        gate_a_sum,
        widen(*[t[:LOW] for t in pair_tables]),
        up_a_sum,
        widen(*[t[LOW:] for t in pair_tables]),
        ranks_first(widen(down_sum)),
        down_b_sum,
    )


def solution(mesh):
    placed = (
        P(("dp", "shard"), None),
        P(("dp", "shard"), None),
        P(),
        P(),
        P(),
        P(),
        P(None, None, "shard"),
        P(None, "shard"),
        P(None, "shard"),
        P(None, "shard", None),
        P(None, "dp"),
        P(None, "dp"),
        P("dp", None),
        P(),
        P(None, None, None, "shard"),
        P(),
        P(None, None, "shard"),
        P(),
        P(None, None, "shard"),
        P(None, None, "shard", None),
        P(),
        P(),
        P(None, None, "dp"),
        P(),
        P(None, None, "dp"),
        P(None, "dp", None),
        P(),
        P(),
        P("dp", None),
        P(("dp", "shard"), None),
    )
    return jax.shard_map(
        on_device,
        mesh=mesh,
        in_specs=placed,
        out_specs=(
            P(("dp", "shard"), None),
            P(("dp", "shard"), None),
            P(None, None, ("dp", "shard"), None),
            P(None, None, "dp", "shard"),
            P(None, ("dp", "shard"), None),
            P(None, "dp", "shard"),
            P(None, ("dp", "shard"), None),
            P(None, "dp", "shard"),
            P(None, None, "shard", "dp"),
            P(None, None, None, ("dp", "shard")),
            P(None, None, ("dp", "shard"), None),
            P(None, None, ("dp", "shard")),
            P(None, None, ("dp", "shard"), None),
            P(None, None, ("dp", "shard")),
            P(None, ("dp", "shard"), None),
            P(None, None, None, ("dp", "shard")),
        ),
        check_vma=False,
    )
```

time: 993 us -> 484 us (0.49)
  matrix products: 352 us -> 7.76 us
  local copies, waits for them, and re-layouts: 284 us -> 41.3 us
  Pallas kernels: 0 us -> 213 us
  other arithmetic: 158 us -> 13.5 us
  waiting for transfers between devices: 111 us -> 157 us
  blocking collectives: 22.7 us -> 0 us
    dot_general x112 -> x6, matrix products: 346 us -> 7.2 us  [the longest x3 3.78 us: tn(): lax.dot_general(a, b, (((0,), (0,)), ((), ())), preferred_element_type=f32)]
    pallas_call x0 -> x15, Pallas kernels: none -> 213 us  [the longest x2 55.5 us: on_device(): call(lambda *refs, first=first, last=last: expert_back_kernel(first, last...]
    gather x31 -> x0, local copies, waits for them, and re-layouts: 78.5 us -> none  [the longest x2 20.8 us: on_device(): query_rows = normed_all[attn_table]]
    scatter-add x3 -> x0, other arithmetic: 54.7 us -> none  [the longest x1 25.3 us: on_device(): grad_normed = jnp.zeros((seq_len, D), jnp.float32).at[attn_table].add(jnp...]
    all_gather x2, waiting for transfers between devices: 13 us -> 61.8 us  [the longest x1 33.2 us: on_device(): xn = lax.all_gather(normed, 'shard', axis=0, tiled=True)]
    unnamed x262 -> x81, local copies, waits for them, and re-layouts: 52.3 us -> 4.96 us
    convert_element_type x9 -> x3, local copies, waits for them, and re-layouts: 44.6 us -> 0.35 us  [the longest x1 0.12 us: on_device(): grad_ob_own.astype(bf16)]
    reshape x18 -> x23, local copies, waits for them, and re-layouts: 42.9 us -> 6.34 us  [the longest x3 1.86 us: ranks_out(): return part.reshape(ADAPTERS, count, ranks_own, width)]
  transfers between devices with their start and end apart: 18 -> 21, of which waited for: 8 -> 11; matrix products, arithmetic and copies ran while one was open for 57% -> 12% of each run, Pallas kernels for 0% -> 25%
where the time goes in v2:
time: 484 us; the launch traced here: 480 us
  Pallas kernels  213 us (44%)
  waiting for transfers between devices  157 us (32%)
  local copies, waits for them, and re-layouts  41.3 us (9%)
  starting transfers between devices  31 us (6%)
  between operations  17.3 us (4%)
  other arithmetic  13.5 us (3%)
  matrix products  7.76 us (2%)
    pallas_call x2, Pallas kernels, on_device(): call(lambda *refs, first=first, last=last: expert_back_kernel(first, last...  55.5 us
    reduce_scatter x1, waiting for transfers between devices, on_device(): attn = lax.psum_scatter(attn_part, 'shard', scatter_dimension=0, tiled=True)  39.5 us
    pallas_call x1, Pallas kernels, on_device(): call(expert_kernel, (steps,), [whole()] * 5 + [columns, columns, weight_r...  39.4 us
    all_gather x1, waiting for transfers between devices, on_device(): xn = lax.all_gather(normed, 'shard', axis=0, tiled=True)  33.2 us
    all_gather x1, waiting for transfers between devices, on_device(): da = lax.all_gather(da_own, 'shard', axis=0, tiled=True)  28.5 us
    pallas_call x1, Pallas kernels, on_device(): call(qkv_kernel, experts, [whole(), projection] + [whole()] * 10, [whole(...  21.9 us
    pallas_call x1, Pallas kernels, on_device(): call(rows_back_kernel, batches, [whole(), projections] + [whole()] * 8, w...  19.4 us
    pallas_call x1, Pallas kernels, on_device(): call(out_back_kernel, experts, [whole(), out_projection] + [whole()] * 5,...  18.2 us
  transfers between devices with their start and end apart: 21, of which 11 were waited for; matrix products, arithmetic and copies ran while one was open for 12% of the time, Pallas kernels for 25%

profile of v2, /device:TPU:0, one launch (start us, length us, event | category | flops | bytes accessed | tf_op | source)
XLA Modules:
  0.0 480.4 jit_solution(9925628332592606748)
XLA Ops:
  7.3 1.3 fusion.10
  9.3 2.0 fusion.12
  17.1 1.6 constant_dynamic-slice_fusion.7
  22.2 1.9 constant_dynamic-slice_fusion.9
  24.2 1.9 constant_dynamic-slice_fusion.6
  27.0 33.2 %all-gather.3.cloned.1.call-done.xn = bf16[512,2048]{1,0:T(8,128)(2,1)} async-done(((bf16[128,2048]{1,0:T(8,128)(2,1)}), bf16[512,2048]{1,0:T(8,128)(2,1)}) %all-gather.3.cloned.1.call-update) | async-done | bytes 2097168 | tf_op jit(solution)/shard_map/all_gather | solution.py:596
  60.2 21.9 %shard_map.405 = (bf16[1024,512]{1,0:T(8,128)(2,1)}, bf16[512,512]{1,0:T(8,128)(2,1)}, bf16[512,512]{1,0:T(8,128)(2,1)}, f32[512,128]{1,0:T(8,128)}, bf16[512,128]{1,0:T(8,128)(2,1)}, /*index=5*/bf16[512,128]{1,0:T(8,128)(2,1)}) custom-call(bf16[512,2048]{1,0:T(8,128)(2,1)} %all-gather.3.cloned.1.call-done.xn, bf16[8,2048,512]{2,1,0:T(8,128)(2,1)} %wq.3, ...), custom_call_target="tpu_custom_call" | custom-call | flops 34359738368 | bytes 67108864 | tf_op jit(solution)/shard_map/pallas_call | solution.py:651
  82.1 6.8 %shard_map.406 = (bf16[1024,512]{1,0:T(8,128)(2,1)}, bf16[1024,512]{1,0:T(8,128)(2,1)}, f32[1024,128]{1,0:T(8,128)}) custom-call(bf16[1024,512]{1,0:T(8,128)(2,1)} %get-tuple-element.81.q, bf16[512,512]{1,0:T(8,128)(2,1)} %get-tuple-element.82.k, bf16[512,512]{1,0:T(8,128)(2,1)} %get-tuple-element.83.v, f32[512,128]{1,0:T(8,128)} %get-tuple-element.84.ga), custom_call_target="tpu_custom_call" | custom-call | flops 4294967296 | bytes 16777216 | tf_op jit(solution)/shard_map/pallas_call | solution.py:669
  88.9 15.3 %shard_map.407 = (bf16[512,2048]{1,0:T(8,128)(2,1)}, bf16[512,128]{1,0:T(8,128)(2,1)}) custom-call(bf16[1024,512]{1,0:T(8,128)(2,1)} %get-tuple-element.85.og, bf16[8,512,2048]{2,1,0:T(8,128)(2,1)} %wo.3, bf16[128,512]{1,0:T(8,128)(2,1)} %bitcast.206, bf16[128,2048]{1,0:T(8,128)(2,1)} %bitcast.192, s32[512,2]{1,0:T(8,128)} %copy.143.routes), custom_call_target="tpu_custom_call" | custom-call | flops 34359738368 | bytes 67108864 | tf_op jit(solution)/shard_map/pallas_call | solution.py:684
  107.5 39.5 %reduce-scatter.6.cloned.1.call-done.refs_0_.refs_1_.attn = bf16[128,2048]{1,0:T(8,128)(2,1)} async-done(((bf16[512,2048]{1,0:T(8,128)(2,1)}), bf16[128,2048]{1,0:T(8,128)(2,1)}) %reduce-scatter.6.cloned.1.call-update) | async-done | bytes 524304 | tf_op jit(solution)/shard_map/reduce_scatter | solution.py:695
  146.9 4.2 shard_map.408
  151.2 3.8 all-to-all-start
  156.2 1.9 constant_dynamic-slice_fusion.3
  158.1 2.3 constant_dynamic-slice_fusion.4
  161.6 1.2 pad_maximum_fusion
  162.8 1.7 collective-permute-start.2
  164.8 1.7 collective-permute-start.1
  166.5 6.6 %all-to-all-done = bf16[8,40,2048]{2,1,0:T(8,128)(2,1)S(1)} async-done(((bf16[8,40,2048]{2,1,0:T(8,128)(2,1)}), bf16[8,40,2048]{2,1,0:T(8,128)(2,1)S(1)}, u32[]{:S(2)}, u32[]{:S(2)}) %all-to-all-start) | async-done | bytes 1310752 | tf_op jit(solution)/shard_map/all_to_all | solution.py:716
  173.2 4.3 all-to-all-start.2
  177.5 39.4 %shard_map.409 = (bf16[320,2176]{1,0:T(8,128)(2,1)}, bf16[320,5632]{1,0:T(8,128)(2,1)}, bf16[320,5632]{1,0:T(8,128)(2,1)}, bf16[320,5632]{1,0:T(8,128)(2,1)}, bf...) custom-call(bf16[320,2048]{1,0:T(8,128)(2,1)} %bitcast.162, ...), custom_call_target="tpu_custom_call" | custom-call | flops 88583700480 | bytes 276824064 | tf_op jit(solution)/shard_map/pallas_call | solution.py:780
  217.0 6.1 %shard_map.411 = (bf16[320,128]{1,0:T(8,128)(2,1)}, bf16[4,128,1408]{2,1,0:T(8,128)(2,1)}) custom-call(bf16[320,2048]{1,0:T(8,128)(2,1)} %bitcast.31.dy.refs_0_, bf16[320,128]{1,0:T(8,128)(2,1)} %compare_convert_fusion.mask.refs_1_, bf16[128,2048]{1,0:T(8,128)(2,1)} %bitcast.195, bf16[320,5632]{1,0:T(8,128)(2,1)} %get-tuple-element.95.h), custom_call_target="tpu_custom_call" | custom-call | flops 1845493760 | bytes 14417920 | tf_op jit(solution)/shard_map/pallas_call | solution.py:804
  223.1 4.1 all-to-all-start.1
  227.8 28.3 %shard_map.412 = (f32[320,2048]{1,0:T(8,128)}, f32[320,128]{1,0:T(8,128)}, f32[320,128]{1,0:T(8,128)}, bf16[16,128]{1,0:T(8,128)(2,1)}, bf16[4,256,768]{2,1,0:T(8,128)(2,1)}) custom-call(bf16[320,2048]{1,0:T(8,128)(2,1)} %bitcast.31.dy.refs_0_, bf16[320,128]{1,0:T(8,128)(2,1)} %compare_convert_fusion.mask.refs_1_, bf16[128,2048]{1,0:T(8,128)(2,1)} %bitcast.180, ...), custom_call_target="tpu_custom_call" | custom-call | flops 48318382080 | bytes 150994944 | tf_op jit(solution)/shard_map/pallas_call | solution.py:832
  256.3 27.2 %shard_map.413 = (f32[320,2048]{1,0:T(8,128)}, f32[320,128]{1,0:T(8,128)}, f32[320,128]{1,0:T(8,128)}, bf16[320,2176]{1,0:T(8,128)(2,1)}, bf16[4,256,640]{2,1,0:T(8,128)(2,1)}) custom-call(bf16[320,2048]{1,0:T(8,128)(2,1)} %bitcast.31.dy.refs_0_, bf16[320,128]{1,0:T(8,128)(2,1)} %compare_convert_fusion.mask.refs_1_, bf16[128,2048]{1,0:T(8,128)(2,1)} %bitcast.181, ...), custom_call_target="tpu_custom_call" | custom-call | flops 40265318400 | bytes 125829120 | tf_op jit(solution)/shard_map/pallas_call | solution.py:832
  283.5 4.2 all-to-all-start.3
  288.4 3.5 shard_map.410
  292.7 14.0 %all-to-all-done.3 = bf16[8,40,2176]{2,1,0:T(8,128)(2,1)S(1)} async-done(((bf16[8,40,2176]{2,1,0:T(8,128)(2,1)}), bf16[8,40,2176]{2,1,0:T(8,128)(2,1)S(1)}, u32[]{:S(2)}, u32[]{:S(2)}) %all-to-all-start.3) | async-done | bytes 1392672 | tf_op jit(solution)/shard_map/all_to_all | solution.py:720
  307.9 4.0 shard_map.414
  312.6 1.5 constant_dynamic-slice_fusion.routes
  314.0 1.5 constant_dynamic-slice_fusion.1.ga
  315.5 3.1 fusion.4
  320.5 1.6 collective-permute-start.8
  322.3 2.1 collective-permute-start.6
  325.3 1.2 collective-permute-done.8
  326.5 2.5 collective-permute-done.7
  329.6 28.5 %all-gather.5.cloned.1.call-done.da = bf16[512,2048]{1,0:T(8,128)(2,1)} async-done(((bf16[128,2048]{1,0:T(8,128)(2,1)}), bf16[512,2048]{1,0:T(8,128)(2,1)}) %all-gather.5.cloned.1.call-update) | async-done | bytes 2097168 | tf_op jit(solution)/shard_map/all_gather | solution.py:879
  358.2 18.2 %shard_map.415 = (bf16[1024,512]{1,0:T(8,128)(2,1)}, f32[1024,128]{1,0:T(8,128)}, bf16[128,512]{1,0:T(8,128)(2,1)}) custom-call(bf16[512,2048]{1,0:T(8,128)(2,1)} %all-gather.5.cloned.1.call-done.da, bf16[8,512,2048]{2,1,0:T(8,128)(2,1)} %wo.3, bf16[128,512]{1,0:T(8,128)(2,1)} %bitcast.207, bf16[128,2048]{1,0:T(8,128)(2,1)} %bitcast.193, ...), custom_call_target="tpu_custom_call" | custom-call | flops 34359738368 | bytes 67108864 | tf_op jit(solution)/shard_map/pallas_call | solution.py:896
  376.4 11.4 %shard_map.416 = (bf16[1024,512]{1,0:T(8,128)(2,1)}, bf16[512,512]{1,0:T(8,128)(2,1)}, bf16[512,512]{1,0:T(8,128)(2,1)}, bf16[512,128]{1,0:T(8,128)(2,1)}, bf16[...) custom-call(bf16[1024,512]{1,0:T(8,128)(2,1)} %get-tuple-element.81.q, ...), custom_call_target="tpu_custom_call" | custom-call | flops 10737418240 | bytes 16777216 | tf_op jit(solution)/shard_map/pallas_call | solution.py:911
  389.0 1.4 collective-permute-start.3
  391.4 3.1 fusion.8
  394.5 19.4 %shard_map.417 = bf16[512,2048]{1,0:T(8,128)(2,1)} custom-call(bf16[1024,512]{1,0:T(8,128)(2,1)} %get-tuple-element.120.dq, bf16[8,2048,512]{2,1,0:T(8,128)(2,1)} %wq.3, bf16[512,512]{1,0:T(8,128)(2,1)} %get-tuple-element.121.dk, bf16[512,512]{1,0:T(8,128)(2,1)} %get-tuple-element.122.dv, bf16[2048,512]{1,0:T(8,128)(2,1)} %wk.3, bf16[2048,512]{1,0:T(8,128)(2,1)} %wv.3, ...), custom_call_target="tpu_custom_call" | custom-call | flops 34359738368 | bytes 67108864 | tf_op jit(solution)/shard_map/pallas_call | solution.py:930
  414.1 3.1 shard_map.419
  417.2 1.2 copy.171
  420.2 2.8 reduce-scatter.12.cloned.1.call-done
  426.4 4.0 all-to-all-start.4
  432.9 12.2 %all-to-all-done.4 = bf16[8,480,128]{2,1,0:T(8,128)(2,1)S(1)} async-done(((bf16[8,480,128]{2,1,0:T(8,128)(2,1)}), bf16[8,480,128]{2,1,0:T(8,128)(2,1)S(1)}, u32[]{:S(2)}, u32[]{:S(2)}) %all-to-all-start.4) | async-done | bytes 983072 | tf_op jit(solution)/shard_map/all_to_all | solution.py:993
  454.2 15.5 %reduce-scatter.14.cloned.1.call-done.dx = bf16[128,2048]{1,0:T(8,128)(2,1)} async-done(((bf16[512,2048]{1,0:T(8,128)(2,1)}), bf16[128,2048]{1,0:T(8,128)(2,1)}) %reduce-scatter.14.cloned.1.call-update) | async-done | bytes 524304 | tf_op jit(solution)/shard_map/reduce_scatter | solution.py:947
  469.7 3.5 shard_map.418
  (218 shorter events, 41.4 us)
Async XLA Ops:
  7.2 9.2 %copy-start = (bf16[8,8,16,512]{3,2,1,0:T(8,128)(2,1)S(1)}, bf16[8,8,16,512]{3,2,1,0:T(8,128)(2,1)}, u32[]{:S(2)}) copy-start(bf16[8,8,16,512]{3,2,1,0:T(8,128)(2,1)} %param.44) | copy-start | bytes 3145732
  7.2 4.2 copy-start.32
  7.2 8.3 %copy-start.24 = (s32[512,2]{0,1:T(2,128)S(1)}, s32[512,2]{0,1:T(2,128)}, u32[]{:S(2)}) copy-start(s32[512,2]{0,1:T(2,128)} %param.58) | copy-start | bytes 12292
  7.2 53.0 %all-gather.3.cloned.1.call-start = ((), (), s32[]{:S(2)}) async-start(), calls=%async_computation.10 | async-start | bytes 2621440 | tf_op jit(solution)/shard_map/all_gather | solution.py:596
  11.3 135.6 %reduce-scatter.6.cloned.1.call-start = ((), (), s32[]{:S(2)}) async-start(), calls=%async_computation.11 | async-start | bytes 2621440 | tf_op jit(solution)/shard_map/reduce_scatter | solution.py:695
  19.6 6.5 %copy-start.21 = (bf16[2048,8]{0,1:T(8,128)(2,1)S(1)}, bf16[2048,8]{0,1:T(8,128)(2,1)}, u32[]{:S(2)}) copy-start(bf16[2048,8]{0,1:T(8,128)(2,1)} %param.34) | copy-start | bytes 98308
  106.0 41.0 %copy-start.8 = (s32[128,2]{1,0:T(8,128)}, s32[128,2]{1,0:T(8,128)S(1)}, u32[]{:S(2)}) copy-start(s32[128,2]{1,0:T(8,128)S(1)} %add.163.refs_6_.refs_5_.mcol) | copy-start | bytes 3076
  151.2 3.8 copy-start.4
  151.2 22.0 %all-to-all-start = ((bf16[8,40,2048]{2,1,0:T(8,128)(2,1)}), bf16[8,40,2048]{2,1,0:T(8,128)(2,1)S(1)}, u32[]{:S(2)}, u32[]{:S(2)}) async-start(bf16[8,40,2048]{2,1,0:T(8,128)(2,1)} %bitcast.163), calls=%async_computation.1 | async-start | bytes 2621440 | tf_op jit(solution)/shard_map/all_to_all | solution.py:716
  154.9 5.5 %copy-start.29 = (s32[128]{0:T(128)}, s32[128]{0:T(128)S(1)}, u32[]{:S(2)}) copy-start(s32[128]{0:T(128)S(1)} %and_select_fusion.1) | copy-start | bytes 1540
  155.4 5.0 %copy-start.18 = (bf16[512,128]{1,0:T(8,128)(2,1)S(1)}, bf16[512,128]{1,0:T(8,128)(2,1)}, u32[]{:S(2)}) copy-start(bf16[512,128]{1,0:T(8,128)(2,1)} %get-tuple-element.94) | copy-start | bytes 393220
  155.5 5.1 %copy-start.9 = (bf16[128,2048]{1,0:T(8,128)(2,1)S(1)}, bf16[128,2048]{1,0:T(8,128)(2,1)}, u32[]{:S(2)}) copy-start(bf16[128,2048]{1,0:T(8,128)(2,1)} %get-tuple-element.93) | copy-start | bytes 1572868
  162.8 54.1 %collective-permute-start.2 = (bf16[128,1536]{1,0:T(8,128)(2,1)}, bf16[128,1536]{1,0:T(8,128)(2,1)S(1)}, u32[]{:S(2)}, u32[]{:S(2)}) collective-permute-start(bf16[128,1536]{1,0:T(8,128)(2,1)} %get-tuple-element.167), channel_id=1, source_target_pairs={{0,3},{1,0},{2,1},{3,2},{4,7},{5,4},{6,5},{7,6},{8,11},{9,8},{10,9... | collective-permute-start | bytes 1179656 | tf_op jit(solution)/shard_map/ppermute | solution.py:730
  164.4 52.5 %collective-permute-start = (bf16[128,1536]{1,0:T(8,128)(2,1)}, bf16[128,1536]{1,0:T(8,128)(2,1)S(1)}, u32[]{:S(2)}, u32[]{:S(2)}) collective-permute-start(bf16[128,1536]{1,0:T(8,128)(2,1)} %get-tuple-element.168), channel_id=1, source_target_pairs={{0,1},{1,2},{2,3},{3,0},{4,5},{5,6},{6,7},{7,4},{8,9},{9,10},{10,1... | collective-permute-start | bytes 1179656 | tf_op jit(solution)/shard_map/ppermute | solution.py:730
  164.8 52.1 %collective-permute-start.1 = (bf16[128,1536]{1,0:T(8,128)(2,1)}, bf16[128,1536]{1,0:T(8,128)(2,1)S(1)}, u32[]{:S(2)}, u32[]{:S(2)}) collective-permute-start(bf16[128,1536]{1,0:T(8,128)(2,1)} %get-tuple-element.169), channel_id=1, source_target_pairs={{0,2},{1,3},{2,0},{3,1},{4,6},{5,7},{6,4},{7,5},{8,10},{9,11},{10,... | collective-permute-start | bytes 1179656 | tf_op jit(solution)/shard_map/ppermute | solution.py:730
  173.2 4.3 copy-start.7
  173.2 43.8 %all-to-all-start.2 = ((bf16[8,40,2048]{2,1,0:T(8,128)(2,1)}), bf16[8,40,2048]{2,1,0:T(8,128)(2,1)}, u32[]{:S(2)}, u32[]{:S(2)}) async-start(bf16[8,40,2048]{2,1,0:T(8,128)(2,1)} %bitcast.30), calls=%async_computation.3 | async-start | bytes 2621440 | tf_op jit(solution)/shard_map/all_to_all | solution.py:716
  177.4 78.8 %reduce-scatter.8.cloned.1.call-start = ((), (), s32[]{:S(2)}) async-start(), calls=%async_computation.12 | async-start | bytes 1802240 | tf_op jit(solution)/shard_map/reduce_scatter | solution.py:818
  216.9 6.2 %copy-start.11 = (bf16[128,1536]{1,0:T(8,128)(2,1)}, bf16[128,1536]{1,0:T(8,128)(2,1)S(1)}, u32[]{:S(2)}) copy-start(bf16[128,1536]{1,0:T(8,128)(2,1)S(1)} %collective-permute-done) | copy-start | bytes 1179652
  216.9 6.2 %copy-start.13 = (bf16[128,1536]{1,0:T(8,128)(2,1)}, bf16[128,1536]{1,0:T(8,128)(2,1)S(1)}, u32[]{:S(2)}) copy-start(bf16[128,1536]{1,0:T(8,128)(2,1)S(1)} %collective-permute-done.1) | copy-start | bytes 1179652
  223.1 33.1 %all-to-all-start.1 = ((bf16[8,40,2176]{2,1,0:T(8,128)(2,1)}), bf16[8,40,2176]{2,1,0:T(8,128)(2,1)S(1)}, u32[]{:S(2)}, u32[]{:S(2)}) async-start(bf16[8,40,2176]{2,1,0:T(8,128)(2,1)} %bitcast.28), calls=%async_computation.2 | async-start | bytes 2785280 | tf_op jit(solution)/shard_map/all_to_all | solution.py:720
  227.2 65.5 %reduce-scatter.10.cloned.1.call-start = ((), (), s32[]{:S(2)}) async-start(), calls=%async_computation.13 | async-start | bytes 1966080 | tf_op jit(solution)/shard_map/reduce_scatter | solution.py:818
  256.2 27.3 %copy-start.6 = (bf16[8,40,2176]{2,1,0:T(8,128)(2,1)}, bf16[8,40,2176]{2,1,0:T(8,128)(2,1)S(1)}, u32[]{:S(2)}) copy-start(bf16[8,40,2176]{2,1,0:T(8,128)(2,1)S(1)} %all-to-all-done.1) | copy-start | bytes 4177924
  283.5 4.2 copy-start.27
  283.5 23.3 %all-to-all-start.3 = ((bf16[8,40,2176]{2,1,0:T(8,128)(2,1)}), bf16[8,40,2176]{2,1,0:T(8,128)(2,1)S(1)}, u32[]{:S(2)}, u32[]{:S(2)}) async-start(bf16[8,40,2176]{2,1,0:T(8,128)(2,1)} %bitcast.160), calls=%async_computation.5 | async-start | bytes 2785280 | tf_op jit(solution)/shard_map/all_to_all | solution.py:720
  287.7 70.5 %all-gather.5.cloned.1.call-start = ((), (), s32[]{:S(2)}) async-start(), calls=%async_computation.14 | async-start | bytes 2621440 | tf_op jit(solution)/shard_map/all_gather | solution.py:879
  307.9 4.1 copy-start.28
  307.9 6.1 %copy-start.25 = (s32[512,2]{0,1:T(2,128)S(1)}, s32[512,2]{0,1:T(2,128)}, u32[]{:S(2)}) copy-start(s32[512,2]{0,1:T(2,128)} %param.58) | copy-start | bytes 12292
  311.9 111.1 %reduce-scatter.12.cloned.1.call-start = ((), (), s32[]{:S(2)}) async-start(), calls=%async_computation.15 | async-start | bytes 1638400 | tf_op jit(solution)/shard_map/reduce_scatter | solution.py:818
  315.5 3.1 copy-start.5
  315.5 3.2 copy-start.12
  315.5 3.2 copy-start.14
  318.9 5.5 %copy-start.15 = (bf16[128,1408]{1,0:T(8,128)(2,1)S(1)}, bf16[128,1408]{1,0:T(8,128)(2,1)}, u32[]{:S(2)}) copy-start(bf16[128,1408]{1,0:T(8,128)(2,1)} %reduce-scatter.8.cloned.1.call-done) | copy-start | bytes 1081348
  320.5 6.0 %collective-permute-start.8 = (bf16[128,128]{1,0:T(8,128)(2,1)S(1)}, bf16[128,128]{1,0:T(8,128)(2,1)S(1)}, u32[]{:S(2)}, u32[]{:S(2)}) collective-permute-start(bf16[128,128]{1,0:T(8,128)(2,1)S(1)} %copy-done.23), channel_id=1, source_target_pairs={{0,3},{1,0},{2,1},{3,2},{4,7},{5,4},{6,5},{7,6},{8,11},{9,8},{10,9... | collective-permute-start | bytes 98312 | tf_op jit(solution)/shard_map/ppermute | solution.py:730
  322.1 6.9 %collective-permute-start.7 = (bf16[128,128]{1,0:T(8,128)(2,1)S(1)}, bf16[128,128]{1,0:T(8,128)(2,1)S(1)}, u32[]{:S(2)}, u32[]{:S(2)}) collective-permute-start(bf16[128,128]{1,0:T(8,128)(2,1)S(1)} %copy-done.23), channel_id=1, source_target_pairs={{0,2},{1,3},{2,0},{3,1},{4,6},{5,7},{6,4},{7,5},{8,10},{9,11},{10,... | collective-permute-start | bytes 98312 | tf_op jit(solution)/shard_map/ppermute | solution.py:730
  322.3 6.7 %collective-permute-start.6 = (bf16[128,128]{1,0:T(8,128)(2,1)S(1)}, bf16[128,128]{1,0:T(8,128)(2,1)S(1)}, u32[]{:S(2)}, u32[]{:S(2)}) collective-permute-start(bf16[128,128]{1,0:T(8,128)(2,1)S(1)} %copy-done.23), channel_id=1, source_target_pairs={{0,1},{1,2},{2,3},{3,0},{4,5},{5,6},{6,7},{7,4},{8,9},{9,10},{10,1... | collective-permute-start | bytes 98312 | tf_op jit(solution)/shard_map/ppermute | solution.py:730
  387.8 35.4 %collective-permute-start.5 = (bf16[512,128]{1,0:T(8,128)(2,1)}, bf16[512,128]{1,0:T(8,128)(2,1)S(1)}, u32[]{:S(2)}, u32[]{:S(2)}) collective-permute-start(bf16[512,128]{1,0:T(8,128)(2,1)} %get-tuple-element.130), channel_id=1, source_target_pairs={{0,3},{1,0},{2,1},{3,2},{4,7},{5,4},{6,5},{7,6},{8,11},{9,8},{10,9... | collective-permute-start | bytes 393224 | tf_op jit(solution)/shard_map/ppermute | solution.py:730
  389.0 34.2 %collective-permute-start.4 = (bf16[512,128]{1,0:T(8,128)(2,1)}, bf16[512,128]{1,0:T(8,128)(2,1)S(1)}, u32[]{:S(2)}, u32[]{:S(2)}) collective-permute-start(bf16[512,128]{1,0:T(8,128)(2,1)} %get-tuple-element.130), channel_id=1, source_target_pairs={{0,2},{1,3},{2,0},{3,1},{4,6},{5,7},{6,4},{7,5},{8,10},{9,11},{10,... | collective-permute-start | bytes 393224 | tf_op jit(solution)/shard_map/ppermute | solution.py:730
  389.0 34.2 %collective-permute-start.3 = (bf16[512,128]{1,0:T(8,128)(2,1)}, bf16[512,128]{1,0:T(8,128)(2,1)S(1)}, u32[]{:S(2)}, u32[]{:S(2)}) collective-permute-start(bf16[512,128]{1,0:T(8,128)(2,1)} %get-tuple-element.130), channel_id=1, source_target_pairs={{0,1},{1,2},{2,3},{3,0},{4,5},{5,6},{6,7},{7,4},{8,9},{9,10},{10,1... | collective-permute-start | bytes 393224 | tf_op jit(solution)/shard_map/ppermute | solution.py:730
  390.4 79.3 %reduce-scatter.14.cloned.1.call-start = ((), (), s32[]{:S(2)}) async-start(), calls=%async_computation.16 | async-start | bytes 2621440 | tf_op jit(solution)/shard_map/reduce_scatter | solution.py:947
  413.9 4.5 copy-start.20
  418.4 4.6 copy-start.19
  419.5 3.8 copy-start.17
  425.3 5.1 %copy-start.16 = (bf16[256,640]{1,0:T(8,128)(2,1)S(1)}, bf16[256,640]{1,0:T(8,128)(2,1)}, u32[]{:S(2)}) copy-start(bf16[256,640]{1,0:T(8,128)(2,1)} %reduce-scatter.12.cloned.1.call-done) | copy-start | bytes 983044
  425.3 5.8 %copy-start.10 = (bf16[256,768]{1,0:T(8,128)(2,1)S(1)}, bf16[256,768]{1,0:T(8,128)(2,1)}, u32[]{:S(2)}) copy-start(bf16[256,768]{1,0:T(8,128)(2,1)} %reduce-scatter.10.cloned.1.call-done) | copy-start | bytes 1179652
  426.4 18.7 %all-to-all-start.4 = ((bf16[8,480,128]{2,1,0:T(8,128)(2,1)}), bf16[8,480,128]{2,1,0:T(8,128)(2,1)S(1)}, u32[]{:S(2)}, u32[]{:S(2)}) async-start(bf16[8,480,128]{2,1,0:T(8,128)(2,1)} %copy.173), calls=%async_computation.9 | async-start | bytes 1966080 | tf_op jit(solution)/shard_map/all_to_all | solution.py:993
  430.4 14.7 %copy-start.33 = (s32[8]{0:T(128)S(1)}, s32[8]{0:T(128)}, u32[]{:S(2)}) copy-start(s32[8]{0:T(128)} %param.57) | copy-start | bytes 100
  453.0 20.2 %copy-start.1 = (bf16[8,8,16,512]{3,2,1,0:T(8,128)(2,1)S(1)}, bf16[8,8,16,512]{3,2,1,0:T(8,128)(2,1)}, u32[]{:S(2)}) copy-start(bf16[8,8,16,512]{3,2,1,0:T(8,128)(2,1)} %param.44) | copy-start | bytes 3145732
  (8 other events, 11.9 us)
Sparse Core Ops, SparseCore 0:
  11.4 48.7 all-gather.2
  104.4 42.4 reduce-scatter.5
  223.2 32.9 reduce-scatter.7
  258.5 34.1 reduce-scatter.9
  312.0 46.0 all-gather.4
  390.5 32.4 reduce-scatter.11
  425.4 44.3 reduce-scatter.13

commit v3 on v2

v3 whole, which is shorter than its diff:
```python
import math

import jax
import jax.numpy as jnp
from jax import lax
from jax.experimental import pallas as pl
from jax.experimental.pallas import tpu as pltpu
from jax.sharding import PartitionSpec as P

D = 2048
HD = 128
EXPERTS = 8
ATT_EXPERTS = 8
ADAPTERS = 8
RANK = 16
LOW = 128
CHUNK = 128
GATE_LANE = 64
ROUTE_LANE = 96
ROUTER_ROW = 32


f32 = jnp.float32
bf16 = jnp.bfloat16
precise = lax.Precision.HIGHEST
eps = 1e-05
score_scale = HD ** (-0.5)


def nn(a, b):
    return lax.dot_general(a, b, (((1,), (0,)), ((), ())), preferred_element_type=f32)


def nt(a, b):
    return lax.dot_general(a, b, (((1,), (1,)), ((), ())), preferred_element_type=f32)


def tn(a, b):
    return lax.dot_general(a, b, (((0,), (0,)), ((), ())), preferred_element_type=f32)


def iota(shape, axis):
    return lax.broadcasted_iota(jnp.int32, shape, axis)


def ones_where(condition):
    return jnp.where(condition, 1.0, 0.0).astype(bf16)


def inverse_rms(values):
    return lax.rsqrt(jnp.mean(values * values, axis=-1, keepdims=True) + eps)


def norm_backward(values, inverse, gain_vector, grad_normed):
    weighted = gain_vector * grad_normed
    return inverse * weighted - values * (inverse * inverse * inverse) * jnp.mean(
        values * weighted, axis=-1, keepdims=True
    )


def softmax_pair(first, second):
    peak = jnp.maximum(first, second)
    one, two = jnp.exp(first - peak), jnp.exp(second - peak)
    total = one + two
    return one / total, two / total


def in_lane(column, lane, width=LOW):
    shape = (column.shape[0], width)
    return jnp.where(iota(shape, 1) == lane, column, 0.0)


def lane_of(values, lane):
    return jnp.sum(jnp.where(iota(values.shape, 1) == lane, values, 0.0), axis=1, keepdims=True)


def expert_lanes(dest, capacity, shape, group):
    lane = iota(shape, 1)
    low = (lane // group) * capacity
    return (dest >= low) & (dest < low + capacity)


def whole():
    return pl.BlockSpec(memory_space=pltpu.VMEM)


def sds(shape, dtype):
    return jax.ShapeDtypeStruct(shape, dtype)


def call(kernel, grid, in_specs, out_specs, out_shape, scratch, flops, moved):
    return pl.pallas_call(
        kernel,
        grid=grid,
        in_specs=in_specs,
        out_specs=out_specs,
        out_shape=out_shape,
        scratch_shapes=scratch,
        compiler_params=pltpu.CompilerParams(
            vmem_limit_bytes=60 * 1024 * 1024,
            dimension_semantics=("arbitrary",) * len(grid) if grid else None,
        ),
        cost_estimate=pl.CostEstimate(
            flops=4 * flops, bytes_accessed=4 * moved, transcendentals=0
        ),
    )


def rope(values, cosine, sine):
    return values * cosine + pltpu.roll(values, HD // 2, 1) * sine


def unrope(values, cosine, sine):
    return values * cosine - pltpu.roll(values, HD // 2, 1) * sine


def routed(route, shape):
    return (iota(shape, 1) // RANK) == route


def select_add(total, part, routes, expert):
    s = part.shape[0]
    for k in range(2):
        total[k * s : (k + 1) * s, :] += jnp.where(routes[:, k : k + 1] == expert, part, 0.0)


def copies(sources, targets, sems):
    return [
        pltpu.make_async_copy(source, target, sems.at[j])
        for j, (source, target) in enumerate(zip(sources, targets, strict=True))
    ]


def join_rows(places, left, parts, out):
    split, rows = left.shape[1], parts[0].shape[0]
    out[:, 0:split] = left[...]
    for j, part in enumerate(parts):
        at = pl.ds(pl.multiple_of(places[j] * rows, 16), rows)
        out[at, split:] = part[:, 0 : out.shape[1] - split]


def attention_kernel(shards, places, left, *refs):
    parts, refs = refs[:shards], refs[shards:]
    *refs, xn = refs

    @pl.when(pl.program_id(0) == 0)
    def _():
        join_rows(places, left, parts, xn)

    attention_steps(xn, *refs)


def attention_steps(
    xn, wq, wo, ob, wk_far, wv_far, aq, amisc, bcat, kb, vb, routes, cosf, sinf, oa,
    attn_out, out_low, q_far, k_far, v_far, ga_far, low_far, misc_far, o_far, lse_far,
    q, k, v, ga, low, misc, o, lse, qsum, og, chosen, wk, wv, load_sems, save_sems,
):
    step = pl.program_id(0)
    s, width = k.shape
    loads = copies((wk_far, wv_far), (wk, wv), load_sems)
    saves = copies(
        (q, k, v, ga, low, misc, o, lse),
        (q_far, k_far, v_far, ga_far, low_far, misc_far, o_far, lse_far),
        save_sems,
    )

    @pl.when(step == 0)
    def _():
        for load in loads:
            load.start()
        x = xn[...]
        low[...] = nt(x, aq[...]).astype(bf16)
        scores = nt(x, amisc[...])
        misc[...] = scores.astype(bf16)
        lane = iota((s, LOW), 1) - ROUTER_ROW
        gates = [
            jnp.sum(jnp.where(lane == routes[:, j : j + 1], scores, 0.0), axis=1, keepdims=True)
            for j in range(2)
        ]
        one, two = softmax_pair(*gates)
        ga[...] = in_lane(one, 0) + in_lane(two, 1)
        for j in range(2):
            mine = routed(routes[:, j : j + 1], (s, LOW))
            part = jnp.where(mine, low[...], jnp.zeros((), bf16))
            qsum[j * s : (j + 1) * s, :] = nn(part, bcat[...])

    @pl.when(step < ATT_EXPERTS)
    def _():
        select_add(qsum, nn(xn[...], wq[0]), routes, step)

    @pl.when(step == ATT_EXPERTS - 1)
    def _():
        for load in loads:
            load.wait()
        x = xn[...]
        keys = nn(x, wk[...]) + nn(misc[...], kb[...])
        for h in range(width // HD):
            hs = slice(h * HD, (h + 1) * HD)
            k[:, hs] = rope(keys[:, hs], cosf[...], sinf[...]).astype(bf16)
            for j in range(2):
                at = slice(j * s, (j + 1) * s)
                q[at, hs] = rope(qsum[at, hs], cosf[...], sinf[...]).astype(bf16)
        v[...] = (nn(x, wv[...]) + nn(misc[...], vb[...])).astype(bf16)
        attend(q, k, v, ga, o, og, lse)
        for save in saves:
            save.start()
        total = jnp.zeros((s, LOW), f32)
        for j in range(2):
            part = nt(og[j * s : (j + 1) * s, :], oa[...])
            total = total + jnp.where(routed(routes[:, j : j + 1], (s, LOW)), part, 0.0)
        out_low[...] = total.astype(bf16)
        spread_rows(og, routes, chosen)

    @pl.when(step >= ATT_EXPERTS)
    def _():
        weights = wo[...].reshape(chosen.shape[1], wo.shape[2])
        attn_out[...] = (nn(chosen[...], weights) + nn(out_low[...], ob[...])).astype(bf16)

    @pl.when(step == pl.num_programs(0) - 1)
    def _():
        for save in saves:
            save.wait()


def spread_rows(pair, routes, chosen):
    s, width = chosen.shape[0], pair.shape[1]
    for e in range(ATT_EXPERTS):
        chosen[:, e * width : (e + 1) * width] = of_expert_rows(pair, routes, e, s)


def causal(i, shape):
    row = (iota(shape, 0) & (CHUNK - 1)) + i * CHUNK
    return iota(shape, 1) <= row


def attend(q, k, v, ga, o_out, og_out, lse_out):
    s, width = k.shape
    for i in range(s // CHUNK):
        end = (i + 1) * CHUNK
        first, second = slice(i * CHUNK, end), slice(s + i * CHUNK, s + end)
        gates = [lane_of(ga[first, :], 0), lane_of(ga[first, :], 1)]
        log_totals = jnp.zeros((2 * CHUNK, LOW), f32)
        for h in range(width // HD):
            hs = slice(h * HD, (h + 1) * HD)
            queries = jnp.concatenate([q[first, hs], q[second, hs]], axis=0)
            scores = nt(queries, k[0:end, hs]) * score_scale
            scores = jnp.where(causal(i, scores.shape), scores, -1e30)
            peak = jnp.max(scores, axis=1, keepdims=True)
            weights = jnp.exp(scores - peak)
            total = jnp.sum(weights, axis=1, keepdims=True)
            mixed = nn(weights.astype(bf16), v[0:end, hs]) / total
            o_out[first, hs] = mixed[:CHUNK].astype(bf16)
            o_out[second, hs] = mixed[CHUNK:].astype(bf16)
            og_out[first, hs] = (mixed[:CHUNK] * gates[0]).astype(bf16)
            og_out[second, hs] = (mixed[CHUNK:] * gates[1]).astype(bf16)
            log_totals = log_totals + in_lane(peak + jnp.log(total), h)
        lse_out[first, :] = log_totals[:CHUNK]
        lse_out[second, :] = log_totals[CHUNK:]


def of_expert_rows(rows, routes, expert, s):
    return rows[0:s, :] * ones_where(routes[:, 0:1] == expert) + rows[s : 2 * s, :] * ones_where(
        routes[:, 1:2] == expert
    )


def second_norm(attn, tokens, gain):
    hidden = tokens[...].astype(f32) + attn[...].astype(f32)
    inverse = inverse_rms(hidden)
    return hidden, inverse, gain[...].astype(f32)


def dispatch_kernel(cap, attn, tokens, gain, router, mrow, mcol, rows_out, gm_out, m_out):
    hidden, inverse, scale = second_norm(attn, tokens, gain)
    m = (hidden * inverse * scale).astype(bf16)
    m_out[...] = m
    logits = nt(m, router[...])
    gates = softmax_pair(
        *[
            jnp.sum(
                jnp.where(
                    expert_lanes(mcol[:, k : k + 1], cap, logits.shape, 1),
                    logits,
                    0.0,
                ),
                axis=1,
                keepdims=True,
            )
            for k in range(2)
        ]
    )
    gm_out[...] = in_lane(gates[0], 0) + in_lane(gates[1], 1)
    slot = iota((rows_out.shape[0], mrow.shape[1]), 0)
    picks = [ones_where(mrow[k : k + 1, :] == slot) for k in range(2)]
    rows_out[:, 0:D] = nn(picks[0] + picks[1], m).astype(bf16)
    total = jnp.zeros((rows_out.shape[0], LOW), f32)
    for k in range(2):
        high = gates[k].astype(bf16).astype(f32)
        middle = (gates[k] - high).astype(bf16).astype(f32)
        both = in_lane(high, 0) + in_lane(middle, 1)
        total = total + nn(picks[k], both.astype(bf16))
    rows_out[:, D : D + LOW] = total.astype(bf16)


def fold(first_lane):
    row, column = iota((LOW, LOW), 0), iota((LOW, LOW), 1)
    return ones_where(column == (row & (RANK - 1)) + first_lane)


def spread(first_lane):
    row, column = iota((LOW, LOW), 0), iota((LOW, LOW), 1)
    return ones_where(row == (column & (RANK - 1)) + first_lane)


def combine_kernel(cap, ze, attn, tokens, cot, gm, mcol, layer_out, dlm_out, low_out):
    hidden = tokens[...].astype(f32) + attn[...].astype(f32)
    grad = cot[...].astype(f32)
    lane = iota((mcol.shape[0], ze.shape[0]), 1)
    gates, slopes, lows = [], [], []
    for k in range(2):
        gates.append(lane_of(gm[...], k))
        pick = ones_where(mcol[:, k : k + 1] == lane)
        expert_out = nn(pick, ze[:, 0:D])
        lows.append(gates[k] * nn(pick, ze[:, D : D + LOW]))
        slopes.append(jnp.sum(grad * expert_out, axis=1, keepdims=True))
        hidden = hidden + gates[k] * expert_out
    layer_out[...] = hidden.astype(bf16)
    low_out[...] = lows[0] + pltpu.roll(lows[1], 3 * RANK, 1)
    mean = gates[0] * slopes[0] + gates[1] * slopes[1]
    total = jnp.zeros(dlm_out.shape, f32)
    for k in range(2):
        mine = expert_lanes(mcol[:, k : k + 1], cap, dlm_out.shape, 1)
        total = total + jnp.where(mine, gates[k] * (slopes[k] - mean), 0.0)
    dlm_out[...] = total.astype(bf16)


def hidden_grad_kernel(
    rows, dlm, low, attn, tokens, cot, gain, router, mcol, routes, dh1_out, da_left, da_right
):
    hidden, inverse, scale = second_norm(attn, tokens, gain)
    lane = iota((mcol.shape[0], rows.shape[0]), 1)
    picks = [ones_where(mcol[:, k : k + 1] == lane) for k in range(2)]
    grad_m = nn(picks[0] + picks[1], rows[:, 0:D]) + nn(dlm[:, 0 : router.shape[0]], router[...])
    lows = [nn(pick, rows[:, D : D + LOW]) for pick in picks]
    total = low[...] + lows[0] + pltpu.roll(lows[1], 3 * RANK, 1)
    for k in range(2):
        total = total + in_lane(routes[:, k : k + 1].astype(f32), ROUTE_LANE + k)
    grad = cot[...].astype(f32) + norm_backward(hidden, inverse, scale, grad_m)
    dh1_out[...] = grad
    split = da_left.shape[1]
    da_left[...] = grad[:, :split].astype(bf16)
    da_right[:, 0 : D - split] = grad[:, split:].astype(bf16)
    da_right[:, D - split :] = total.astype(bf16)


def select_columns(places, shards, select):
    row, column = iota(select.shape, 0), iota(select.shape, 1)
    size = places[shards]
    group = lax.div(column, size)
    source = group * (size * shards) + places[0] * size + (column - group * size)
    select[...] = ones_where(row == source)


def own_columns_kernel(shards, places, *refs):
    parts, (out, gathered, select) = refs[: shards + 1], refs[shards + 1 :]
    select_columns(places, shards, select)
    join_rows(places, parts[0], parts[1:], gathered)
    out[...] = nn(gathered[...], select[...]).astype(bf16)


def owner_kernel(shards, places, *refs):
    da_refs, refs = refs[: shards + 1], refs[shards + 1 :]
    out_lows, columns, factors, grad_ob, da_own, gathered, select = refs
    own = da_own.shape[1]
    select_columns(places, shards, select)
    join_rows(places, da_refs[0], da_refs[1:], gathered)
    da_own[...] = nn(gathered[...], select[...]).astype(bf16)
    grad_ob[...] = tn(out_lows[...], da_own[...]).astype(bf16)
    right = D - da_refs[0].shape[1]
    lows = jnp.concatenate([ref[:, right : right + LOW] for ref in da_refs[1:]], axis=0)
    lane = (iota(lows.shape, 1) // RANK).astype(f32)
    mine = [lane_of(lows.astype(f32), ROUTE_LANE + k) == lane for k in range(2)]
    for part in range(3):
        dense = jnp.zeros(lows.shape, f32)
        for k in range(2):
            wide = nn(lows, spread((3 * k + part) * RANK))
            dense = dense + jnp.where(mine[k], wide, 0.0)
        at = slice(own, 2 * own) if part == 2 else slice(0, own)
        factors[part * LOW : (part + 1) * LOW, :] = tn(dense.astype(bf16), columns[:, at]).astype(
            bf16
        )


def identity():
    return ones_where(iota((LOW, LOW), 0) == iota((LOW, LOW), 1))


def expert_up_kernel(
    x, mask, ga, ua, gate_w, up_w, gate_b, up_b, g_out, u_out, lg_out, lu_out
):
    x = x.at[:, 0:D]

    @pl.when(pl.program_id(0) == 0)
    def _():
        lg_out[...] = nt(x[...], ga[...]).astype(bf16) * mask[...]
        lu_out[...] = nt(x[...], ua[...]).astype(bf16) * mask[...]

    g_out[...] = (nn(x[...], gate_w[...]) + nn(lg_out[...], gate_b[...])).astype(bf16)
    u_out[...] = (nn(x[...], up_w[...]) + nn(lu_out[...], up_b[...])).astype(bf16)


def expert_down_kernel(
    grads, x, mask, db, lg, lu, g, u, down_w, gate_b, up_b, down_a,
    ze_out, dg_out, du_out, dlg_out, dlu_out, *rest,
):
    *tables_out, dy, total, pd, dlg, dlu, dpd, lg_t, lu_t, dpd_t, tables = rest
    f = pl.program_id(0)
    width = down_w.shape[0]

    @pl.when(f == 0)
    def _():
        gate = x[:, D : D + LOW].astype(f32)
        gate = lane_of(gate, 0) + lane_of(gate, 1)
        dy[...] = (gate * grads[...].astype(f32)).astype(bf16)
        dpd[...] = nt(dy[...], db[...]).astype(bf16) * mask[...]
        lg_t[...] = nt(identity(), lg[...]).astype(bf16)
        lu_t[...] = nt(identity(), lu[...]).astype(bf16)
        dpd_t[...] = nt(identity(), dpd[...]).astype(bf16)
        for sums in (total, pd, dlg, dlu):
            sums[...] = jnp.zeros_like(sums)

    dh = nt(dy[...], down_w[...]) + nn(dpd[...], down_a[...])
    gate = g[...].astype(f32)
    up = u[...].astype(f32)
    sig = jax.nn.sigmoid(gate)
    act = gate * sig
    hidden = (act * up).astype(bf16)
    dgate = (dh * up * (sig + act * (1.0 - sig))).astype(bf16)
    dup = (dh * act).astype(bf16)
    dg_out[...] = dgate
    du_out[...] = dup
    total[...] += nn(hidden, down_w[...])
    pd[...] += nt(hidden, down_a[...])
    dlg[...] += nt(dgate, gate_b[...])
    dlu[...] += nt(dup, up_b[...])
    at = pl.ds(pl.multiple_of(f * width, LOW), width)
    tables[0:LOW, at] = nn(lg_t[...], dgate).astype(bf16)
    tables[LOW : 2 * LOW, at] = nn(lu_t[...], dup).astype(bf16)
    tables[2 * LOW : 3 * LOW, at] = nn(dpd_t[...], hidden).astype(bf16)

    @pl.when(f == pl.num_programs(0) - 1)
    def _():
        low = pd[...].astype(bf16) * mask[...]
        ze_out[:, 0:D] = (total[...] + nn(low, db[...])).astype(bf16)
        ze_out[:, D : D + LOW] = nn(low, fold(2 * RANK)).astype(bf16)
        dlg_out[...] = dlg[...].astype(bf16) * mask[...]
        dlu_out[...] = dlu[...].astype(bf16) * mask[...]
        first = 0
        for out in tables_out:
            parts, _, size = out.shape
            for z in range(parts):
                start = z * (tables.shape[1] // parts) + first
                out[z] = tables[:, start : start + size]
            first += size


def expert_rows_kernel(dg, du, dlg, dlu, gate_w, up_w, ga, ua, dm_out):
    n = pl.program_id(0)
    width = gate_w.shape[0]

    @pl.when(n == 0)
    def _():
        low = nn(dlg[...], fold(0)) + nn(dlu[...], fold(RANK))
        dm_out[:, D : D + LOW] = low.astype(bf16)

    total = nt(dg[...], gate_w[...]) + nt(du[...], up_w[...])
    total = total + nn(dlg[...], ga[...]) + nn(dlu[...], ua[...])
    dm_out[:, pl.ds(pl.multiple_of(n * width, LOW), width)] = total.astype(bf16)


def attention_back_kernel(shards, places, left, *refs):
    parts, refs = refs[:shards], refs[shards:]
    *refs, da = refs

    @pl.when(pl.program_id(0) == 0)
    def _():
        join_rows(places, left, parts, da)

    attention_back_steps(da, *refs)


def attention_back_steps(
    da, wo, wq, wk, wv, aq, amisc, bcat, kb, vb, oa, ob, routes,
    ga_far, o_far, q_far, k_far, v_far, lse_far, low_far, misc_far, cosf_far, sinf_far,
    dx_out, lows_out, grad_oa_out, grad_qb_out, grad_kv_out,
    ga, o, q, k, v, lse, low, misc, cosf, sinf, sems,
    dzl, dosum, do, stats, dq, dk, dv, lows_dense, dk_sum, dv_sum, chosen,
):
    step = pl.program_id(0)
    s, width = k.shape
    loads = copies(
        (ga_far, o_far, q_far, k_far, v_far, lse_far, low_far, misc_far, cosf_far, sinf_far),
        (ga, o, q, k, v, lse, low, misc, cosf, sinf),
        sems,
    )

    @pl.when(step == 0)
    def _():
        for load in loads:
            load.start()
        dzl[...] = nt(da[...], ob[...])
        for j in range(2):
            mine = routed(routes[:, j : j + 1], (s, LOW))
            part = jnp.where(mine, dzl[...], 0.0).astype(bf16)
            dosum[j * s : (j + 1) * s, :] = nn(part, oa[...])

    @pl.when(step < ATT_EXPERTS)
    def _():
        select_add(dosum, nt(da[...], wo[0]), routes, step)

    @pl.when(step == ATT_EXPERTS - 1)
    def _():
        for load in loads:
            load.wait()
        out_back(routes, ga, o, dzl, dosum, do, stats, grad_oa_out)
        attend_back(
            q, k, v, do, lse, stats, cosf, sinf, bcat, kb, vb, low, misc, routes,
            dq, dk, dv, lows_out, lows_dense, grad_qb_out, grad_kv_out, dk_sum, dv_sum,
        )
        spread_rows(dq, routes, chosen)

    @pl.when(step >= ATT_EXPERTS)
    def _():
        total = (
            nn(lows_dense[:, 0:LOW], aq[...])
            + nn(lows_dense[:, LOW : 2 * LOW], amisc[...])
            + nt(dk[...], wk[...])
            + nt(dv[...], wv[...])
        )
        for e in range(ATT_EXPERTS):
            total = total + nt(chosen[:, e * width : (e + 1) * width], wq[e])
        dx_out[...] = total.astype(bf16)


def out_back(routes, ga, o, dzl, dosum, do_out, stats_out, grad_oa_out):
    s, width = o.shape[0] // 2, o.shape[1]
    grad_oa = jnp.zeros((LOW, width), f32)
    for k in range(2):
        at = slice(k * s, (k + 1) * s)
        gate = lane_of(ga[...], k)
        mine = routed(routes[:, k : k + 1], (s, LOW))
        low = jnp.where(mine, gate * dzl[...], 0.0).astype(bf16)
        grad_oa = grad_oa + tn(low, o[at, :])
        stats = jnp.zeros((s, LOW), f32)
        slope = jnp.zeros((s, 1), f32)
        for h in range(width // HD):
            hs = slice(h * HD, (h + 1) * HD)
            before = dosum[at, hs]
            part = jnp.sum(o[at, hs].astype(f32) * before, axis=1, keepdims=True)
            slope = slope + part
            stats = stats + in_lane(gate * part, h)
            do_out[at, hs] = (gate * before).astype(bf16)
        stats_out[at, :] = stats + in_lane(slope, GATE_LANE)
    grad_oa_out[...] = grad_oa.astype(bf16)


def attend_back(
    q, k, v, do, lse, stats, cosf, sinf, bcat, kb, vb, low, misc, routes,
    dq_out, dk_out, dv_out, lows_out, misc_back_out, grad_qb_out, grad_kv_out, dk_sum, dv_sum,
):
    s, width = k.shape
    for h in range(width // HD):
        hs = slice(h * HD, (h + 1) * HD)
        dk_sum[...] = jnp.zeros_like(dk_sum)
        dv_sum[...] = jnp.zeros_like(dv_sum)
        for i in range(s // CHUNK):
            end = (i + 1) * CHUNK
            first, second = slice(i * CHUNK, end), slice(s + i * CHUNK, s + end)
            queries = jnp.concatenate([q[first, hs], q[second, hs]], axis=0)
            grads = jnp.concatenate([do[first, hs], do[second, hs]], axis=0)
            logs = jnp.concatenate(
                [lane_of(lse[first, :], h), lane_of(lse[second, :], h)], axis=0
            )
            centre = jnp.concatenate(
                [lane_of(stats[first, :], h), lane_of(stats[second, :], h)], axis=0
            )
            scores = nt(queries, k[0:end, hs]) * score_scale
            weights = jnp.where(causal(i, scores.shape), jnp.exp(scores - logs), 0.0)
            dscores = (weights * (nt(grads, v[0:end, hs]) - centre)).astype(bf16)
            dq = nn(dscores, k[0:end, hs]) * score_scale
            cosine, sine = cosf[first, :], sinf[first, :]
            dq_out[first, hs] = unrope(dq[:CHUNK], cosine, sine).astype(bf16)
            dq_out[second, hs] = unrope(dq[CHUNK:], cosine, sine).astype(bf16)
            dk_sum[0:end, :] += tn(dscores, queries)
            dv_sum[0:end, :] += tn(weights.astype(bf16), grads)
        dk_out[:, hs] = unrope(dk_sum[...] * score_scale, cosf[...], sinf[...]).astype(bf16)
        dv_out[:, hs] = dv_sum[...].astype(bf16)
    row, column = iota((LOW, LOW), 0), iota((LOW, LOW), 1)
    grad_qb = jnp.zeros((LOW, width), f32)
    chunks = s // CHUNK
    half = chunks // 2
    packed = [None] * half
    slopes = jnp.zeros((16, LOW), f32)
    line, at_lane = iota((16, LOW), 0), iota((16, LOW), 1) == GATE_LANE
    for i in range(chunks):
        rs = slice(i * CHUNK, (i + 1) * CHUNK)
        misc_back = (nt(dk_out[rs, :], kb[...]) + nt(dv_out[rs, :], vb[...])).astype(bf16)
        lows = nn(misc_back, ones_where((column == row + 2 * RANK) & (row < 2 * RANK)))
        dense = jnp.zeros((CHUNK, LOW), f32)
        for j in range(2):
            at = slice(j * s + i * CHUNK, j * s + (i + 1) * CHUNK)
            mine = routed(routes[rs, j : j + 1], (CHUNK, LOW))
            part = jnp.where(mine, nt(dq_out[at, :], bcat[...]), 0.0).astype(bf16)
            dense = dense + part.astype(f32)
            fold_pair = ones_where((column == (row & (RANK - 1)) + j * RANK) & (column < 2 * RANK))
            lows = lows + nn(part, fold_pair)
            mark = ones_where((line == j * chunks + i) & at_lane)
            slopes = slopes + nt(mark, stats[at, :].astype(bf16))
            grad_qb = grad_qb + tn(
                jnp.where(mine, low[rs, :], jnp.zeros((), bf16)), dq_out[at, :]
            )
        if i < half:
            packed[i] = lows
        else:
            together = packed[i - half] + pltpu.roll(lows, LOW // 2, 1)
            lows_out[(i - half) * CHUNK : (i - half + 1) * CHUNK, :] = together.astype(bf16)
        misc_back_out[rs, 0:LOW] = dense.astype(bf16)
        misc_back_out[rs, LOW : 2 * LOW] = misc_back
    lows_out[half * CHUNK : half * CHUNK + 16, :] = slopes.astype(bf16)
    grad_qb_out[...] = grad_qb.astype(bf16)
    grad_kv_out[0:LOW, :] = tn(misc[...], dk_out[...]).astype(bf16)
    grad_kv_out[LOW : 2 * LOW, :] = tn(misc[...], dv_out[...]).astype(bf16)


def input_grad_kernel(dx, slopes, ga, tokens, gain, router, dh1, routes, out):
    x = tokens[...].astype(f32)
    gates = [lane_of(ga[...], k) for k in range(2)]
    slope = [slopes[:, k : k + 1] for k in range(2)]
    mean = gates[0] * slope[0] + gates[1] * slope[1]
    total = jnp.zeros(ga.shape, f32)
    lane = iota(ga.shape, 1)
    for k in range(2):
        mine = lane == routes[:, k : k + 1]
        total = total + jnp.where(mine, gates[k] * (slope[k] - mean), 0.0)
    grad = dx[...].astype(f32) + nn(total[:, 0 : router.shape[0]].astype(bf16), router[...])
    out[...] = dh1[...] + norm_backward(x, inverse_rms(x), gain[...].astype(f32), grad)


def after(value, *earlier):
    return lax.optimization_barrier((value, *earlier))[0]


def slot_places(routes, expert_count, capacity):
    choose = (routes[:, :, None] == jnp.arange(expert_count, dtype=jnp.int32)).astype(bf16)
    member = choose[:, 0] + choose[:, 1]
    count = routes.shape[0]
    before = (iota((count, count), 1) < iota((count, count), 0)).astype(bf16)
    slots = nn(before, member)
    mine = jnp.sum(slots[:, None, :] * choose.astype(f32), axis=2)
    return routes * capacity + mine.astype(jnp.int32)


def rotary_tables(count):
    half = HD // 2
    freq = jnp.exp(jnp.arange(half, dtype=f32) * (-2.0 * math.log(10000.0) / HD))
    angles = jnp.arange(count, dtype=jnp.int32).astype(f32)[:, None] * freq
    cosine, sine = jnp.cos(angles), jnp.sin(angles)
    return (
        jnp.concatenate([cosine, cosine], axis=1),
        jnp.concatenate([-sine, sine], axis=1),
    )


def on_device(
    tokens, cotangent, gain_first, gain_second, router_attn, router_mlp, query_w, key_w, value_w,
    output_w, gate_w, up_w, down_w, query_a, query_b, key_a, key_b, value_a, value_b, output_a,
    output_b, gate_a, gate_b, up_a, up_b, down_a, down_b, adapter_ids, attn_routes, mlp_routes,
):
    shards = lax.axis_size("shard")
    groups = lax.axis_size("dp")
    shard_at = lax.axis_index("shard")
    group_at = lax.axis_index("dp")
    rows = tokens.shape[0]
    seq = rows * shards
    cap_mlp = rows // 4 + rows // 16
    slices = groups // EXPERTS
    ff = gate_w.shape[1]
    width = key_w.shape[1]
    block = D // (groups * shards)
    own = groups * block
    adapter = adapter_ids[group_at]
    expert = group_at // slices

    x = tokens.astype(f32)
    normed = (x * inverse_rms(x) * gain_first.astype(f32)).astype(bf16)
    split = (D // LOW * 9 // 16) * LOW
    places = lax.rem(shard_at + shards - jnp.arange(shards, dtype=jnp.int32), shards)

    def shifted(part, step):
        pairs = [(i, (i + step) % shards) for i in range(shards)]
        return lax.ppermute(part, "shard", pairs) if step else part

    def gathered(left, right):
        return [lax.all_gather(left, "shard", axis=0, tiled=True)] + [
            shifted(right, step) for step in range(shards)
        ]

    xn_parts = gathered(normed[:, :split], normed[:, split:])

    mcol = slot_places(mlp_routes, EXPERTS, cap_mlp)
    mrow = mcol.T
    cosf, sinf = rotary_tables(seq)

    def ranks_first(factor):
        return jnp.swapaxes(factor, -1, -2)

    def of_adapter(factor, axis):
        return lax.dynamic_index_in_dim(factor, adapter, axis, keepdims=False)

    def pad_rows(parts, count=LOW):
        have = sum(p.shape[0] for p in parts)
        fill = jnp.zeros((count - have, parts[0].shape[1]), bf16)
        return jnp.concatenate(list(parts) + [fill], axis=0)

    aq = of_adapter(ranks_first(query_a), 1).reshape(LOW, D)
    amisc = pad_rows(
        [of_adapter(ranks_first(key_a), 0), of_adapter(ranks_first(value_a), 0), router_attn.T]
    )
    bcat = of_adapter(query_b, 1).reshape(LOW, width)
    key_second, value_second = of_adapter(key_b, 0), of_adapter(value_b, 0)
    kb = pad_rows([key_second])
    vb = pad_rows([jnp.zeros_like(value_second), value_second])
    oa = of_adapter(ranks_first(output_a), 1).reshape(LOW, width)
    ob = of_adapter(output_b, 1).reshape(LOW, D)
    router = pad_rows([router_mlp.T], 2 * EXPERTS)
    router_first = pad_rows([router_attn.T], 2 * ATT_EXPERTS)
    gain1, gain2 = gain_first.reshape(1, D), gain_second.reshape(1, D)

    def of_expert(factor):
        return lax.dynamic_index_in_dim(factor, expert, 0, keepdims=False).reshape(LOW, D)

    gate_first = of_expert(ranks_first(gate_a))
    up_first = of_expert(ranks_first(up_a))
    down_second = of_expert(down_b)
    gate_table = gate_b.reshape(LOW, ff)
    up_table = up_b.reshape(LOW, ff)
    down_table = ranks_first(down_a).reshape(LOW, ff)
    expert_rows = groups * cap_mlp
    source_adapter = jnp.repeat(adapter_ids, cap_mlp)
    mask = (
        source_adapter[:, None] == (jnp.arange(LOW, dtype=jnp.int32) // RANK)[None, :]
    ).astype(bf16)

    experts = (ATT_EXPERTS,)
    batch = 2
    batches = (ATT_EXPERTS // batch,)
    def to_experts(sent):
        wide = sent.shape[1]
        sent = jnp.repeat(sent.reshape(EXPERTS, cap_mlp, wide), slices, axis=0)
        got = lax.all_to_all(sent, "dp", split_axis=0, concat_axis=0, tiled=True)
        return got.reshape(expert_rows, wide)

    sent_rows = EXPERTS * cap_mlp
    picked = (mrow[0][None, :] == iota((sent_rows, rows), 0)) | (
        mrow[1][None, :] == iota((sent_rows, rows), 0)
    )
    grads_in = to_experts(nn(picked.astype(bf16), cotangent).astype(bf16))
    own_rows = lambda array: lax.dynamic_slice_in_dim(array, shard_at * rows, rows, 0)
    routes_own = own_rows(attn_routes)
    early_made = (router, router_first, gain1, gain2, mask, mrow, mcol, routes_own)
    early_made += (gate_first, up_first, down_second)
    early_made, xn_parts, grads_in = lax.optimization_barrier((early_made, xn_parts, grads_in))
    router, router_first, gain1, gain2, mask, mrow, mcol, routes_own, *firsts = early_made
    gate_first, up_first, down_second = firsts

    column_parts = 8
    width_d = D // column_parts
    steps_attn = ATT_EXPERTS + column_parts
    early = lambda e: (jnp.minimum(e, ATT_EXPERTS - 1), 0, 0)
    late = lambda e: jnp.maximum(e - ATT_EXPERTS, 0)
    column_block = pl.BlockSpec((LOW, width_d), lambda e: (0, late(e)))
    out_block = pl.BlockSpec((seq, width_d), lambda e: (0, late(e)))
    key_block = pl.BlockSpec((width_d, width), lambda e: (late(e), 0))
    far = pl.BlockSpec(memory_space=pl.ANY)
    project_flops = 4 * ATT_EXPERTS * seq * D * width
    weight_bytes = 4 * ATT_EXPERTS * D * width
    pair, row = ((2 * seq, width), bf16), ((seq, width), bf16)
    narrow, stat = ((seq, LOW), bf16), ((2 * seq, LOW), f32)
    saved = [pair, row, row, ((seq, LOW), f32), narrow, narrow, pair, stat]

    attn_part, low_part, q, k, v, ga, low, misc, o, lse = call(
        lambda *refs: attention_kernel(shards, *refs),
        (steps_attn,),
        [pl.BlockSpec(memory_space=pltpu.SMEM)]
        + [whole()] * (1 + shards)
        + [
            pl.BlockSpec((1, D, width), early),
            pl.BlockSpec((ATT_EXPERTS, width, width_d), lambda e: (0, 0, late(e))),
            column_block,
            far,
            far,
        ]
        + [whole()] * 9,
        [out_block, whole()] + [far] * 8,
        [sds((seq, D), bf16), sds(*narrow)] + [sds(*shape) for shape in saved],
        [pltpu.VMEM(*shape) for shape in saved]
        + [
            pltpu.VMEM((2 * seq, width), f32),
            pltpu.VMEM(*pair),
            pltpu.VMEM((seq, ATT_EXPERTS * width), bf16),
            pltpu.VMEM((D, width), bf16),
            pltpu.VMEM((D, width), bf16),
            pltpu.SemaphoreType.DMA((2,)),
            pltpu.SemaphoreType.DMA((8,)),
            pltpu.VMEM((seq, D), bf16),
        ],
        project_flops,
        weight_bytes,
    )(places, *xn_parts, query_w, output_w, ob, key_w, value_w, aq, amisc, bcat, kb, vb, attn_routes, cosf, sinf, oa)

    attn = lax.psum_scatter(attn_part, "shard", scatter_dimension=0, tiled=True)

    rows_sent, gm, m = call(
        lambda *refs: dispatch_kernel(cap_mlp, *refs),
        (),
        [whole()] * 6,
        [whole()] * 3,
        [
            sds((sent_rows, D + LOW), bf16),
            sds((rows, LOW), f32),
            sds((rows, D), bf16),
        ],
        [],
        6 * sent_rows * rows * D,
        8 * sent_rows * D,
    )(attn, tokens, gain2, router, mrow, mcol)

    def from_experts(made):
        got = lax.all_to_all(
            made.reshape(groups, cap_mlp, D + LOW), "dp", split_axis=0, concat_axis=0, tiled=True
        )
        if slices > 1:
            parts = got.reshape(EXPERTS, slices, cap_mlp, D + LOW).astype(f32)
            got = jnp.sum(parts, axis=1).astype(bf16)
        return got.reshape(sent_rows, D + LOW)

    def by_column_owner(part):
        split = part.reshape(rows, groups, shards, block)
        return split.transpose(2, 0, 1, 3).reshape(shards, rows, own)

    columns_sent = jnp.concatenate([by_column_owner(m), by_column_owner(cotangent)], axis=2)
    low_lanes = low_part.reshape(shards, rows, LOW).transpose(1, 0, 2).reshape(rows, shards * LOW)
    arrived = []
    for step in range(shards):
        piece = lax.dynamic_index_in_dim(
            columns_sent, lax.rem(shard_at + step, shards), 0, keepdims=False
        )
        piece = jnp.concatenate([piece, low_lanes], axis=1)
        arrived.append(shifted(piece, step))

    rows_in = to_experts(rows_sent)

    steps = 11
    fb = ff // steps
    columns = pl.BlockSpec((D, fb), lambda f: (0, f))
    weight_rows = pl.BlockSpec((fb, D), lambda f: (f, 0))
    table = pl.BlockSpec((LOW, fb), lambda f: (0, f))
    kept = pl.BlockSpec((expert_rows, fb), lambda f: (0, f))
    weight_flops = 2 * expert_rows * D * ff
    weight_moved = 2 * D * ff
    low_shape = sds((expert_rows, LOW), bf16)
    wide_shape = sds((expert_rows, ff), bf16)
    out_shape = sds((expert_rows, D + LOW), bf16)

    g, u, lg, lu = call(
        expert_up_kernel,
        (steps,),
        [whole()] * 4 + [columns, columns, table, table],
        [kept, kept, whole(), whole()],
        [wide_shape, wide_shape, low_shape, low_shape],
        [],
        2 * weight_flops,
        2 * weight_moved,
    )(rows_in, mask, gate_first, up_first, gate_w, up_w, gate_table, up_table)

    g, *arrived = lax.optimization_barrier((g, *arrived))
    arrived = jnp.concatenate(arrived, axis=0)
    mlp_columns = arrived[:, : 2 * own]
    out_lows = jnp.sum(
        arrived[:, 2 * own :].reshape(shards, rows, shards, LOW).astype(f32), axis=0
    )
    out_lows = out_lows.astype(bf16).transpose(1, 0, 2).reshape(seq, LOW)

    each = ff // shards
    head = ((each // LOW + 1) // 2) * LOW
    spans = [head, each - head] if each % LOW == 0 else [each]
    low_sum = pltpu.VMEM((expert_rows, LOW), f32)
    low_turned = pltpu.VMEM((LOW, expert_rows), bf16)
    ze, dg, du, dlg, dlu, *tables = call(
        expert_down_kernel,
        (steps,),
        [whole()] * 6 + [kept, kept, weight_rows, table, table, table],
        [whole(), kept, kept, whole(), whole()] + [whole() for _ in spans],
        [out_shape, wide_shape, wide_shape, low_shape, low_shape]
        + [sds((shards, 3 * LOW, span), bf16) for span in spans],
        [pltpu.VMEM((expert_rows, D), bf16)]
        + [pltpu.VMEM((expert_rows, D), f32), low_sum, low_sum, low_sum]
        + [pltpu.VMEM((expert_rows, LOW), bf16)]
        + [low_turned] * 3
        + [pltpu.VMEM((3 * LOW, ff), bf16)],
        2 * weight_flops,
        weight_moved,
    )(grads_in, rows_in, mask, down_second, lg, lu, g, u, down_w, gate_table, up_table, down_table)

    ze_back = from_experts(ze)

    def table_sum(part):
        part = part.reshape(-1, part.shape[-1])
        return lax.psum_scatter(part, "shard", scatter_dimension=0, tiled=True)

    head_tables = table_sum(tables[0])

    parts = 8
    db = D // parts
    row_block = pl.BlockSpec((db, ff), lambda n: (n, 0))
    low_block = pl.BlockSpec((LOW, db), lambda n: (0, n))
    dm = call(
        expert_rows_kernel,
        (parts,),
        [whole()] * 4 + [row_block, row_block, low_block, low_block],
        whole(),
        out_shape,
        [],
        2 * weight_flops,
        2 * weight_moved,
    )(dg, du, dlg, dlu, gate_w, up_w, gate_first, up_first)

    dm_back = from_experts(dm)

    layer_out, dlm, low_down = call(
        lambda *refs: combine_kernel(cap_mlp, *refs),
        (),
        [whole()] * 6,
        [whole()] * 3,
        [sds((rows, D), bf16), sds((rows, LOW), bf16), sds((rows, LOW), f32)],
        [],
        4 * sent_rows * rows * D,
        4 * sent_rows * D,
    )(ze_back, attn, tokens, cotangent, gm, mcol)

    dm_back = after(dm_back, head_tables)
    dh1, da_left, da_right = call(
        hidden_grad_kernel,
        (),
        [whole()] * 10,
        [whole()] * 3,
        [
            sds((rows, D), f32),
            sds((rows, split), bf16),
            sds((rows, D - split + LOW), bf16),
        ],
        [],
        2 * sent_rows * rows * D,
        4 * sent_rows * D,
    )(dm_back, dlm, low_down, attn, tokens, cotangent, gain2, router, mcol, mlp_routes)

    da_parts = gathered(da_left, da_right)
    owner_places = jnp.concatenate([places, jnp.full((1,), block, jnp.int32)])
    xn_own = call(
        lambda *refs: own_columns_kernel(shards, *refs),
        (),
        [pl.BlockSpec(memory_space=pltpu.SMEM)] + [whole()] * (shards + 1),
        whole(),
        sds((seq, own), bf16),
        [pltpu.VMEM((seq, D), bf16), pltpu.VMEM((D, own), bf16)],
        0,
        0,
    )(owner_places, *after(xn_parts, da_left))
    *da_parts, xn_own = lax.optimization_barrier((*da_parts, xn_own))
    tables_sum = [head_tables] + [table_sum(after(part, *da_parts)) for part in tables[1:]]

    loaded = [((seq, LOW), f32), pair, pair, row, row, stat, narrow, narrow]
    loaded += [((seq, HD), f32), ((seq, HD), f32)]
    dx_part, lows, grad_oa, grad_qb, grad_kv = call(
        lambda *refs: attention_back_kernel(shards, *refs),
        (steps_attn,),
        [pl.BlockSpec(memory_space=pltpu.SMEM)]
        + [whole()] * (1 + shards)
        + [
            pl.BlockSpec((1, width, D), early),
            pl.BlockSpec((ATT_EXPERTS, width_d, width), lambda e: (0, late(e), 0)),
            key_block,
            key_block,
            column_block,
            column_block,
        ]
        + [whole()] * 6
        + [far] * 10,
        [out_block] + [whole()] * 4,
        [
            sds((seq, D), bf16),
            sds((seq // 2 + 16, LOW), bf16),
            sds((LOW, width), bf16),
            sds((LOW, width), bf16),
            sds((2 * LOW, width), bf16),
        ],
        [pltpu.VMEM(*shape) for shape in loaded]
        + [
            pltpu.SemaphoreType.DMA((10,)),
            pltpu.VMEM((seq, LOW), f32),
            pltpu.VMEM((2 * seq, width), f32),
            pltpu.VMEM(*pair),
            pltpu.VMEM(*stat),
            pltpu.VMEM(*pair),
            pltpu.VMEM(*row),
            pltpu.VMEM(*row),
            pltpu.VMEM((seq, 2 * LOW), bf16),
            pltpu.VMEM((seq, HD), f32),
            pltpu.VMEM((seq, HD), f32),
            pltpu.VMEM((seq, ATT_EXPERTS * width), bf16),
            pltpu.VMEM((seq, D), bf16),
        ],
        project_flops,
        weight_bytes,
    )(places, *da_parts, output_w, query_w, key_w, value_w, aq, amisc, bcat, kb, vb, oa, ob, attn_routes, ga, o, q, k, v, lse, low, misc, cosf, sinf)

    held = (dx_part, lows, grad_oa, grad_qb, grad_kv, *da_parts, *tables_sum)
    dx_part, lows, grad_oa, grad_qb, grad_kv, *held = lax.optimization_barrier(held)
    da_parts, tables_sum = held[: shards + 1], held[shards + 1 :]
    lows_parts = [lows] + [shifted(lows, step) for step in range(1, shards)]
    chain = (*lows_parts, *da_parts)
    chain = lax.optimization_barrier(chain)
    lows_parts, da_parts = chain[:shards], chain[shards:]
    factors, grad_ob_own = call(
        lambda *refs: owner_kernel(shards, *refs),
        (),
        [pl.BlockSpec(memory_space=pltpu.SMEM)] + [whole()] * (shards + 3),
        [whole()] * 2,
        [sds((3 * LOW, own), bf16), sds((LOW, own), bf16)],
        [
            pltpu.VMEM((seq, own), bf16),
            pltpu.VMEM((seq, D), bf16),
            pltpu.VMEM((D, own), bf16),
        ],
        0,
        0,
    )(owner_places, *da_parts, out_lows, mlp_columns)
    lows_sum = sum(part.astype(f32) for part in lows_parts)
    half = LOW // 2
    lows_all = jnp.concatenate([lows_sum[: seq // 2, :half], lows_sum[: seq // 2, half:]], axis=0)
    lows_all = lows_all.astype(bf16)
    slopes = lows_sum[seq // 2 : seq // 2 + 2 * (seq // CHUNK)].reshape(2, seq).T
    dx = lax.psum_scatter(dx_part, "shard", scatter_dimension=0, tiled=True)

    input_grad = call(
        input_grad_kernel,
        (),
        [whole()] * 8,
        whole(),
        sds((rows, D), f32),
        [],
        2 * rows * LOW * D,
        24 * rows * D,
    )(dx, own_rows(slopes), own_rows(ga), tokens, gain1, router_first, dh1, routes_own)

    lane = jnp.arange(LOW, dtype=jnp.int32)
    dense = jnp.zeros((seq, LOW), f32)
    for j in range(2):
        spread = (iota((half, LOW), 0) == (lane % RANK + j * RANK)[None, :]).astype(bf16)
        chosen = attn_routes[:, j : j + 1] == (lane // RANK)[None, :]
        dense = dense + jnp.where(chosen, nn(lows_all, spread), 0.0)
    grad_qa_own = tn(dense.astype(bf16), xn_own)
    grad_kva_own = tn(lows_all[:, 2 * RANK : 4 * RANK], xn_own)

    def to_owner_columns(part):
        return part.reshape(-1, groups, block).transpose(1, 0, 2).reshape(groups, -1)

    def to_owner_ranks(part):
        parts = part.reshape(-1, groups, RANK // groups, width)
        return parts.transpose(1, 0, 2, 3).reshape(groups, -1)

    sending = [
        to_owner_columns(grad_qa_own.astype(bf16)),
        to_owner_columns(grad_ob_own),
        to_owner_columns(grad_kva_own.astype(bf16)),
        to_owner_ranks(grad_qb),
        to_owner_ranks(grad_oa),
        to_owner_ranks(jnp.concatenate([grad_kv[:RANK], grad_kv[LOW + RANK : LOW + 2 * RANK]])),
        to_owner_columns(factors),
    ]
    sizes = [piece.shape[1] for piece in sending]
    sent = jnp.concatenate(sending, axis=1).reshape(groups, -1, LOW)
    got = lax.all_to_all(sent, "dp", split_axis=0, concat_axis=0, tiled=True)
    got = got.reshape(groups, -1).astype(f32)
    pick_source = (adapter_ids[:, None] == jnp.arange(ADAPTERS, dtype=jnp.int32)[None, :]).astype(
        f32
    )
    placed_sums = jnp.einsum("sa,sn->an", pick_source, got, precision=precise)
    parts = []
    start = 0
    for size in sizes:
        parts.append(placed_sums[:, start : start + size])
        start += size
    ranks_own = RANK // groups

    def columns_out(part, count):
        return part.reshape(ADAPTERS, count, RANK, block)

    def ranks_out(part, count):
        return part.reshape(ADAPTERS, count, ranks_own, width)

    query_a_sum = columns_out(parts[0], ATT_EXPERTS).transpose(1, 0, 3, 2)
    output_b_sum = columns_out(parts[1], ATT_EXPERTS).transpose(1, 0, 2, 3)
    kv_a_sum = columns_out(parts[2], 2).transpose(1, 0, 3, 2)
    query_b_sum = ranks_out(parts[3], ATT_EXPERTS).transpose(1, 0, 2, 3)
    output_a_sum = ranks_out(parts[4], ATT_EXPERTS).transpose(1, 0, 3, 2)
    kv_b_sum = ranks_out(parts[5], 2).transpose(1, 0, 2, 3)
    factor_sum = columns_out(parts[6], 3 * EXPERTS).transpose(1, 0, 2, 3)
    gate_a_sum = factor_sum[:EXPERTS].transpose(0, 1, 3, 2)
    up_a_sum = factor_sum[EXPERTS : 2 * EXPERTS].transpose(0, 1, 3, 2)
    down_b_sum = factor_sum[2 * EXPERTS :]

    joined = jnp.concatenate(tables_sum, axis=1) if len(tables_sum) > 1 else tables_sum[0]
    joined = joined.astype(f32).reshape(3, ADAPTERS, RANK, each)

    return (
        layer_out,
        input_grad,
        query_a_sum,
        query_b_sum,
        kv_a_sum[0],
        kv_b_sum[0],
        kv_a_sum[1],
        kv_b_sum[1],
        output_a_sum,
        output_b_sum,
        gate_a_sum,
        joined[0],
        up_a_sum,
        joined[1],
        ranks_first(joined[2]),
        down_b_sum,
    )


def solution(mesh):
    placed = (
        P(("dp", "shard"), None),
        P(("dp", "shard"), None),
        P(),
        P(),
        P(),
        P(),
        P(None, None, "shard"),
        P(None, "shard"),
        P(None, "shard"),
        P(None, "shard", None),
        P(None, "dp"),
        P(None, "dp"),
        P("dp", None),
        P(),
        P(None, None, None, "shard"),
        P(),
        P(None, None, "shard"),
        P(),
        P(None, None, "shard"),
        P(None, None, "shard", None),
        P(),
        P(),
        P(None, None, "dp"),
        P(),
        P(None, None, "dp"),
        P(None, "dp", None),
        P(),
        P(),
        P("dp", None),
        P(("dp", "shard"), None),
    )
    return jax.shard_map(
        on_device,
        mesh=mesh,
        in_specs=placed,
        out_specs=(
            P(("dp", "shard"), None),
            P(("dp", "shard"), None),
            P(None, None, ("dp", "shard"), None),
            P(None, None, "dp", "shard"),
            P(None, ("dp", "shard"), None),
            P(None, "dp", "shard"),
            P(None, ("dp", "shard"), None),
            P(None, "dp", "shard"),
            P(None, None, "shard", "dp"),
            P(None, None, None, ("dp", "shard")),
            P(None, None, ("dp", "shard"), None),
            P(None, None, ("dp", "shard")),
            P(None, None, ("dp", "shard"), None),
            P(None, None, ("dp", "shard")),
            P(None, ("dp", "shard"), None),
            P(None, None, None, ("dp", "shard")),
        ),
        check_vma=False,
    )
```

time: 484 us -> 437 us (0.903)
  waiting for transfers between devices: 157 us -> 126 us
  Pallas kernels: 213 us -> 192 us
  starting transfers between devices: 31 us -> 37.7 us
    all_gather x2, waiting for transfers between devices: 61.8 us -> 6.47 us  [gathered(): lax.all_gather(left, 'shard', axis=0, tiled=True)]
    ppermute x9 -> x12, waiting for transfers between devices: 3.68 us -> 36.1 us  [shifted(): return lax.ppermute(part, 'shard', pairs) if step else part]
    pallas_call x12 -> x8, Pallas kernels: 201 us -> 181 us  [the longest x1 43 us: on_device(): call(lambda *refs: attention_back_kernel(shards, *refs), (steps_attn,), [...]
    reduce_scatter x1, waiting for transfers between devices: 15.5 us -> 0.01 us  [on_device(): dx = lax.psum_scatter(dx_part, 'shard', scatter_dimension=0, tiled=True)]
    ppermute x9 -> x12, starting transfers between devices: 10.2 us -> 18.1 us  [shifted(): return lax.ppermute(part, 'shard', pairs) if step else part]
    reduce_scatter x1, waiting for transfers between devices: 39.5 us -> 44.7 us  [on_device(): attn = lax.psum_scatter(attn_part, 'shard', scatter_dimension=0, tiled=True)]
  transfers between devices with their start and end apart: 21 -> 23, of which waited for: 11 -> 11; matrix products, arithmetic and copies ran while one was open for 12% -> 12% of each run, Pallas kernels for 25% -> 26%
where the time goes in v3:
time: 437 us; the launch traced here: 432 us
  Pallas kernels  192 us (44%)
  waiting for transfers between devices  126 us (29%)
  local copies, waits for them, and re-layouts  45.5 us (10%)
  starting transfers between devices  37.7 us (9%)
  between operations  17.5 us (4%)
  other arithmetic  10.7 us (2%)
    reduce_scatter x1, waiting for transfers between devices, on_device(): attn = lax.psum_scatter(attn_part, 'shard', scatter_dimension=0, tiled=True)  44.7 us
    pallas_call x1, Pallas kernels, on_device(): call(lambda *refs: attention_back_kernel(shards, *refs), (steps_attn,), [...  43 us
    pallas_call x1, Pallas kernels, on_device(): call(lambda *refs: attention_kernel(shards, *refs), (steps_attn,), [pl.Bl...  37.9 us
    ppermute x12, waiting for transfers between devices, shifted(): return lax.ppermute(part, 'shard', pairs) if step else part  36.1 us
    pallas_call x1, Pallas kernels, on_device(): call(expert_down_kernel, (steps,), [whole()] * 6 + [kept, kept, weight_ro...  33.1 us
    pallas_call x1, Pallas kernels, on_device(): call(expert_up_kernel, (steps,), [whole()] * 4 + [columns, columns, table...  28 us
    pallas_call x1, Pallas kernels, on_device(): call(expert_rows_kernel, (parts,), [whole()] * 4 + [row_block, row_block,...  26.2 us
    ppermute x12, starting transfers between devices, shifted(): return lax.ppermute(part, 'shard', pairs) if step else part  18.1 us
  transfers between devices with their start and end apart: 23, of which 11 were waited for; matrix products, arithmetic and copies ran while one was open for 12% of the time, Pallas kernels for 26%

profile of v3, /device:TPU:0, one launch (start us, length us, event | category | flops | bytes accessed | tf_op | source)
XLA Modules:
  0.0 432.4 jit_solution(5074188097847452701)
XLA Ops:
  7.3 1.3 fusion.2
  9.3 1.2 fusion.4
  10.6 5.1 %collective-permute-start.2 = (bf16[128,896]{1,0:T(8,128)(2,1)S(1)}, bf16[128,896]{1,0:T(8,128)(2,1)S(1)}, u32[]{:S(2)}, u32[]{:S(2)}) collective-permute-start(bf16[128,896]{1,0:T(8,128)(2,1)S(1)} %slice.140.refs_2_), channel_id=1, source_target_pairs={{0,3},{1,0},{2,1},{3,2},{4,7},{5,4},{6,5},{7,6},{8,11},{9,8},{10,9... | collective-permute-start | bytes 688136 | tf_op jit(solution)/shard_map/ppermute | solution.py:701
  18.1 1.6 convolution_convert_fusion
  19.7 3.9 all-to-all-start
  27.0 1.6 constant_dynamic-slice_fusion.2
  28.8 2.0 constant_dynamic-slice_fusion.4
  35.1 1.9 constant_dynamic-slice_fusion.5
  37.0 1.9 constant_dynamic-slice_fusion.6
  39.7 2.3 constant_dynamic-slice_fusion.7
  48.3 6.3 %all-gather.3.cloned.1.call-done.refs_1_ = bf16[512,1152]{1,0:T(8,128)(2,1)} async-done(((bf16[128,1152]{1,0:T(8,128)(2,1)}), bf16[512,1152]{1,0:T(8,128)(2,1)}) %all-gather.3.cloned.1.call-update) | async-done | bytes 1179664 | tf_op jit(solution)/shard_map/all_gather | solution.py:704
  54.6 37.9 %shard_map.405 = (bf16[512,2048]{1,0:T(8,128)(2,1)}, bf16[512,128]{1,0:T(8,128)(2,1)}, bf16[1024,512]{1,0:T(8,128)(2,1)}, bf16[512,512]{1,0:T(8,128)(2,1)}, bf16...) custom-call(s32[4]{0:T(128)} %compare_select_fusion.refs_0_, ...), custom_call_target="tpu_custom_call" | custom-call | flops 68719476736 | bytes 134217728 | tf_op jit(solution)/shard_map/pallas_call | solution.py:791
  93.1 44.7 %reduce-scatter.5.cloned.1.call-done.refs_0_.refs_1_.attn = bf16[128,2048]{1,0:T(8,128)(2,1)} async-done(((bf16[512,2048]{1,0:T(8,128)(2,1)}), bf16[128,2048]{1,0:T(8,128)(2,1)}) %reduce-scatter.5.cloned.1.call-update) | async-done | bytes 524304 | tf_op jit(solution)/shard_map/reduce_scatter | solution.py:821
  137.8 3.3 shard_map.406
  141.1 3.7 all-to-all-start.1
  148.1 1.2 pad_maximum_fusion
  149.3 1.7 collective-permute-start.5
  151.5 1.8 collective-permute-start.4
  153.3 10.6 %all-to-all-done.1 = bf16[8,40,2176]{2,1,0:T(8,128)(2,1)S(1)} async-done(((bf16[8,40,2176]{2,1,0:T(8,128)(2,1)}), bf16[8,40,2176]{2,1,0:T(8,128)(2,1)S(1)}, u32[]{:S(2)}, u32[]{:S(2)}) %all-to-all-start.1) | async-done | bytes 1392672 | tf_op jit(solution)/shard_map/all_to_all | solution.py:760
  163.9 1.1 copy-done.8
  165.0 28.0 %shard_map.407 = (bf16[320,5632]{1,0:T(8,128)(2,1)}, bf16[320,5632]{1,0:T(8,128)(2,1)}, bf16[320,128]{1,0:T(8,128)(2,1)}, bf16[320,128]{1,0:T(8,128)(2,1)}) custom-call(bf16[320,2176]{1,0:T(8,128)(2,1)} %bitcast.154, bf16[320,128]{1,0:T(8,128)(2,1)} %compare_convert_fusion.mask, bf16[128,2048]{1,0:T(8,128)(2,1)} %bitcast.172, bf16[128,2048]{1,0:T(8,128)(2,1)} %bitcast.170, ...), custom_call_target="tpu_custom_call" | custom-call | flops 59055800320 | bytes 184549376 | tf_op jit(solution)/shard_map/pallas_call | solution.py:875
  193.0 33.1 %shard_map.408 = (bf16[320,2176]{1,0:T(8,128)(2,1)}, bf16[320,5632]{1,0:T(8,128)(2,1)}, bf16[320,5632]{1,0:T(8,128)(2,1)}, bf16[320,128]{1,0:T(8,128)(2,1)}, bf1...) custom-call(bf16[320,2048]{1,0:T(8,128)(2,1)} %bitcast.159, ...), custom_call_target="tpu_custom_call" | custom-call | flops 59055800320 | bytes 92274688 | tf_op jit(solution)/shard_map/pallas_call | solution.py:899
  226.1 3.6 all-to-all-start.2
  229.7 26.2 %shard_map.410 = bf16[320,2176]{1,0:T(8,128)(2,1)} custom-call(bf16[320,5632]{1,0:T(8,128)(2,1)} %get-tuple-element.135.dg, bf16[320,5632]{1,0:T(8,128)(2,1)} %get-tuple-element.136.du, bf16[320,128]{1,0:T(8,128)(2,1)} %get-tuple-element.137.dlg, bf16[320,128]{1,0:T(8,128)(2,1)} %get-tuple-element.138.dlu, bf16[2048,5632]{1,0:T(8,128)(2,1)} %gate_w.3, ...), custom_call_target="tpu_custom_call" | custom-call | flops 59055800320 | bytes 184549376 | tf_op jit(solution)/shard_map/pallas_call | solution.py:927
  255.9 4.1 all-to-all-start.3
  260.8 3.5 shard_map.409
  264.3 14.8 %all-to-all-done.3 = bf16[8,40,2176]{2,1,0:T(8,128)(2,1)S(1)} async-done(((bf16[8,40,2176]{2,1,0:T(8,128)(2,1)}), bf16[8,40,2176]{2,1,0:T(8,128)(2,1)S(1)}, u32[]{:S(2)}, u32[]{:S(2)}) %all-to-all-start.3) | async-done | bytes 1392672 | tf_op jit(solution)/shard_map/all_to_all | solution.py:839
  279.1 1.1 copy-done.3
  280.2 3.9 shard_map.411
  284.8 1.5 constant_dynamic-slice_fusion.ga
  286.4 2.1 collective-permute-start.8
  288.5 1.9 collective-permute-start.6
  290.6 1.2 slice.147.refs_7_
  292.8 3.9 shard_map.412
  296.8 3.5 collective-permute-done.8.refs_5_
  300.3 27.5 %collective-permute-done.7.refs_4_ = bf16[128,1024]{1,0:T(8,128)(2,1)S(1)} collective-permute-done((bf16[128,1024]{1,0:T(8,128)(2,1)S(1)}, bf16[128,1024]{1,0:T(8,128)(2,1)S(1)}, u32[]{:S(2)}, u32[]{:S(2)}) %collective-permute-start.7) | collective-permute-done | bytes 262176 | tf_op jit(solution)/shard_map/ppermute | solution.py:701
  328.6 43.0 %shard_map.413 = (bf16[512,2048]{1,0:T(8,128)(2,1)}, bf16[272,128]{1,0:T(8,128)(2,1)}, bf16[128,512]{1,0:T(8,128)(2,1)}, bf16[128,512]{1,0:T(8,128)(2,1)}, bf16[256,512]{1,0:T(8,128)(2,1)}) custom-call(s32[4]{0:T(128)} %compare_select_fusion.refs_0_, bf16[512,1152]{1,0:T(8,128)(2,1)} %all-gather.5.cloned.1.call-done.refs_1_, ...), custom_call_target="tpu_custom_call" | custom-call | flops 68719476736 | bytes 134217728 | tf_op jit(solution)/shard_map/pallas_call | solution.py:984
  372.4 1.8 collective-permute-start.11
  374.5 1.8 collective-permute-start.9
  377.7 4.2 collective-permute-done.10
  381.9 5.7 %shard_map.415 = (bf16[384,512]{1,0:T(8,128)(2,1)}, bf16[128,512]{1,0:T(8,128)(2,1)}) custom-call(s32[5]{0:T(128)} %pad_add_fusion.refs_0_, bf16[512,1152]{1,0:T(8,128)(2,1)} %all-gather.5.cloned.1.call-done.refs_1_, bf16[128,1024]{1,0:T(8,128)(2,1)} %get-tuple-element.187.refs_2_, bf16[128,1024]{1,0:T(8,128)(2,1)} %copy-done.25, ...), custom_call_target="tpu_custom_call" | custom-call | tf_op jit(solution)/shard_map/pallas_call | solution.py:1034
  392.4 1.1 copy.164
  393.5 4.2 all-to-all-start.4
  397.9 1.4 fusion.39
  400.0 12.4 %all-to-all-done.4 = bf16[8,480,128]{2,1,0:T(8,128)(2,1)S(1)} async-done(((bf16[8,480,128]{2,1,0:T(8,128)(2,1)}), bf16[8,480,128]{2,1,0:T(8,128)(2,1)S(1)}, u32[]{:S(2)}, u32[]{:S(2)}) %all-to-all-start.4) | async-done | bytes 983072 | tf_op jit(solution)/shard_map/all_to_all | solution.py:1093
  413.3 1.1 copy-done.2
  420.4 1.2 fusion.42
  421.6 3.6 shard_map.414
  (239 shorter events, 39.0 us)
Async XLA Ops:
  7.2 19.2 %copy-start = (bf16[8,8,16,512]{3,2,1,0:T(8,128)(2,1)S(1)}, bf16[8,8,16,512]{3,2,1,0:T(8,128)(2,1)}, u32[]{:S(2)}) copy-start(bf16[8,8,16,512]{3,2,1,0:T(8,128)(2,1)} %param.44) | copy-start | bytes 3145732
  7.2 10.3 %copy-start.34 = (s32[128,2]{0,1:T(2,128)S(1)}, s32[128,2]{0,1:T(2,128)}, u32[]{:S(2)}) copy-start(s32[128,2]{0,1:T(2,128)} %param.59) | copy-start | bytes 3076
  7.2 10.9 %copy-start.4 = (bf16[128,2048]{1,0:T(8,128)(2,1)S(1)}, bf16[128,2048]{1,0:T(8,128)(2,1)}, u32[]{:S(2)}) copy-start(bf16[128,2048]{1,0:T(8,128)(2,1)} %cot.1) | copy-start | bytes 1572868
  7.2 47.3 %all-gather.3.cloned.1.call-start = ((), (), s32[]{:S(2)}) async-start(), calls=%async_computation.9 | async-start | bytes 1474560 | tf_op jit(solution)/shard_map/all_gather | solution.py:704
  10.6 9.1 %copy-start.11 = (bf16[128,896]{1,0:T(8,128)(2,1)}, bf16[128,896]{1,0:T(8,128)(2,1)S(1)}, u32[]{:S(2)}) copy-start(bf16[128,896]{1,0:T(8,128)(2,1)S(1)} %slice.140.refs_2_) | copy-start | bytes 688132
  10.6 36.9 %collective-permute-start.2 = (bf16[128,896]{1,0:T(8,128)(2,1)S(1)}, bf16[128,896]{1,0:T(8,128)(2,1)S(1)}, u32[]{:S(2)}, u32[]{:S(2)}) collective-permute-start(bf16[128,896]{1,0:T(8,128)(2,1)S(1)} %slice.140.refs_2_), channel_id=1, source_target_pairs={{0,3},{1,0},{2,1},{3,2},{4,7},{5,4},{6,5},{7,6},{8,11},{9,8},{10,9... | collective-permute-start | bytes 688136 | tf_op jit(solution)/shard_map/ppermute | solution.py:701
  15.7 32.6 %collective-permute-start.1 = (bf16[128,896]{1,0:T(8,128)(2,1)S(1)}, bf16[128,896]{1,0:T(8,128)(2,1)}, u32[]{:S(2)}, u32[]{:S(2)}) collective-permute-start(bf16[128,896]{1,0:T(8,128)(2,1)S(1)} %slice.140.refs_2_), channel_id=1, source_target_pairs={{0,2},{1,3},{2,0},{3,1},{4,6},{5,7},{6,4},{7,5},{8,10},{9,11},{10,... | collective-permute-start | bytes 688136 | tf_op jit(solution)/shard_map/ppermute | solution.py:701
  15.7 32.6 %collective-permute-start = (bf16[128,896]{1,0:T(8,128)(2,1)S(1)}, bf16[128,896]{1,0:T(8,128)(2,1)}, u32[]{:S(2)}, u32[]{:S(2)}) collective-permute-start(bf16[128,896]{1,0:T(8,128)(2,1)S(1)} %slice.140.refs_2_), channel_id=1, source_target_pairs={{0,1},{1,2},{2,3},{3,0},{4,5},{5,6},{6,7},{7,4},{8,9},{9,10},{10,1... | collective-permute-start | bytes 688136 | tf_op jit(solution)/shard_map/ppermute | solution.py:701
  17.9 74.6 %copy-start.6 = (s32[128,2]{1,0:T(8,128)}, s32[128,2]{1,0:T(8,128)S(1)}, u32[]{:S(2)}) copy-start(s32[128,2]{1,0:T(8,128)S(1)} %add.130.refs_5_.mcol) | copy-start | bytes 3076
  19.7 8.9 %copy-start.32 = (s32[512,2]{0,1:T(2,128)S(1)}, s32[512,2]{0,1:T(2,128)}, u32[]{:S(2)}) copy-start(s32[512,2]{0,1:T(2,128)} %param.58) | copy-start | bytes 12292
  19.7 28.6 %all-to-all-start = ((bf16[8,40,2048]{2,1,0:T(8,128)(2,1)}), bf16[8,40,2048]{2,1,0:T(8,128)(2,1)S(1)}, u32[]{:S(2)}, u32[]{:S(2)}) async-start(bf16[8,40,2048]{2,1,0:T(8,128)(2,1)} %bitcast.9), calls=%async_computation | async-start | bytes 2621440 | tf_op jit(solution)/shard_map/all_to_all | solution.py:760
  23.5 114.3 %reduce-scatter.5.cloned.1.call-start = ((), (), s32[]{:S(2)}) async-start(), calls=%async_computation.10 | async-start | bytes 2621440 | tf_op jit(solution)/shard_map/reduce_scatter | solution.py:821
  28.8 8.2 %copy-start.16 = (s32[512,2]{1,0:T(8,128)}, s32[512,2]{1,0:T(8,128)S(1)}, u32[]{:S(2)}) copy-start(s32[512,2]{1,0:T(8,128)S(1)} %copy.138.refs_16_.refs_17_) | copy-start | bytes 12292
  35.1 6.8 %copy-start.27 = (bf16[2048,8]{0,1:T(8,128)(2,1)S(1)}, bf16[2048,8]{0,1:T(8,128)(2,1)}, u32[]{:S(2)}) copy-start(bf16[2048,8]{0,1:T(8,128)(2,1)} %param.34) | copy-start | bytes 98308
  37.0 6.4 %copy-start.36 = (bf16[2048]{0:T(1024)(128)(2,1)S(1)}, bf16[2048]{0:T(1024)(128)(2,1)}, u32[]{:S(2)}) copy-start(bf16[2048]{0:T(1024)(128)(2,1)} %param.32) | copy-start | bytes 12292
  37.0 7.8 %copy-start.37 = (bf16[2048]{0:T(1024)(128)(2,1)S(1)}, bf16[2048]{0:T(1024)(128)(2,1)}, u32[]{:S(2)}) copy-start(bf16[2048]{0:T(1024)(128)(2,1)} %param.33) | copy-start | bytes 12292
  37.0 8.4 %copy-start.31 = (bf16[2048,8]{0,1:T(8,128)(2,1)S(1)}, bf16[2048,8]{0,1:T(8,128)(2,1)}, u32[]{:S(2)}) copy-start(bf16[2048,8]{0,1:T(8,128)(2,1)} %param.35) | copy-start | bytes 98308
  47.4 7.1 %copy-start.26 = (bf16[128,896]{1,0:T(8,128)(2,1)}, bf16[128,896]{1,0:T(8,128)(2,1)S(1)}, u32[]{:S(2)}) copy-start(bf16[128,896]{1,0:T(8,128)(2,1)S(1)} %collective-permute-done.2.refs_5_) | copy-start | bytes 688132
  48.3 44.2 %copy-start.10 = (bf16[8,40,2048]{2,1,0:T(8,128)(2,1)}, bf16[8,40,2048]{2,1,0:T(8,128)(2,1)S(1)}, u32[]{:S(2)}) copy-start(bf16[8,40,2048]{2,1,0:T(8,128)(2,1)S(1)} %all-to-all-done) | copy-start | bytes 3932164
  141.1 22.8 %all-to-all-start.1 = ((bf16[8,40,2176]{2,1,0:T(8,128)(2,1)}), bf16[8,40,2176]{2,1,0:T(8,128)(2,1)S(1)}, u32[]{:S(2)}, u32[]{:S(2)}) async-start(bf16[8,40,2176]{2,1,0:T(8,128)(2,1)} %bitcast.156), calls=%async_computation.2 | async-start | bytes 2785280 | tf_op jit(solution)/shard_map/all_to_all | solution.py:760
  144.8 134.3 %reduce-scatter.7.cloned.1.call-start = ((), (), s32[]{:S(2)}) async-start(), calls=%async_computation.11 | async-start | bytes 2949120 | tf_op jit(solution)/shard_map/reduce_scatter | solution.py:919
  149.3 43.6 %collective-permute-start.5 = (bf16[128,1536]{1,0:T(8,128)(2,1)}, bf16[128,1536]{1,0:T(8,128)(2,1)S(1)}, u32[]{:S(2)}, u32[]{:S(2)}) collective-permute-start(bf16[128,1536]{1,0:T(8,128)(2,1)} %get-tuple-element.226), channel_id=1, source_target_pairs={{0,3},{1,0},{2,1},{3,2},{4,7},{5,4},{6,5},{7,6},{8,11},{9,8},{10,9... | collective-permute-start | bytes 1179656 | tf_op jit(solution)/shard_map/ppermute | solution.py:701
  151.0 42.0 %collective-permute-start.3 = (bf16[128,1536]{1,0:T(8,128)(2,1)}, bf16[128,1536]{1,0:T(8,128)(2,1)S(1)}, u32[]{:S(2)}, u32[]{:S(2)}) collective-permute-start(bf16[128,1536]{1,0:T(8,128)(2,1)} %get-tuple-element.227), channel_id=1, source_target_pairs={{0,1},{1,2},{2,3},{3,0},{4,5},{5,6},{6,7},{7,4},{8,9},{9,10},{10,1... | collective-permute-start | bytes 1179656 | tf_op jit(solution)/shard_map/ppermute | solution.py:701
  151.5 41.5 %collective-permute-start.4 = (bf16[128,1536]{1,0:T(8,128)(2,1)}, bf16[128,1536]{1,0:T(8,128)(2,1)S(1)}, u32[]{:S(2)}, u32[]{:S(2)}) collective-permute-start(bf16[128,1536]{1,0:T(8,128)(2,1)} %get-tuple-element.228), channel_id=1, source_target_pairs={{0,2},{1,3},{2,0},{3,1},{4,6},{5,7},{6,4},{7,5},{8,10},{9,11},{10,... | collective-permute-start | bytes 1179656 | tf_op jit(solution)/shard_map/ppermute | solution.py:701
  193.0 33.1 %copy-start.19 = (bf16[128,1536]{1,0:T(8,128)(2,1)}, bf16[128,1536]{1,0:T(8,128)(2,1)S(1)}, u32[]{:S(2)}) copy-start(bf16[128,1536]{1,0:T(8,128)(2,1)S(1)} %collective-permute-done.3) | copy-start | bytes 1179652
  193.0 33.1 %copy-start.17 = (bf16[128,1536]{1,0:T(8,128)(2,1)}, bf16[128,1536]{1,0:T(8,128)(2,1)S(1)}, u32[]{:S(2)}) copy-start(bf16[128,1536]{1,0:T(8,128)(2,1)S(1)} %collective-permute-done.4) | copy-start | bytes 1179652
  226.1 29.8 %all-to-all-start.2 = ((bf16[8,40,2176]{2,1,0:T(8,128)(2,1)}), bf16[8,40,2176]{2,1,0:T(8,128)(2,1)S(1)}, u32[]{:S(2)}, u32[]{:S(2)}) async-start(bf16[8,40,2176]{2,1,0:T(8,128)(2,1)} %bitcast.42), calls=%async_computation.3 | async-start | bytes 2785280 | tf_op jit(solution)/shard_map/all_to_all | solution.py:839
  255.9 23.2 %all-to-all-start.3 = ((bf16[8,40,2176]{2,1,0:T(8,128)(2,1)}), bf16[8,40,2176]{2,1,0:T(8,128)(2,1)S(1)}, u32[]{:S(2)}, u32[]{:S(2)}) async-start(bf16[8,40,2176]{2,1,0:T(8,128)(2,1)} %bitcast.158), calls=%async_computation.4 | async-start | bytes 2785280 | tf_op jit(solution)/shard_map/all_to_all | solution.py:839
  260.0 68.0 %all-gather.5.cloned.1.call-start = ((), (), s32[]{:S(2)}) async-start(), calls=%async_computation.12 | async-start | bytes 1474560 | tf_op jit(solution)/shard_map/all_gather | solution.py:704
  264.3 19.9 %copy-start.42 = (s32[4]{0:T(128)S(1)}, s32[4]{0:T(128)}, u32[]{:S(2)}) copy-start(s32[4]{0:T(128)} %compare_select_fusion.refs_0_) | copy-start | bytes 52
  264.3 20.5 %copy-start.33 = (s32[512,2]{0,1:T(2,128)S(1)}, s32[512,2]{0,1:T(2,128)}, u32[]{:S(2)}) copy-start(s32[512,2]{0,1:T(2,128)} %param.58) | copy-start | bytes 12292
  264.3 21.9 %copy-start.7 = (bf16[128,1536]{1,0:T(8,128)(2,1)S(1)}, bf16[128,1536]{1,0:T(8,128)(2,1)}, u32[]{:S(2)}) copy-start(bf16[128,1536]{1,0:T(8,128)(2,1)} %get-tuple-element.191) | copy-start | bytes 1179652
  280.2 6.1 %copy-start.20 = (bf16[128,1536]{1,0:T(8,128)(2,1)S(1)}, bf16[128,1536]{1,0:T(8,128)(2,1)}, u32[]{:S(2)}) copy-start(bf16[128,1536]{1,0:T(8,128)(2,1)} %copy-done.19) | copy-start | bytes 1179652
  280.2 10.2 %copy-start.18 = (bf16[128,1536]{1,0:T(8,128)(2,1)S(1)}, bf16[128,1536]{1,0:T(8,128)(2,1)}, u32[]{:S(2)}) copy-start(bf16[128,1536]{1,0:T(8,128)(2,1)} %copy-done.17) | copy-start | bytes 1179652
  284.1 88.3 %reduce-scatter.9.cloned.1.call-start = ((), (), s32[]{:S(2)}) async-start(), calls=%async_computation.13 | async-start | bytes 2457600 | tf_op jit(solution)/shard_map/reduce_scatter | solution.py:919
  286.4 13.9 %collective-permute-start.8 = (bf16[128,1024]{1,0:T(8,128)(2,1)S(1)}, bf16[128,1024]{1,0:T(8,128)(2,1)S(1)}, u32[]{:S(2)}, u32[]{:S(2)}) collective-permute-start(bf16[128,1024]{1,0:T(8,128)(2,1)S(1)} %copy-done.22), channel_id=1, source_target_pairs={{0,3},{1,0},{2,1},{3,2},{4,7},{5,4},{6,5},{7,6},{8,11},{9,8},{10,9... | collective-permute-start | bytes 786440 | tf_op jit(solution)/shard_map/ppermute | solution.py:701
  288.5 39.3 %collective-permute-start.7 = (bf16[128,1024]{1,0:T(8,128)(2,1)S(1)}, bf16[128,1024]{1,0:T(8,128)(2,1)S(1)}, u32[]{:S(2)}, u32[]{:S(2)}) collective-permute-start(bf16[128,1024]{1,0:T(8,128)(2,1)S(1)} %copy-done.22), channel_id=1, source_target_pairs={{0,2},{1,3},{2,0},{3,1},{4,6},{5,7},{6,4},{7,5},{8,10},{9,11},{10,... | collective-permute-start | bytes 786440 | tf_op jit(solution)/shard_map/ppermute | solution.py:701
  288.5 39.3 %collective-permute-start.6 = (bf16[128,1024]{1,0:T(8,128)(2,1)S(1)}, bf16[128,1024]{1,0:T(8,128)(2,1)S(1)}, u32[]{:S(2)}, u32[]{:S(2)}) collective-permute-start(bf16[128,1024]{1,0:T(8,128)(2,1)S(1)} %copy-done.22), channel_id=1, source_target_pairs={{0,1},{1,2},{2,3},{3,0},{4,5},{5,6},{6,7},{7,4},{8,9},{9,10},{10,1... | collective-permute-start | bytes 786440 | tf_op jit(solution)/shard_map/ppermute | solution.py:701
  300.3 27.8 %copy-start.23 = (bf16[128,1024]{1,0:T(8,128)(2,1)}, bf16[128,1024]{1,0:T(8,128)(2,1)S(1)}, u32[]{:S(2)}) copy-start(bf16[128,1024]{1,0:T(8,128)(2,1)S(1)} %collective-permute-done.8.refs_5_) | copy-start | bytes 786436
  328.0 93.6 %reduce-scatter.11.cloned.1.call-start = ((), (), s32[]{:S(2)}) async-start(), calls=%async_computation.14 | async-start | bytes 2621440 | tf_op jit(solution)/shard_map/reduce_scatter | solution.py:1053
  371.5 5.9 %copy-start.28 = (bf16[128,512]{1,0:T(8,128)(2,1)S(1)}, bf16[128,512]{1,0:T(8,128)(2,1)}, u32[]{:S(2)}) copy-start(bf16[128,512]{1,0:T(8,128)(2,1)} %get-tuple-element.197) | copy-start | bytes 393220
  372.4 5.3 %collective-permute-start.11 = (bf16[272,128]{1,0:T(8,128)(2,1)}, bf16[272,128]{1,0:T(8,128)(2,1)S(1)}, u32[]{:S(2)}, u32[]{:S(2)}) collective-permute-start(bf16[272,128]{1,0:T(8,128)(2,1)} %get-tuple-element.177), channel_id=1, source_target_pairs={{0,3},{1,0},{2,1},{3,2},{4,7},{5,4},{6,5},{7,6},{8,11},{9,8},{10,9... | collective-permute-start | bytes 208904 | tf_op jit(solution)/shard_map/ppermute | solution.py:701
  374.2 7.7 %collective-permute-start.10 = (bf16[272,128]{1,0:T(8,128)(2,1)}, bf16[272,128]{1,0:T(8,128)(2,1)S(1)}, u32[]{:S(2)}, u32[]{:S(2)}) collective-permute-start(bf16[272,128]{1,0:T(8,128)(2,1)} %get-tuple-element.177), channel_id=1, source_target_pairs={{0,2},{1,3},{2,0},{3,1},{4,6},{5,7},{6,4},{7,5},{8,10},{9,11},{10,... | collective-permute-start | bytes 208904 | tf_op jit(solution)/shard_map/ppermute | solution.py:701
  374.5 7.4 %collective-permute-start.9 = (bf16[272,128]{1,0:T(8,128)(2,1)}, bf16[272,128]{1,0:T(8,128)(2,1)S(1)}, u32[]{:S(2)}, u32[]{:S(2)}) collective-permute-start(bf16[272,128]{1,0:T(8,128)(2,1)} %get-tuple-element.177), channel_id=1, source_target_pairs={{0,1},{1,2},{2,3},{3,0},{4,5},{5,6},{6,7},{7,4},{8,9},{9,10},{10,1... | collective-permute-start | bytes 208904 | tf_op jit(solution)/shard_map/ppermute | solution.py:701
  377.6 11.1 %copy-start.30 = (bf16[272,128]{1,0:T(8,128)(2,1)S(1)}, bf16[272,128]{1,0:T(8,128)(2,1)}, u32[]{:S(2)}) copy-start(bf16[272,128]{1,0:T(8,128)(2,1)} %get-tuple-element.177) | copy-start | bytes 208900
  381.9 6.9 %copy-start.5 = (bf16[512,512]{1,0:T(8,128)(2,1)S(1)}, bf16[512,512]{1,0:T(8,128)(2,1)}, u32[]{:S(2)}) copy-start(bf16[512,512]{1,0:T(8,128)(2,1)} %shard_map.412) | copy-start | bytes 1572868
  393.5 18.9 %all-to-all-start.4 = ((bf16[8,480,128]{2,1,0:T(8,128)(2,1)}), bf16[8,480,128]{2,1,0:T(8,128)(2,1)S(1)}, u32[]{:S(2)}, u32[]{:S(2)}) async-start(bf16[8,480,128]{2,1,0:T(8,128)(2,1)} %copy.164), calls=%async_computation.8 | async-start | bytes 1966080 | tf_op jit(solution)/shard_map/all_to_all | solution.py:1093
  397.9 14.5 %copy-start.41 = (s32[8]{0:T(128)S(1)}, s32[8]{0:T(128)}, u32[]{:S(2)}) copy-start(s32[8]{0:T(128)} %param.57) | copy-start | bytes 100
  (19 other events, 58.3 us)
Sparse Core Ops, SparseCore 0:
  17.6 36.9 all-gather.2
  92.6 45.1 reduce-scatter.4
  226.2 45.5 reduce-scatter.6
  284.2 43.6 all-gather.4
  330.3 42.0 reduce-scatter.8
  376.5 44.4 reduce-scatter.10

commit v4 on v3

--- a/solution.py
+++ b/solution.py
@@ -18,6 +18,7 @@
 GATE_LANE = 64
 ROUTE_LANE = 96
 ROUTER_ROW = 32
+DEPTH = 3
 
 
 f32 = jnp.float32
@@ -124,6 +125,30 @@
         total[k * s : (k + 1) * s, :] += jnp.where(routes[:, k : k + 1] == expert, part, 0.0)
 
 
+def weight_stream(n, count, fetch):
+    def prime():
+        for j in range(min(DEPTH - 1, count)):
+            for copy in fetch(j, j):
+                copy.start()
+
+    def advance():
+        later = n + DEPTH - 1
+
+        @pl.when(later < count)
+        def _():
+            for copy in fetch(later, lax.rem(later, DEPTH)):
+                copy.start()
+
+        for copy in fetch(n, lax.rem(n, DEPTH)):
+            copy.wait()
+
+    return prime, advance
+
+
+def block_at(n, width):
+    return pl.ds(pl.multiple_of(n * width, LOW), width)
+
+
 def copies(sources, targets, sems):
     return [
         pltpu.make_async_copy(source, target, sems.at[j])
@@ -151,13 +176,30 @@
 
 
 def attention_steps(
-    xn, wq, wo, ob, wk_far, wv_far, aq, amisc, bcat, kb, vb, routes, cosf, sinf, oa,
+    xn, wq_far, wo_far, ob, wk_far, wv_far, aq, amisc, bcat, kb, vb, routes, cosf, sinf, oa,
     attn_out, out_low, q_far, k_far, v_far, ga_far, low_far, misc_far, o_far, lse_far,
-    q, k, v, ga, low, misc, o, lse, qsum, og, chosen, wk, wv, load_sems, save_sems,
+    q, k, v, ga, low, misc, o, lse, qsum, og, chosen, wk, wv, load_sems, save_sems, wq, wo, wq_sems, wo_sems,
 ):
     step = pl.program_id(0)
     s, width = k.shape
     loads = copies((wk_far, wv_far), (wk, wv), load_sems)
+    width_d = wo.shape[3]
+    prime_q, next_q = weight_stream(
+        step,
+        ATT_EXPERTS,
+        lambda n, slot: [
+            pltpu.make_async_copy(wq_far.at[n], wq.at[slot], wq_sems.at[slot]),
+        ],
+    )
+    prime_o, next_o = weight_stream(
+        step - ATT_EXPERTS,
+        D // width_d,
+        lambda n, slot: [
+            pltpu.make_async_copy(
+                wo_far.at[:, :, block_at(n, width_d)], wo.at[slot], wo_sems.at[slot]
+            ),
+        ],
+    )
     saves = copies(
         (q, k, v, ga, low, misc, o, lse),
         (q_far, k_far, v_far, ga_far, low_far, misc_far, o_far, lse_far),
@@ -166,6 +208,7 @@
 
     @pl.when(step == 0)
     def _():
+        prime_q()
         for load in loads:
             load.start()
         x = xn[...]
@@ -186,10 +229,12 @@
 
     @pl.when(step < ATT_EXPERTS)
     def _():
-        select_add(qsum, nn(xn[...], wq[0]), routes, step)
+        next_q()
+        select_add(qsum, nn(xn[...], wq[lax.rem(step, DEPTH)]), routes, step)
 
     @pl.when(step == ATT_EXPERTS - 1)
     def _():
+        prime_o()
         for load in loads:
             load.wait()
         x = xn[...]
@@ -213,7 +258,8 @@
 
     @pl.when(step >= ATT_EXPERTS)
     def _():
-        weights = wo[...].reshape(chosen.shape[1], wo.shape[2])
+        next_o()
+        weights = wo[lax.rem(step - ATT_EXPERTS, DEPTH)].reshape(chosen.shape[1], width_d)
         attn_out[...] = (nn(chosen[...], weights) + nn(out_low[...], ob[...])).astype(bf16)
 
     @pl.when(step == pl.num_programs(0) - 1)
@@ -238,7 +284,7 @@
     for i in range(s // CHUNK):
         end = (i + 1) * CHUNK
         first, second = slice(i * CHUNK, end), slice(s + i * CHUNK, s + end)
-        gates = [lane_of(ga[first, :], 0), lane_of(ga[first, :], 1)]
+        gates = [ga[first, 0:1], ga[first, 1:2]]
         log_totals = jnp.zeros((2 * CHUNK, LOW), f32)
         for h in range(width // HD):
             hs = slice(h * HD, (h + 1) * HD)
@@ -318,7 +364,7 @@
     lane = iota((mcol.shape[0], ze.shape[0]), 1)
     gates, slopes, lows = [], [], []
     for k in range(2):
-        gates.append(lane_of(gm[...], k))
+        gates.append(gm[:, k : k + 1])
         pick = ones_where(mcol[:, k : k + 1] == lane)
         expert_out = nn(pick, ze[:, 0:D])
         lows.append(gates[k] * nn(pick, ze[:, D : D + LOW]))
@@ -396,29 +442,57 @@
 
 
 def expert_up_kernel(
-    x, mask, ga, ua, gate_w, up_w, gate_b, up_b, g_out, u_out, lg_out, lu_out
+    x, mask, ga, ua, gate_far, up_far, gate_b, up_b, g_out, u_out, lg_out, lu_out,
+    gate_w, up_w, sems,
 ):
     x = x.at[:, 0:D]
-
-    @pl.when(pl.program_id(0) == 0)
-    def _():
+    f = pl.program_id(0)
+    width = gate_w.shape[2]
+    prime, advance = weight_stream(
+        f,
+        gate_far.shape[1] // width,
+        lambda n, slot: [
+            pltpu.make_async_copy(
+                gate_far.at[:, block_at(n, width)], gate_w.at[slot], sems.at[0, slot]
+            ),
+            pltpu.make_async_copy(
+                up_far.at[:, block_at(n, width)], up_w.at[slot], sems.at[1, slot]
+            ),
+        ],
+    )
+
+    @pl.when(f == 0)
+    def _():
+        prime()
         lg_out[...] = nt(x[...], ga[...]).astype(bf16) * mask[...]
         lu_out[...] = nt(x[...], ua[...]).astype(bf16) * mask[...]
 
-    g_out[...] = (nn(x[...], gate_w[...]) + nn(lg_out[...], gate_b[...])).astype(bf16)
-    u_out[...] = (nn(x[...], up_w[...]) + nn(lu_out[...], up_b[...])).astype(bf16)
+    advance()
+    slot = lax.rem(f, DEPTH)
+    g_out[...] = (nn(x[...], gate_w[slot]) + nn(lg_out[...], gate_b[...])).astype(bf16)
+    u_out[...] = (nn(x[...], up_w[slot]) + nn(lu_out[...], up_b[...])).astype(bf16)
 
 
 def expert_down_kernel(
-    grads, x, mask, db, lg, lu, g, u, down_w, gate_b, up_b, down_a,
+    grads, x, mask, db, lg, lu, g, u, down_far, gate_b, up_b, down_a,
     ze_out, dg_out, du_out, dlg_out, dlu_out, *rest,
 ):
-    *tables_out, dy, total, pd, dlg, dlu, dpd, lg_t, lu_t, dpd_t, tables = rest
+    *tables_out, dy, total, pd, dlg, dlu, dpd, lg_t, lu_t, dpd_t, tables, down, sems = rest
     f = pl.program_id(0)
-    width = down_w.shape[0]
+    width = down.shape[1]
+    prime, advance = weight_stream(
+        f,
+        down_far.shape[0] // width,
+        lambda n, slot: [
+            pltpu.make_async_copy(
+                down_far.at[block_at(n, width), :], down.at[slot], sems.at[slot]
+            ),
+        ],
+    )
 
     @pl.when(f == 0)
     def _():
+        prime()
         gate = x[:, D : D + LOW].astype(f32)
         gate = lane_of(gate, 0) + lane_of(gate, 1)
         dy[...] = (gate * grads[...].astype(f32)).astype(bf16)
@@ -429,6 +503,8 @@
         for sums in (total, pd, dlg, dlu):
             sums[...] = jnp.zeros_like(sums)
 
+    advance()
+    down_w = down.at[lax.rem(f, DEPTH)]
     dh = nt(dy[...], down_w[...]) + nn(dpd[...], down_a[...])
     gate = g[...].astype(f32)
     up = u[...].astype(f32)
@@ -464,18 +540,66 @@
             first += size
 
 
-def expert_rows_kernel(dg, du, dlg, dlu, gate_w, up_w, ga, ua, dm_out):
+def expert_rows_kernel(
+    dg_far, du_far, dlg, dlu, gate_far, up_far, ga, ua, dm_out,
+    dg, du, gate_w, up_w, load_sems, sems,
+):
     n = pl.program_id(0)
-    width = gate_w.shape[0]
+    width, depth = gate_w.shape[1:]
+    span = depth // load_sems.shape[1]
+    prime, advance = weight_stream(
+        n,
+        D // width,
+        lambda at, slot: [
+            pltpu.make_async_copy(
+                gate_far.at[block_at(at, width), :], gate_w.at[slot], sems.at[0, slot]
+            ),
+            pltpu.make_async_copy(
+                up_far.at[block_at(at, width), :], up_w.at[slot], sems.at[1, slot]
+            ),
+        ],
+    )
+    parts = [slice(j * span, (j + 1) * span) for j in range(load_sems.shape[1])]
+    loads = [
+        (
+            pltpu.make_async_copy(dg_far.at[:, at], dg.at[:, at], load_sems.at[0, j]),
+            pltpu.make_async_copy(du_far.at[:, at], du.at[:, at], load_sems.at[1, j]),
+        )
+        for j, at in enumerate(parts)
+    ]
+    slot = lax.rem(n, DEPTH)
+
+    def give(total):
+        total = total + nn(dlg[...], ga[...]) + nn(dlu[...], ua[...])
+        dm_out[:, block_at(n, width)] = total.astype(bf16)
 
     @pl.when(n == 0)
     def _():
+        for pair in loads[:1]:
+            for load in pair:
+                load.start()
+        prime()
+        for pair in loads[1:]:
+            for load in pair:
+                load.start()
         low = nn(dlg[...], fold(0)) + nn(dlu[...], fold(RANK))
         dm_out[:, D : D + LOW] = low.astype(bf16)
 
-    total = nt(dg[...], gate_w[...]) + nt(du[...], up_w[...])
-    total = total + nn(dlg[...], ga[...]) + nn(dlu[...], ua[...])
-    dm_out[:, pl.ds(pl.multiple_of(n * width, LOW), width)] = total.astype(bf16)
+    advance()
+
+    @pl.when(n == 0)
+    def _():
+        total = None
+        for at, pair in zip(parts, loads, strict=True):
+            for load in pair:
+                load.wait()
+            new = nt(dg[:, at], gate_w[slot, :, at]) + nt(du[:, at], up_w[slot, :, at])
+            total = new if total is None else total + new
+        give(total)
+
+    @pl.when(n > 0)
+    def _():
+        give(nt(dg[...], gate_w[slot]) + nt(du[...], up_w[slot]))
 
 
 def attention_back_kernel(shards, places, left, *refs):
@@ -490,14 +614,31 @@
 
 
 def attention_back_steps(
-    da, wo, wq, wk, wv, aq, amisc, bcat, kb, vb, oa, ob, routes,
+    da, wo_far, wq_far, wk, wv, aq, amisc, bcat, kb, vb, oa, ob, routes,
     ga_far, o_far, q_far, k_far, v_far, lse_far, low_far, misc_far, cosf_far, sinf_far,
     dx_out, lows_out, grad_oa_out, grad_qb_out, grad_kv_out,
     ga, o, q, k, v, lse, low, misc, cosf, sinf, sems,
-    dzl, dosum, do, stats, dq, dk, dv, lows_dense, dk_sum, dv_sum, chosen,
+    dzl, dosum, do, stats, dq, dk, dv, lows_dense, dk_sum, dv_sum, chosen, wo, wq, wo_sems, wq_sems,
 ):
     step = pl.program_id(0)
     s, width = k.shape
+    width_d = wq.shape[2]
+    prime_o, next_o = weight_stream(
+        step,
+        ATT_EXPERTS,
+        lambda n, slot: [
+            pltpu.make_async_copy(wo_far.at[n], wo.at[slot], wo_sems.at[slot]),
+        ],
+    )
+    prime_q, next_q = weight_stream(
+        step - ATT_EXPERTS,
+        D // width_d,
+        lambda n, slot: [
+            pltpu.make_async_copy(
+                wq_far.at[:, block_at(n, width_d), :], wq.at[slot], wq_sems.at[slot]
+            ),
+        ],
+    )
     loads = copies(
         (ga_far, o_far, q_far, k_far, v_far, lse_far, low_far, misc_far, cosf_far, sinf_far),
         (ga, o, q, k, v, lse, low, misc, cosf, sinf),
@@ -506,6 +647,7 @@
 
     @pl.when(step == 0)
     def _():
+        prime_o()
         for load in loads:
             load.start()
         dzl[...] = nt(da[...], ob[...])
@@ -516,10 +658,12 @@
 
     @pl.when(step < ATT_EXPERTS)
     def _():
-        select_add(dosum, nt(da[...], wo[0]), routes, step)
+        next_o()
+        select_add(dosum, nt(da[...], wo[lax.rem(step, DEPTH)]), routes, step)
 
     @pl.when(step == ATT_EXPERTS - 1)
     def _():
+        prime_q()
         for load in loads:
             load.wait()
         out_back(routes, ga, o, dzl, dosum, do, stats, grad_oa_out)
@@ -531,6 +675,8 @@
 
     @pl.when(step >= ATT_EXPERTS)
     def _():
+        next_q()
+        slot = lax.rem(step - ATT_EXPERTS, DEPTH)
         total = (
             nn(lows_dense[:, 0:LOW], aq[...])
             + nn(lows_dense[:, LOW : 2 * LOW], amisc[...])
@@ -538,7 +684,7 @@
             + nt(dv[...], wv[...])
         )
         for e in range(ATT_EXPERTS):
-            total = total + nt(chosen[:, e * width : (e + 1) * width], wq[e])
+            total = total + nt(chosen[:, e * width : (e + 1) * width], wq[slot, e])
         dx_out[...] = total.astype(bf16)
 
 
@@ -547,7 +693,7 @@
     grad_oa = jnp.zeros((LOW, width), f32)
     for k in range(2):
         at = slice(k * s, (k + 1) * s)
-        gate = lane_of(ga[...], k)
+        gate = ga[:, k : k + 1]
         mine = routed(routes[:, k : k + 1], (s, LOW))
         low = jnp.where(mine, gate * dzl[...], 0.0).astype(bf16)
         grad_oa = grad_oa + tn(low, o[at, :])
@@ -578,12 +724,8 @@
             first, second = slice(i * CHUNK, end), slice(s + i * CHUNK, s + end)
             queries = jnp.concatenate([q[first, hs], q[second, hs]], axis=0)
             grads = jnp.concatenate([do[first, hs], do[second, hs]], axis=0)
-            logs = jnp.concatenate(
-                [lane_of(lse[first, :], h), lane_of(lse[second, :], h)], axis=0
-            )
-            centre = jnp.concatenate(
-                [lane_of(stats[first, :], h), lane_of(stats[second, :], h)], axis=0
-            )
+            logs = jnp.concatenate([lse[first, h : h + 1], lse[second, h : h + 1]], axis=0)
+            centre = jnp.concatenate([stats[first, h : h + 1], stats[second, h : h + 1]], axis=0)
             scores = nt(queries, k[0:end, hs]) * score_scale
             weights = jnp.where(causal(i, scores.shape), jnp.exp(scores - logs), 0.0)
             dscores = (weights * (nt(grads, v[0:end, hs]) - centre)).astype(bf16)
@@ -634,7 +776,7 @@
 
 def input_grad_kernel(dx, slopes, ga, tokens, gain, router, dh1, routes, out):
     x = tokens[...].astype(f32)
-    gates = [lane_of(ga[...], k) for k in range(2)]
+    gates = [ga[:, k : k + 1] for k in range(2)]
     slope = [slopes[:, k : k + 1] for k in range(2)]
     mean = gates[0] * slope[0] + gates[1] * slope[1]
     total = jnp.zeros(ga.shape, f32)
@@ -776,7 +918,6 @@
     column_parts = 8
     width_d = D // column_parts
     steps_attn = ATT_EXPERTS + column_parts
-    early = lambda e: (jnp.minimum(e, ATT_EXPERTS - 1), 0, 0)
     late = lambda e: jnp.maximum(e - ATT_EXPERTS, 0)
     column_block = pl.BlockSpec((LOW, width_d), lambda e: (0, late(e)))
     out_block = pl.BlockSpec((seq, width_d), lambda e: (0, late(e)))
@@ -794,8 +935,8 @@
         [pl.BlockSpec(memory_space=pltpu.SMEM)]
         + [whole()] * (1 + shards)
         + [
-            pl.BlockSpec((1, D, width), early),
-            pl.BlockSpec((ATT_EXPERTS, width, width_d), lambda e: (0, 0, late(e))),
+            far,
+            far,
             column_block,
             far,
             far,
@@ -812,6 +953,10 @@
             pltpu.VMEM((D, width), bf16),
             pltpu.SemaphoreType.DMA((2,)),
             pltpu.SemaphoreType.DMA((8,)),
+            pltpu.VMEM((DEPTH, D, width), bf16),
+            pltpu.VMEM((DEPTH, ATT_EXPERTS, width, width_d), bf16),
+            pltpu.SemaphoreType.DMA((DEPTH,)),
+            pltpu.SemaphoreType.DMA((DEPTH,)),
             pltpu.VMEM((seq, D), bf16),
         ],
         project_flops,
@@ -862,8 +1007,6 @@
 
     steps = 11
     fb = ff // steps
-    columns = pl.BlockSpec((D, fb), lambda f: (0, f))
-    weight_rows = pl.BlockSpec((fb, D), lambda f: (f, 0))
     table = pl.BlockSpec((LOW, fb), lambda f: (0, f))
     kept = pl.BlockSpec((expert_rows, fb), lambda f: (0, f))
     weight_flops = 2 * expert_rows * D * ff
@@ -875,10 +1018,14 @@
     g, u, lg, lu = call(
         expert_up_kernel,
         (steps,),
-        [whole()] * 4 + [columns, columns, table, table],
+        [whole()] * 4 + [far, far, table, table],
         [kept, kept, whole(), whole()],
         [wide_shape, wide_shape, low_shape, low_shape],
-        [],
+        [
+            pltpu.VMEM((DEPTH, D, fb), bf16),
+            pltpu.VMEM((DEPTH, D, fb), bf16),
+            pltpu.SemaphoreType.DMA((2, DEPTH)),
+        ],
         2 * weight_flops,
         2 * weight_moved,
     )(rows_in, mask, gate_first, up_first, gate_w, up_w, gate_table, up_table)
@@ -892,14 +1039,14 @@
     out_lows = out_lows.astype(bf16).transpose(1, 0, 2).reshape(seq, LOW)
 
     each = ff // shards
-    head = ((each // LOW + 1) // 2) * LOW
+    head = (each // LOW * 2 // 3) * LOW
     spans = [head, each - head] if each % LOW == 0 else [each]
     low_sum = pltpu.VMEM((expert_rows, LOW), f32)
     low_turned = pltpu.VMEM((LOW, expert_rows), bf16)
     ze, dg, du, dlg, dlu, *tables = call(
         expert_down_kernel,
         (steps,),
-        [whole()] * 6 + [kept, kept, weight_rows, table, table, table],
+        [whole()] * 6 + [kept, kept, far, table, table, table],
         [whole(), kept, kept, whole(), whole()] + [whole() for _ in spans],
         [out_shape, wide_shape, wide_shape, low_shape, low_shape]
         + [sds((shards, 3 * LOW, span), bf16) for span in spans],
@@ -907,7 +1054,11 @@
         + [pltpu.VMEM((expert_rows, D), f32), low_sum, low_sum, low_sum]
         + [pltpu.VMEM((expert_rows, LOW), bf16)]
         + [low_turned] * 3
-        + [pltpu.VMEM((3 * LOW, ff), bf16)],
+        + [
+            pltpu.VMEM((3 * LOW, ff), bf16),
+            pltpu.VMEM((DEPTH, fb, D), bf16),
+            pltpu.SemaphoreType.DMA((DEPTH,)),
+        ],
         2 * weight_flops,
         weight_moved,
     )(grads_in, rows_in, mask, down_second, lg, lu, g, u, down_w, gate_table, up_table, down_table)
@@ -920,17 +1071,24 @@
 
     head_tables = table_sum(tables[0])
 
-    parts = 8
+    parts = 4
     db = D // parts
-    row_block = pl.BlockSpec((db, ff), lambda n: (n, 0))
+    loads = ff // (11 * LOW) if ff % (11 * LOW) == 0 else 1
     low_block = pl.BlockSpec((LOW, db), lambda n: (0, n))
     dm = call(
         expert_rows_kernel,
         (parts,),
-        [whole()] * 4 + [row_block, row_block, low_block, low_block],
+        [far, far, whole(), whole(), far, far, low_block, low_block],
         whole(),
         out_shape,
-        [],
+        [
+            pltpu.VMEM((expert_rows, ff), bf16),
+            pltpu.VMEM((expert_rows, ff), bf16),
+            pltpu.VMEM((DEPTH, db, ff), bf16),
+            pltpu.VMEM((DEPTH, db, ff), bf16),
+            pltpu.SemaphoreType.DMA((2, loads)),
+            pltpu.SemaphoreType.DMA((2, DEPTH)),
+        ],
         2 * weight_flops,
         2 * weight_moved,
     )(dg, du, dlg, dlu, gate_w, up_w, gate_first, up_first)
@@ -987,8 +1145,8 @@
         [pl.BlockSpec(memory_space=pltpu.SMEM)]
         + [whole()] * (1 + shards)
         + [
-            pl.BlockSpec((1, width, D), early),
-            pl.BlockSpec((ATT_EXPERTS, width_d, width), lambda e: (0, late(e), 0)),
+            far,
+            far,
             key_block,
             key_block,
             column_block,
@@ -1018,6 +1176,10 @@
             pltpu.VMEM((seq, HD), f32),
             pltpu.VMEM((seq, HD), f32),
             pltpu.VMEM((seq, ATT_EXPERTS * width), bf16),
+            pltpu.VMEM((DEPTH, width, D), bf16),
+            pltpu.VMEM((DEPTH, ATT_EXPERTS, width_d, width), bf16),
+            pltpu.SemaphoreType.DMA((DEPTH,)),
+            pltpu.SemaphoreType.DMA((DEPTH,)),
             pltpu.VMEM((seq, D), bf16),
         ],
         project_flops,

time: 437 us -> 428 us (0.979)
  Pallas kernels: 192 us -> 184 us
  transfers between devices with their start and end apart: 23 -> 23, of which waited for: 11 -> 10; matrix products, arithmetic and copies ran while one was open for 12% -> 12% of each run, Pallas kernels for 26% -> 25%
where the time goes in v4:
time: 428 us; the launch traced here: 424 us
  Pallas kernels  184 us (43%)
  waiting for transfers between devices  126 us (29%)
  local copies, waits for them, and re-layouts  45 us (11%)
  starting transfers between devices  38.1 us (9%)
  between operations  17.3 us (4%)
  other arithmetic  10.7 us (2%)
    reduce_scatter x1, waiting for transfers between devices, on_device(): attn = lax.psum_scatter(attn_part, 'shard', scatter_dimension=0, tiled=True)  44.7 us
    pallas_call x1, Pallas kernels, on_device(): call(lambda *refs: attention_back_kernel(shards, *refs), (steps_attn,), [...  41.9 us
    ppermute x12, waiting for transfers between devices, shifted(): return lax.ppermute(part, 'shard', pairs) if step else part  35.4 us
    pallas_call x1, Pallas kernels, on_device(): call(lambda *refs: attention_kernel(shards, *refs), (steps_attn,), [pl.Bl...  34.5 us
    pallas_call x1, Pallas kernels, on_device(): call(expert_down_kernel, (steps,), [whole()] * 6 + [kept, kept, far, tabl...  33.4 us
    pallas_call x1, Pallas kernels, on_device(): call(expert_rows_kernel, (parts,), [far, far, whole(), whole(), far, far,...  25.9 us
    pallas_call x1, Pallas kernels, on_device(): call(expert_up_kernel, (steps,), [whole()] * 4 + [far, far, table, table]...  23.8 us
    ppermute x12, starting transfers between devices, shifted(): return lax.ppermute(part, 'shard', pairs) if step else part  18.8 us
  transfers between devices with their start and end apart: 23, of which 10 were waited for; matrix products, arithmetic and copies ran while one was open for 12% of the time, Pallas kernels for 25%

profile of v4, /device:TPU:0, one launch (start us, length us, event | category | flops | bytes accessed | tf_op | source)
XLA Modules:
  0.0 423.9 jit_solution(7449135458349544744)
XLA Ops:
  7.3 1.3 fusion.2
  9.3 1.2 fusion.4
  10.6 5.1 %collective-permute-start.2 = (bf16[128,896]{1,0:T(8,128)(2,1)S(1)}, bf16[128,896]{1,0:T(8,128)(2,1)S(1)}, u32[]{:S(2)}, u32[]{:S(2)}) collective-permute-start(bf16[128,896]{1,0:T(8,128)(2,1)S(1)} %slice.140.refs_2_), channel_id=1, source_target_pairs={{0,3},{1,0},{2,1},{3,2},{4,7},{5,4},{6,5},{7,6},{8,11},{9,8},{10,9... | collective-permute-start | bytes 688136 | tf_op jit(solution)/shard_map/ppermute | solution.py:843
  18.1 1.6 convolution_convert_fusion
  19.7 3.9 all-to-all-start
  27.1 1.6 constant_dynamic-slice_fusion.2
  28.8 2.0 constant_dynamic-slice_fusion.4
  35.1 1.9 constant_dynamic-slice_fusion.5
  37.0 1.9 constant_dynamic-slice_fusion.6
  39.7 2.3 constant_dynamic-slice_fusion.7
  48.3 6.3 %all-gather.3.cloned.1.call-done.refs_1_ = bf16[512,1152]{1,0:T(8,128)(2,1)} async-done(((bf16[128,1152]{1,0:T(8,128)(2,1)}), bf16[512,1152]{1,0:T(8,128)(2,1)}) %all-gather.3.cloned.1.call-update) | async-done | bytes 1179664 | tf_op jit(solution)/shard_map/all_gather | solution.py:846
  54.6 34.5 %shard_map.405 = (bf16[512,2048]{1,0:T(8,128)(2,1)}, bf16[512,128]{1,0:T(8,128)(2,1)}, bf16[1024,512]{1,0:T(8,128)(2,1)}, bf16[512,512]{1,0:T(8,128)(2,1)}, bf16...) custom-call(s32[4]{0:T(128)} %compare_select_fusion.refs_0_, ...), custom_call_target="tpu_custom_call" | custom-call | flops 68719476736 | bytes 134217728 | tf_op jit(solution)/shard_map/pallas_call | solution.py:932
  89.8 44.7 %reduce-scatter.5.cloned.1.call-done.refs_0_.refs_1_.attn = bf16[128,2048]{1,0:T(8,128)(2,1)} async-done(((bf16[512,2048]{1,0:T(8,128)(2,1)}), bf16[128,2048]{1,0:T(8,128)(2,1)}) %reduce-scatter.5.cloned.1.call-update) | async-done | bytes 524304 | tf_op jit(solution)/shard_map/reduce_scatter | solution.py:966
  134.5 3.3 shard_map.406
  137.8 3.7 all-to-all-start.1
  144.8 1.2 pad_maximum_fusion
  146.0 2.1 collective-permute-start.5
  148.4 1.7 collective-permute-start.4
  150.2 10.4 %all-to-all-done.1 = bf16[8,40,2176]{2,1,0:T(8,128)(2,1)S(1)} async-done(((bf16[8,40,2176]{2,1,0:T(8,128)(2,1)}), bf16[8,40,2176]{2,1,0:T(8,128)(2,1)S(1)}, u32[]{:S(2)}, u32[]{:S(2)}) %all-to-all-start.1) | async-done | bytes 1392672 | tf_op jit(solution)/shard_map/all_to_all | solution.py:902
  160.5 1.1 copy-done.8
  161.6 23.8 %shard_map.407 = (bf16[320,5632]{1,0:T(8,128)(2,1)}, bf16[320,5632]{1,0:T(8,128)(2,1)}, bf16[320,128]{1,0:T(8,128)(2,1)}, bf16[320,128]{1,0:T(8,128)(2,1)}) custom-call(bf16[320,2176]{1,0:T(8,128)(2,1)} %bitcast.154, bf16[320,128]{1,0:T(8,128)(2,1)} %compare_convert_fusion.mask, bf16[128,2048]{1,0:T(8,128)(2,1)} %bitcast.172, bf16[128,2048]{1,0:T(8,128)(2,1)} %bitcast.170, ...), custom_call_target="tpu_custom_call" | custom-call | flops 59055800320 | bytes 184549376 | tf_op jit(solution)/shard_map/pallas_call | solution.py:1018
  185.4 33.4 %shard_map.408 = (bf16[320,2176]{1,0:T(8,128)(2,1)}, bf16[320,5632]{1,0:T(8,128)(2,1)}, bf16[320,5632]{1,0:T(8,128)(2,1)}, bf16[320,128]{1,0:T(8,128)(2,1)}, bf1...) custom-call(bf16[320,2048]{1,0:T(8,128)(2,1)} %bitcast.159, ...), custom_call_target="tpu_custom_call" | custom-call | flops 59055800320 | bytes 92274688 | tf_op jit(solution)/shard_map/pallas_call | solution.py:1046
  218.9 3.6 all-to-all-start.2
  222.5 25.9 %shard_map.410 = bf16[320,2176]{1,0:T(8,128)(2,1)} custom-call(bf16[320,5632]{1,0:T(8,128)(2,1)} %get-tuple-element.135.dg_far, bf16[320,5632]{1,0:T(8,128)(2,1)} %get-tuple-element.136.du_far, bf16[320,128]{1,0:T(8,128)(2,1)} %get-tuple-element.137.dlg, bf16[320,128]{1,0:T(8,128)(2,1)} %get-tuple-element.138.dlu, bf16[2048,5632]{1,0:T(8,128)(2,1)} %gate_far.3, ...), custom_call_target="tpu_custom_call" | custom-call | flops 59055800320 | bytes 184549376 | tf_op jit(solution)/shard_map/pallas_call | solution.py:1078
  248.5 4.1 all-to-all-start.3
  253.4 3.8 shard_map.409
  257.2 14.5 %all-to-all-done.3 = bf16[8,40,2176]{2,1,0:T(8,128)(2,1)S(1)} async-done(((bf16[8,40,2176]{2,1,0:T(8,128)(2,1)}), bf16[8,40,2176]{2,1,0:T(8,128)(2,1)S(1)}, u32[]{:S(2)}, u32[]{:S(2)}) %all-to-all-start.3) | async-done | bytes 1392672 | tf_op jit(solution)/shard_map/all_to_all | solution.py:984
  271.7 1.1 copy-done.3
  272.8 3.9 shard_map.411
  277.4 1.5 constant_dynamic-slice_fusion.ga
  278.9 2.0 collective-permute-start.8
  281.0 1.8 collective-permute-start.6
  282.9 1.2 slice.147.refs_7_
  285.2 3.9 shard_map.412
  289.1 3.0 collective-permute-done.8.refs_5_
  292.1 27.9 %collective-permute-done.7.refs_4_ = bf16[128,1024]{1,0:T(8,128)(2,1)S(1)} collective-permute-done((bf16[128,1024]{1,0:T(8,128)(2,1)S(1)}, bf16[128,1024]{1,0:T(8,128)(2,1)S(1)}, u32[]{:S(2)}, u32[]{:S(2)}) %collective-permute-start.7) | collective-permute-done | bytes 262176 | tf_op jit(solution)/shard_map/ppermute | solution.py:843
  320.0 2.4 all-gather.5.cloned.1.call-done.refs_1_
  322.5 41.9 %shard_map.413 = (bf16[512,2048]{1,0:T(8,128)(2,1)}, bf16[272,128]{1,0:T(8,128)(2,1)}, bf16[128,512]{1,0:T(8,128)(2,1)}, bf16[128,512]{1,0:T(8,128)(2,1)}, bf16[256,512]{1,0:T(8,128)(2,1)}) custom-call(s32[4]{0:T(128)} %compare_select_fusion.refs_0_, bf16[512,1152]{1,0:T(8,128)(2,1)} %all-gather.5.cloned.1.call-done.refs_1_, ...), custom_call_target="tpu_custom_call" | custom-call | flops 68719476736 | bytes 134217728 | tf_op jit(solution)/shard_map/pallas_call | solution.py:1142
  364.5 1.4 collective-permute-start.11
  365.9 1.4 collective-permute-start.10
  367.2 1.9 collective-permute-start.9
  370.6 3.6 collective-permute-done.10
  374.2 5.6 %shard_map.415 = (bf16[384,512]{1,0:T(8,128)(2,1)}, bf16[128,512]{1,0:T(8,128)(2,1)}) custom-call(s32[5]{0:T(128)} %pad_add_fusion.refs_0_, bf16[512,1152]{1,0:T(8,128)(2,1)} %all-gather.5.cloned.1.call-done.refs_1_, bf16[128,1024]{1,0:T(8,128)(2,1)} %get-tuple-element.187.refs_2_, bf16[128,1024]{1,0:T(8,128)(2,1)} %copy-done.25, ...), custom_call_target="tpu_custom_call" | custom-call | tf_op jit(solution)/shard_map/pallas_call | solution.py:1196
  385.8 3.8 all-to-all-start.4
  389.7 1.4 fusion.39
  391.9 12.4 %all-to-all-done.4 = bf16[8,480,128]{2,1,0:T(8,128)(2,1)S(1)} async-done(((bf16[8,480,128]{2,1,0:T(8,128)(2,1)}), bf16[8,480,128]{2,1,0:T(8,128)(2,1)S(1)}, u32[]{:S(2)}, u32[]{:S(2)}) %all-to-all-start.4) | async-done | bytes 983072 | tf_op jit(solution)/shard_map/all_to_all | solution.py:1255
  412.2 1.2 fusion.42
  413.4 3.4 shard_map.414
  (239 shorter events, 39.1 us)
Async XLA Ops:
  7.2 19.2 %copy-start = (bf16[8,8,16,512]{3,2,1,0:T(8,128)(2,1)S(1)}, bf16[8,8,16,512]{3,2,1,0:T(8,128)(2,1)}, u32[]{:S(2)}) copy-start(bf16[8,8,16,512]{3,2,1,0:T(8,128)(2,1)} %param.44) | copy-start | bytes 3145732
  7.2 10.3 %copy-start.34 = (s32[128,2]{0,1:T(2,128)S(1)}, s32[128,2]{0,1:T(2,128)}, u32[]{:S(2)}) copy-start(s32[128,2]{0,1:T(2,128)} %param.59) | copy-start | bytes 3076
  7.2 10.9 %copy-start.4 = (bf16[128,2048]{1,0:T(8,128)(2,1)S(1)}, bf16[128,2048]{1,0:T(8,128)(2,1)}, u32[]{:S(2)}) copy-start(bf16[128,2048]{1,0:T(8,128)(2,1)} %cot.1) | copy-start | bytes 1572868
  7.2 47.3 %all-gather.3.cloned.1.call-start = ((), (), s32[]{:S(2)}) async-start(), calls=%async_computation.9 | async-start | bytes 1474560 | tf_op jit(solution)/shard_map/all_gather | solution.py:846
  10.6 9.1 %copy-start.11 = (bf16[128,896]{1,0:T(8,128)(2,1)}, bf16[128,896]{1,0:T(8,128)(2,1)S(1)}, u32[]{:S(2)}) copy-start(bf16[128,896]{1,0:T(8,128)(2,1)S(1)} %slice.140.refs_2_) | copy-start | bytes 688132
  10.6 36.9 %collective-permute-start.2 = (bf16[128,896]{1,0:T(8,128)(2,1)S(1)}, bf16[128,896]{1,0:T(8,128)(2,1)S(1)}, u32[]{:S(2)}, u32[]{:S(2)}) collective-permute-start(bf16[128,896]{1,0:T(8,128)(2,1)S(1)} %slice.140.refs_2_), channel_id=1, source_target_pairs={{0,3},{1,0},{2,1},{3,2},{4,7},{5,4},{6,5},{7,6},{8,11},{9,8},{10,9... | collective-permute-start | bytes 688136 | tf_op jit(solution)/shard_map/ppermute | solution.py:843
  15.7 32.6 %collective-permute-start.1 = (bf16[128,896]{1,0:T(8,128)(2,1)S(1)}, bf16[128,896]{1,0:T(8,128)(2,1)}, u32[]{:S(2)}, u32[]{:S(2)}) collective-permute-start(bf16[128,896]{1,0:T(8,128)(2,1)S(1)} %slice.140.refs_2_), channel_id=1, source_target_pairs={{0,2},{1,3},{2,0},{3,1},{4,6},{5,7},{6,4},{7,5},{8,10},{9,11},{10,... | collective-permute-start | bytes 688136 | tf_op jit(solution)/shard_map/ppermute | solution.py:843
  15.7 32.6 %collective-permute-start = (bf16[128,896]{1,0:T(8,128)(2,1)S(1)}, bf16[128,896]{1,0:T(8,128)(2,1)}, u32[]{:S(2)}, u32[]{:S(2)}) collective-permute-start(bf16[128,896]{1,0:T(8,128)(2,1)S(1)} %slice.140.refs_2_), channel_id=1, source_target_pairs={{0,1},{1,2},{2,3},{3,0},{4,5},{5,6},{6,7},{7,4},{8,9},{9,10},{10,1... | collective-permute-start | bytes 688136 | tf_op jit(solution)/shard_map/ppermute | solution.py:843
  17.9 71.2 %copy-start.6 = (s32[128,2]{1,0:T(8,128)}, s32[128,2]{1,0:T(8,128)S(1)}, u32[]{:S(2)}) copy-start(s32[128,2]{1,0:T(8,128)S(1)} %add.130.refs_5_.mcol) | copy-start | bytes 3076
  19.7 8.9 %copy-start.32 = (s32[512,2]{0,1:T(2,128)S(1)}, s32[512,2]{0,1:T(2,128)}, u32[]{:S(2)}) copy-start(s32[512,2]{0,1:T(2,128)} %param.58) | copy-start | bytes 12292
  19.7 28.6 %all-to-all-start = ((bf16[8,40,2048]{2,1,0:T(8,128)(2,1)}), bf16[8,40,2048]{2,1,0:T(8,128)(2,1)S(1)}, u32[]{:S(2)}, u32[]{:S(2)}) async-start(bf16[8,40,2048]{2,1,0:T(8,128)(2,1)} %bitcast.9), calls=%async_computation | async-start | bytes 2621440 | tf_op jit(solution)/shard_map/all_to_all | solution.py:902
  23.5 110.9 %reduce-scatter.5.cloned.1.call-start = ((), (), s32[]{:S(2)}) async-start(), calls=%async_computation.10 | async-start | bytes 2621440 | tf_op jit(solution)/shard_map/reduce_scatter | solution.py:966
  28.8 8.2 %copy-start.15 = (s32[512,2]{1,0:T(8,128)}, s32[512,2]{1,0:T(8,128)S(1)}, u32[]{:S(2)}) copy-start(s32[512,2]{1,0:T(8,128)S(1)} %copy.138.refs_16_.refs_17_) | copy-start | bytes 12292
  35.1 6.8 %copy-start.27 = (bf16[2048,8]{0,1:T(8,128)(2,1)S(1)}, bf16[2048,8]{0,1:T(8,128)(2,1)}, u32[]{:S(2)}) copy-start(bf16[2048,8]{0,1:T(8,128)(2,1)} %param.34) | copy-start | bytes 98308
  37.0 6.4 %copy-start.36 = (bf16[2048]{0:T(1024)(128)(2,1)S(1)}, bf16[2048]{0:T(1024)(128)(2,1)}, u32[]{:S(2)}) copy-start(bf16[2048]{0:T(1024)(128)(2,1)} %param.32) | copy-start | bytes 12292
  37.0 7.8 %copy-start.37 = (bf16[2048]{0:T(1024)(128)(2,1)S(1)}, bf16[2048]{0:T(1024)(128)(2,1)}, u32[]{:S(2)}) copy-start(bf16[2048]{0:T(1024)(128)(2,1)} %param.33) | copy-start | bytes 12292
  37.0 8.4 %copy-start.31 = (bf16[2048,8]{0,1:T(8,128)(2,1)S(1)}, bf16[2048,8]{0,1:T(8,128)(2,1)}, u32[]{:S(2)}) copy-start(bf16[2048,8]{0,1:T(8,128)(2,1)} %param.35) | copy-start | bytes 98308
  47.4 7.1 %copy-start.26 = (bf16[128,896]{1,0:T(8,128)(2,1)}, bf16[128,896]{1,0:T(8,128)(2,1)S(1)}, u32[]{:S(2)}) copy-start(bf16[128,896]{1,0:T(8,128)(2,1)S(1)} %collective-permute-done.2.refs_5_) | copy-start | bytes 688132
  48.3 40.8 %copy-start.10 = (bf16[8,40,2048]{2,1,0:T(8,128)(2,1)}, bf16[8,40,2048]{2,1,0:T(8,128)(2,1)S(1)}, u32[]{:S(2)}) copy-start(bf16[8,40,2048]{2,1,0:T(8,128)(2,1)S(1)} %all-to-all-done) | copy-start | bytes 3932164
  137.8 22.8 %all-to-all-start.1 = ((bf16[8,40,2176]{2,1,0:T(8,128)(2,1)}), bf16[8,40,2176]{2,1,0:T(8,128)(2,1)S(1)}, u32[]{:S(2)}, u32[]{:S(2)}) async-start(bf16[8,40,2176]{2,1,0:T(8,128)(2,1)} %bitcast.156), calls=%async_computation.2 | async-start | bytes 2785280 | tf_op jit(solution)/shard_map/all_to_all | solution.py:902
  141.4 130.2 %reduce-scatter.7.cloned.1.call-start = ((), (), s32[]{:S(2)}) async-start(), calls=%async_computation.11 | async-start | bytes 3440640 | tf_op jit(solution)/shard_map/reduce_scatter | solution.py:1070
  146.0 39.4 %collective-permute-start.5 = (bf16[128,1536]{1,0:T(8,128)(2,1)}, bf16[128,1536]{1,0:T(8,128)(2,1)S(1)}, u32[]{:S(2)}, u32[]{:S(2)}) collective-permute-start(bf16[128,1536]{1,0:T(8,128)(2,1)} %get-tuple-element.226), channel_id=1, source_target_pairs={{0,3},{1,0},{2,1},{3,2},{4,7},{5,4},{6,5},{7,6},{8,11},{9,8},{10,9... | collective-permute-start | bytes 1179656 | tf_op jit(solution)/shard_map/ppermute | solution.py:843
  148.1 37.3 %collective-permute-start.3 = (bf16[128,1536]{1,0:T(8,128)(2,1)}, bf16[128,1536]{1,0:T(8,128)(2,1)S(1)}, u32[]{:S(2)}, u32[]{:S(2)}) collective-permute-start(bf16[128,1536]{1,0:T(8,128)(2,1)} %get-tuple-element.227), channel_id=1, source_target_pairs={{0,1},{1,2},{2,3},{3,0},{4,5},{5,6},{6,7},{7,4},{8,9},{9,10},{10,1... | collective-permute-start | bytes 1179656 | tf_op jit(solution)/shard_map/ppermute | solution.py:843
  148.4 37.0 %collective-permute-start.4 = (bf16[128,1536]{1,0:T(8,128)(2,1)}, bf16[128,1536]{1,0:T(8,128)(2,1)S(1)}, u32[]{:S(2)}, u32[]{:S(2)}) collective-permute-start(bf16[128,1536]{1,0:T(8,128)(2,1)} %get-tuple-element.228), channel_id=1, source_target_pairs={{0,2},{1,3},{2,0},{3,1},{4,6},{5,7},{6,4},{7,5},{8,10},{9,11},{10,... | collective-permute-start | bytes 1179656 | tf_op jit(solution)/shard_map/ppermute | solution.py:843
  185.4 33.5 %copy-start.19 = (bf16[128,1536]{1,0:T(8,128)(2,1)}, bf16[128,1536]{1,0:T(8,128)(2,1)S(1)}, u32[]{:S(2)}) copy-start(bf16[128,1536]{1,0:T(8,128)(2,1)S(1)} %collective-permute-done.3) | copy-start | bytes 1179652
  185.4 33.4 %copy-start.17 = (bf16[128,1536]{1,0:T(8,128)(2,1)}, bf16[128,1536]{1,0:T(8,128)(2,1)S(1)}, u32[]{:S(2)}) copy-start(bf16[128,1536]{1,0:T(8,128)(2,1)S(1)} %collective-permute-done.4) | copy-start | bytes 1179652
  218.9 29.6 %all-to-all-start.2 = ((bf16[8,40,2176]{2,1,0:T(8,128)(2,1)}), bf16[8,40,2176]{2,1,0:T(8,128)(2,1)S(1)}, u32[]{:S(2)}, u32[]{:S(2)}) async-start(bf16[8,40,2176]{2,1,0:T(8,128)(2,1)} %bitcast.42), calls=%async_computation.3 | async-start | bytes 2785280 | tf_op jit(solution)/shard_map/all_to_all | solution.py:984
  248.5 23.2 %all-to-all-start.3 = ((bf16[8,40,2176]{2,1,0:T(8,128)(2,1)}), bf16[8,40,2176]{2,1,0:T(8,128)(2,1)S(1)}, u32[]{:S(2)}, u32[]{:S(2)}) async-start(bf16[8,40,2176]{2,1,0:T(8,128)(2,1)} %bitcast.158), calls=%async_computation.4 | async-start | bytes 2785280 | tf_op jit(solution)/shard_map/all_to_all | solution.py:984
  252.6 69.8 %all-gather.5.cloned.1.call-start = ((), (), s32[]{:S(2)}) async-start(), calls=%async_computation.12 | async-start | bytes 1474560 | tf_op jit(solution)/shard_map/all_gather | solution.py:846
  257.2 19.6 %copy-start.42 = (s32[4]{0:T(128)S(1)}, s32[4]{0:T(128)}, u32[]{:S(2)}) copy-start(s32[4]{0:T(128)} %compare_select_fusion.refs_0_) | copy-start | bytes 52
  257.2 20.2 %copy-start.33 = (s32[512,2]{0,1:T(2,128)S(1)}, s32[512,2]{0,1:T(2,128)}, u32[]{:S(2)}) copy-start(s32[512,2]{0,1:T(2,128)} %param.58) | copy-start | bytes 12292
  257.2 21.6 %copy-start.7 = (bf16[128,1536]{1,0:T(8,128)(2,1)S(1)}, bf16[128,1536]{1,0:T(8,128)(2,1)}, u32[]{:S(2)}) copy-start(bf16[128,1536]{1,0:T(8,128)(2,1)} %get-tuple-element.191) | copy-start | bytes 1179652
  272.8 6.1 %copy-start.20 = (bf16[128,1536]{1,0:T(8,128)(2,1)S(1)}, bf16[128,1536]{1,0:T(8,128)(2,1)}, u32[]{:S(2)}) copy-start(bf16[128,1536]{1,0:T(8,128)(2,1)} %copy-done.19) | copy-start | bytes 1179652
  272.8 10.0 %copy-start.18 = (bf16[128,1536]{1,0:T(8,128)(2,1)S(1)}, bf16[128,1536]{1,0:T(8,128)(2,1)}, u32[]{:S(2)}) copy-start(bf16[128,1536]{1,0:T(8,128)(2,1)} %copy-done.17) | copy-start | bytes 1179652
  276.7 87.8 %reduce-scatter.9.cloned.1.call-start = ((), (), s32[]{:S(2)}) async-start(), calls=%async_computation.13 | async-start | bytes 1966080 | tf_op jit(solution)/shard_map/reduce_scatter | solution.py:1070
  278.9 13.2 %collective-permute-start.8 = (bf16[128,1024]{1,0:T(8,128)(2,1)S(1)}, bf16[128,1024]{1,0:T(8,128)(2,1)S(1)}, u32[]{:S(2)}, u32[]{:S(2)}) collective-permute-start(bf16[128,1024]{1,0:T(8,128)(2,1)S(1)} %copy-done.22), channel_id=1, source_target_pairs={{0,3},{1,0},{2,1},{3,2},{4,7},{5,4},{6,5},{7,6},{8,11},{9,8},{10,9... | collective-permute-start | bytes 786440 | tf_op jit(solution)/shard_map/ppermute | solution.py:843
  280.9 39.1 %collective-permute-start.7 = (bf16[128,1024]{1,0:T(8,128)(2,1)S(1)}, bf16[128,1024]{1,0:T(8,128)(2,1)S(1)}, u32[]{:S(2)}, u32[]{:S(2)}) collective-permute-start(bf16[128,1024]{1,0:T(8,128)(2,1)S(1)} %copy-done.22), channel_id=1, source_target_pairs={{0,2},{1,3},{2,0},{3,1},{4,6},{5,7},{6,4},{7,5},{8,10},{9,11},{10,... | collective-permute-start | bytes 786440 | tf_op jit(solution)/shard_map/ppermute | solution.py:843
  281.0 39.1 %collective-permute-start.6 = (bf16[128,1024]{1,0:T(8,128)(2,1)S(1)}, bf16[128,1024]{1,0:T(8,128)(2,1)S(1)}, u32[]{:S(2)}, u32[]{:S(2)}) collective-permute-start(bf16[128,1024]{1,0:T(8,128)(2,1)S(1)} %copy-done.22), channel_id=1, source_target_pairs={{0,1},{1,2},{2,3},{3,0},{4,5},{5,6},{6,7},{7,4},{8,9},{9,10},{10,1... | collective-permute-start | bytes 786440 | tf_op jit(solution)/shard_map/ppermute | solution.py:843
  292.1 30.4 %copy-start.23 = (bf16[128,1024]{1,0:T(8,128)(2,1)}, bf16[128,1024]{1,0:T(8,128)(2,1)S(1)}, u32[]{:S(2)}) copy-start(bf16[128,1024]{1,0:T(8,128)(2,1)S(1)} %collective-permute-done.8.refs_5_) | copy-start | bytes 786436
  322.4 91.0 %reduce-scatter.11.cloned.1.call-start = ((), (), s32[]{:S(2)}) async-start(), calls=%async_computation.14 | async-start | bytes 2621440 | tf_op jit(solution)/shard_map/reduce_scatter | solution.py:1215
  364.5 5.9 %copy-start.28 = (bf16[128,512]{1,0:T(8,128)(2,1)S(1)}, bf16[128,512]{1,0:T(8,128)(2,1)}, u32[]{:S(2)}) copy-start(bf16[128,512]{1,0:T(8,128)(2,1)} %get-tuple-element.197) | copy-start | bytes 393220
  364.5 6.1 %collective-permute-start.11 = (bf16[272,128]{1,0:T(8,128)(2,1)}, bf16[272,128]{1,0:T(8,128)(2,1)S(1)}, u32[]{:S(2)}, u32[]{:S(2)}) collective-permute-start(bf16[272,128]{1,0:T(8,128)(2,1)} %get-tuple-element.177), channel_id=1, source_target_pairs={{0,3},{1,0},{2,1},{3,2},{4,7},{5,4},{6,5},{7,6},{8,11},{9,8},{10,9... | collective-permute-start | bytes 208904 | tf_op jit(solution)/shard_map/ppermute | solution.py:843
  365.9 8.3 %collective-permute-start.10 = (bf16[272,128]{1,0:T(8,128)(2,1)}, bf16[272,128]{1,0:T(8,128)(2,1)S(1)}, u32[]{:S(2)}, u32[]{:S(2)}) collective-permute-start(bf16[272,128]{1,0:T(8,128)(2,1)} %get-tuple-element.177), channel_id=1, source_target_pairs={{0,2},{1,3},{2,0},{3,1},{4,6},{5,7},{6,4},{7,5},{8,10},{9,11},{10,... | collective-permute-start | bytes 208904 | tf_op jit(solution)/shard_map/ppermute | solution.py:843
  367.2 7.0 %collective-permute-start.9 = (bf16[272,128]{1,0:T(8,128)(2,1)}, bf16[272,128]{1,0:T(8,128)(2,1)S(1)}, u32[]{:S(2)}, u32[]{:S(2)}) collective-permute-start(bf16[272,128]{1,0:T(8,128)(2,1)} %get-tuple-element.177), channel_id=1, source_target_pairs={{0,1},{1,2},{2,3},{3,0},{4,5},{5,6},{6,7},{7,4},{8,9},{9,10},{10,1... | collective-permute-start | bytes 208904 | tf_op jit(solution)/shard_map/ppermute | solution.py:843
  370.5 10.4 %copy-start.30 = (bf16[272,128]{1,0:T(8,128)(2,1)S(1)}, bf16[272,128]{1,0:T(8,128)(2,1)}, u32[]{:S(2)}) copy-start(bf16[272,128]{1,0:T(8,128)(2,1)} %get-tuple-element.177) | copy-start | bytes 208900
  374.2 6.8 %copy-start.5 = (bf16[512,512]{1,0:T(8,128)(2,1)S(1)}, bf16[512,512]{1,0:T(8,128)(2,1)}, u32[]{:S(2)}) copy-start(bf16[512,512]{1,0:T(8,128)(2,1)} %shard_map.412) | copy-start | bytes 1572868
  385.8 18.5 %all-to-all-start.4 = ((bf16[8,480,128]{2,1,0:T(8,128)(2,1)}), bf16[8,480,128]{2,1,0:T(8,128)(2,1)S(1)}, u32[]{:S(2)}, u32[]{:S(2)}) async-start(bf16[8,480,128]{2,1,0:T(8,128)(2,1)} %copy.164), calls=%async_computation.8 | async-start | bytes 1966080 | tf_op jit(solution)/shard_map/all_to_all | solution.py:1255
  389.7 14.5 %copy-start.41 = (s32[8]{0:T(128)S(1)}, s32[8]{0:T(128)}, u32[]{:S(2)}) copy-start(s32[8]{0:T(128)} %param.57) | copy-start | bytes 100
  (19 other events, 60.7 us)
Sparse Core Ops, SparseCore 0:
  17.6 36.9 all-gather.2
  89.3 45.1 reduce-scatter.4
  219.0 52.3 reduce-scatter.6
  276.8 45.5 all-gather.4
  324.7 34.8 reduce-scatter.8
  369.3 43.5 reduce-scatter.10

commit v5 on v4

--- a/solution.py
+++ b/solution.py
@@ -119,10 +119,12 @@
     return (iota(shape, 1) // RANK) == route
 
 
-def select_add(total, part, routes, expert):
-    s = part.shape[0]
+def select_add(total, parts, routes, expert):
+    s = parts[0].shape[0]
     for k in range(2):
-        total[k * s : (k + 1) * s, :] += jnp.where(routes[:, k : k + 1] == expert, part, 0.0)
+        route = routes[:, k : k + 1]
+        chosen = jnp.where(route == expert + 1, parts[1], 0.0)
+        total[k * s : (k + 1) * s, :] += jnp.where(route == expert, parts[0], chosen)
 
 
 def weight_stream(n, count, fetch):
@@ -181,18 +183,21 @@
     q, k, v, ga, low, misc, o, lse, qsum, og, chosen, wk, wv, load_sems, save_sems, wq, wo, wq_sems, wo_sems,
 ):
     step = pl.program_id(0)
+    phase = ATT_EXPERTS // 2
     s, width = k.shape
     loads = copies((wk_far, wv_far), (wk, wv), load_sems)
     width_d = wo.shape[3]
     prime_q, next_q = weight_stream(
         step,
-        ATT_EXPERTS,
+        phase,
         lambda n, slot: [
-            pltpu.make_async_copy(wq_far.at[n], wq.at[slot], wq_sems.at[slot]),
+            pltpu.make_async_copy(
+                wq_far.at[pl.ds(2 * n, 2)], wq.at[slot], wq_sems.at[slot]
+            ),
         ],
     )
     prime_o, next_o = weight_stream(
-        step - ATT_EXPERTS,
+        step - phase,
         D // width_d,
         lambda n, slot: [
             pltpu.make_async_copy(
@@ -227,12 +232,14 @@
             part = jnp.where(mine, low[...], jnp.zeros((), bf16))
             qsum[j * s : (j + 1) * s, :] = nn(part, bcat[...])
 
-    @pl.when(step < ATT_EXPERTS)
+    @pl.when(step < phase)
     def _():
         next_q()
-        select_add(qsum, nn(xn[...], wq[lax.rem(step, DEPTH)]), routes, step)
-
-    @pl.when(step == ATT_EXPERTS - 1)
+        slot = lax.rem(step, DEPTH)
+        parts = [nn(xn[...], wq[slot, j]) for j in range(2)]
+        select_add(qsum, parts, routes, 2 * step)
+
+    @pl.when(step == phase - 1)
     def _():
         prime_o()
         for load in loads:
@@ -256,10 +263,10 @@
         out_low[...] = total.astype(bf16)
         spread_rows(og, routes, chosen)
 
-    @pl.when(step >= ATT_EXPERTS)
+    @pl.when(step >= phase)
     def _():
         next_o()
-        weights = wo[lax.rem(step - ATT_EXPERTS, DEPTH)].reshape(chosen.shape[1], width_d)
+        weights = wo[lax.rem(step - phase, DEPTH)].reshape(chosen.shape[1], width_d)
         attn_out[...] = (nn(chosen[...], weights) + nn(out_low[...], ob[...])).astype(bf16)
 
     @pl.when(step == pl.num_programs(0) - 1)
@@ -621,17 +628,20 @@
     dzl, dosum, do, stats, dq, dk, dv, lows_dense, dk_sum, dv_sum, chosen, wo, wq, wo_sems, wq_sems,
 ):
     step = pl.program_id(0)
+    phase = ATT_EXPERTS // 2
     s, width = k.shape
     width_d = wq.shape[2]
     prime_o, next_o = weight_stream(
         step,
-        ATT_EXPERTS,
+        phase,
         lambda n, slot: [
-            pltpu.make_async_copy(wo_far.at[n], wo.at[slot], wo_sems.at[slot]),
+            pltpu.make_async_copy(
+                wo_far.at[pl.ds(2 * n, 2)], wo.at[slot], wo_sems.at[slot]
+            ),
         ],
     )
     prime_q, next_q = weight_stream(
-        step - ATT_EXPERTS,
+        step - phase,
         D // width_d,
         lambda n, slot: [
             pltpu.make_async_copy(
@@ -656,12 +666,14 @@
             part = jnp.where(mine, dzl[...], 0.0).astype(bf16)
             dosum[j * s : (j + 1) * s, :] = nn(part, oa[...])
 
-    @pl.when(step < ATT_EXPERTS)
+    @pl.when(step < phase)
     def _():
         next_o()
-        select_add(dosum, nt(da[...], wo[lax.rem(step, DEPTH)]), routes, step)
-
-    @pl.when(step == ATT_EXPERTS - 1)
+        slot = lax.rem(step, DEPTH)
+        parts = [nt(da[...], wo[slot, j]) for j in range(2)]
+        select_add(dosum, parts, routes, 2 * step)
+
+    @pl.when(step == phase - 1)
     def _():
         prime_q()
         for load in loads:
@@ -673,10 +685,10 @@
         )
         spread_rows(dq, routes, chosen)
 
-    @pl.when(step >= ATT_EXPERTS)
+    @pl.when(step >= phase)
     def _():
         next_q()
-        slot = lax.rem(step - ATT_EXPERTS, DEPTH)
+        slot = lax.rem(step - phase, DEPTH)
         total = (
             nn(lows_dense[:, 0:LOW], aq[...])
             + nn(lows_dense[:, LOW : 2 * LOW], amisc[...])
@@ -909,16 +921,17 @@
     grads_in = to_experts(nn(picked.astype(bf16), cotangent).astype(bf16))
     own_rows = lambda array: lax.dynamic_slice_in_dim(array, shard_at * rows, rows, 0)
     routes_own = own_rows(attn_routes)
+    owner_places = jnp.concatenate([places, jnp.full((1,), block, jnp.int32)])
     early_made = (router, router_first, gain1, gain2, mask, mrow, mcol, routes_own)
-    early_made += (gate_first, up_first, down_second)
+    early_made += (gate_first, up_first, down_second, owner_places)
     early_made, xn_parts, grads_in = lax.optimization_barrier((early_made, xn_parts, grads_in))
     router, router_first, gain1, gain2, mask, mrow, mcol, routes_own, *firsts = early_made
-    gate_first, up_first, down_second = firsts
-
-    column_parts = 8
+    gate_first, up_first, down_second, owner_places = firsts
+
+    column_parts = 4
     width_d = D // column_parts
-    steps_attn = ATT_EXPERTS + column_parts
-    late = lambda e: jnp.maximum(e - ATT_EXPERTS, 0)
+    steps_attn = ATT_EXPERTS // 2 + column_parts
+    late = lambda e: jnp.maximum(e - ATT_EXPERTS // 2, 0)
     column_block = pl.BlockSpec((LOW, width_d), lambda e: (0, late(e)))
     out_block = pl.BlockSpec((seq, width_d), lambda e: (0, late(e)))
     key_block = pl.BlockSpec((width_d, width), lambda e: (late(e), 0))
@@ -953,7 +966,7 @@
             pltpu.VMEM((D, width), bf16),
             pltpu.SemaphoreType.DMA((2,)),
             pltpu.SemaphoreType.DMA((8,)),
-            pltpu.VMEM((DEPTH, D, width), bf16),
+            pltpu.VMEM((DEPTH, 2, D, width), bf16),
             pltpu.VMEM((DEPTH, ATT_EXPERTS, width, width_d), bf16),
             pltpu.SemaphoreType.DMA((DEPTH,)),
             pltpu.SemaphoreType.DMA((DEPTH,)),
@@ -1030,7 +1043,7 @@
         2 * weight_moved,
     )(rows_in, mask, gate_first, up_first, gate_w, up_w, gate_table, up_table)
 
-    g, *arrived = lax.optimization_barrier((g, *arrived))
+    g, ga_own, *arrived = lax.optimization_barrier((g, own_rows(ga), *arrived))
     arrived = jnp.concatenate(arrived, axis=0)
     mlp_columns = arrived[:, : 2 * own]
     out_lows = jnp.sum(
@@ -1123,7 +1136,6 @@
     )(dm_back, dlm, low_down, attn, tokens, cotangent, gain2, router, mcol, mlp_routes)
 
     da_parts = gathered(da_left, da_right)
-    owner_places = jnp.concatenate([places, jnp.full((1,), block, jnp.int32)])
     xn_own = call(
         lambda *refs: own_columns_kernel(shards, *refs),
         (),
@@ -1176,7 +1188,7 @@
             pltpu.VMEM((seq, HD), f32),
             pltpu.VMEM((seq, HD), f32),
             pltpu.VMEM((seq, ATT_EXPERTS * width), bf16),
-            pltpu.VMEM((DEPTH, width, D), bf16),
+            pltpu.VMEM((DEPTH, 2, width, D), bf16),
             pltpu.VMEM((DEPTH, ATT_EXPERTS, width_d, width), bf16),
             pltpu.SemaphoreType.DMA((DEPTH,)),
             pltpu.SemaphoreType.DMA((DEPTH,)),
@@ -1190,9 +1202,7 @@
     dx_part, lows, grad_oa, grad_qb, grad_kv, *held = lax.optimization_barrier(held)
     da_parts, tables_sum = held[: shards + 1], held[shards + 1 :]
     lows_parts = [lows] + [shifted(lows, step) for step in range(1, shards)]
-    chain = (*lows_parts, *da_parts)
-    chain = lax.optimization_barrier(chain)
-    lows_parts, da_parts = chain[:shards], chain[shards:]
+    lows_parts[1], *da_parts = lax.optimization_barrier((lows_parts[1], *da_parts))
     factors, grad_ob_own = call(
         lambda *refs: owner_kernel(shards, *refs),
         (),
@@ -1223,7 +1233,7 @@
         [],
         2 * rows * LOW * D,
         24 * rows * D,
-    )(dx, own_rows(slopes), own_rows(ga), tokens, gain1, router_first, dh1, routes_own)
+    )(dx, own_rows(slopes), ga_own, tokens, gain1, router_first, dh1, routes_own)
 
     lane = jnp.arange(LOW, dtype=jnp.int32)
     dense = jnp.zeros((seq, LOW), f32)

time: 428 us -> 426 us (level)
  transfers between devices with their start and end apart: 23 -> 23, of which waited for: 10 -> 11; matrix products, arithmetic and copies ran while one was open for 12% -> 12% of each run, Pallas kernels for 25% -> 25%
where the time goes in v5:
time: 426 us; the launch traced here: 421 us
  Pallas kernels  181 us (42%)
  waiting for transfers between devices  125 us (29%)
  local copies, waits for them, and re-layouts  45.3 us (11%)
  starting transfers between devices  39.3 us (9%)
  between operations  17.4 us (4%)
  other arithmetic  10.2 us (2%)
    reduce_scatter x1, waiting for transfers between devices, on_device(): attn = lax.psum_scatter(attn_part, 'shard', scatter_dimension=0, tiled=True)  44.7 us
    pallas_call x1, Pallas kernels, on_device(): call(lambda *refs: attention_back_kernel(shards, *refs), (steps_attn,), [...  40.7 us
    pallas_call x1, Pallas kernels, on_device(): call(expert_down_kernel, (steps,), [whole()] * 6 + [kept, kept, far, tabl...  33.5 us
    ppermute x12, waiting for transfers between devices, shifted(): return lax.ppermute(part, 'shard', pairs) if step else part  33.4 us
    pallas_call x1, Pallas kernels, on_device(): call(lambda *refs: attention_kernel(shards, *refs), (steps_attn,), [pl.Bl...  33.4 us
    pallas_call x1, Pallas kernels, on_device(): call(expert_rows_kernel, (parts,), [far, far, whole(), whole(), far, far,...  26 us
    pallas_call x1, Pallas kernels, on_device(): call(expert_up_kernel, (steps,), [whole()] * 4 + [far, far, table, table]...  23.8 us
    ppermute x12, starting transfers between devices, shifted(): return lax.ppermute(part, 'shard', pairs) if step else part  18.6 us
  transfers between devices with their start and end apart: 23, of which 11 were waited for; matrix products, arithmetic and copies ran while one was open for 12% of the time, Pallas kernels for 25%

profile of v5, /device:TPU:0, one launch (start us, length us, event | category | flops | bytes accessed | tf_op | source)
XLA Modules:
  0.0 421.2 jit_solution(15113895183919912303)
XLA Ops:
  7.3 1.3 fusion.2
  9.3 1.2 fusion.4
  10.6 5.1 %collective-permute-start.2 = (bf16[128,896]{1,0:T(8,128)(2,1)S(1)}, bf16[128,896]{1,0:T(8,128)(2,1)S(1)}, u32[]{:S(2)}, u32[]{:S(2)}) collective-permute-start(bf16[128,896]{1,0:T(8,128)(2,1)S(1)} %slice.140.refs_2_), channel_id=1, source_target_pairs={{0,3},{1,0},{2,1},{3,2},{4,7},{5,4},{6,5},{7,6},{8,11},{9,8},{10,9... | collective-permute-start | bytes 688136 | tf_op jit(solution)/shard_map/ppermute | solution.py:855
  18.1 1.6 convolution_convert_fusion
  19.7 3.9 all-to-all-start
  27.1 1.6 constant_dynamic-slice_fusion.2
  28.8 2.0 constant_dynamic-slice_fusion.4
  34.0 1.3 dynamic-slice_bitcast_fusion.2
  36.5 1.9 constant_dynamic-slice_fusion.5
  38.4 1.9 constant_dynamic-slice_fusion.6
  40.3 2.3 constant_dynamic-slice_fusion.7
  48.3 6.2 %all-gather.3.cloned.1.call-done.refs_1_ = bf16[512,1152]{1,0:T(8,128)(2,1)} async-done(((bf16[128,1152]{1,0:T(8,128)(2,1)}), bf16[512,1152]{1,0:T(8,128)(2,1)}) %all-gather.3.cloned.1.call-update) | async-done | bytes 1179664 | tf_op jit(solution)/shard_map/all_gather | solution.py:858
  54.6 33.4 %shard_map.405 = (bf16[512,2048]{1,0:T(8,128)(2,1)}, bf16[512,128]{1,0:T(8,128)(2,1)}, bf16[1024,512]{1,0:T(8,128)(2,1)}, bf16[512,512]{1,0:T(8,128)(2,1)}, bf16...) custom-call(s32[4]{0:T(128)} %copy-done.42, ...), custom_call_target="tpu_custom_call" | custom-call | flops 68719476736 | bytes 134217728 | tf_op jit(solution)/shard_map/pallas_call | solution.py:945
  88.6 44.7 %reduce-scatter.5.cloned.1.call-done.refs_0_.refs_1_.attn = bf16[128,2048]{1,0:T(8,128)(2,1)} async-done(((bf16[512,2048]{1,0:T(8,128)(2,1)}), bf16[128,2048]{1,0:T(8,128)(2,1)}) %reduce-scatter.5.cloned.1.call-update) | async-done | bytes 524304 | tf_op jit(solution)/shard_map/reduce_scatter | solution.py:979
  133.3 3.3 shard_map.406
  136.6 3.7 all-to-all-start.1
  142.6 1.5 constant_dynamic-slice_fusion.1.ga
  145.3 1.2 pad_maximum_fusion
  146.5 1.6 collective-permute-start.5
  148.5 1.7 collective-permute-start.4
  150.3 9.1 %all-to-all-done.1 = bf16[8,40,2176]{2,1,0:T(8,128)(2,1)S(1)} async-done(((bf16[8,40,2176]{2,1,0:T(8,128)(2,1)}), bf16[8,40,2176]{2,1,0:T(8,128)(2,1)S(1)}, u32[]{:S(2)}, u32[]{:S(2)}) %all-to-all-start.1) | async-done | bytes 1392672 | tf_op jit(solution)/shard_map/all_to_all | solution.py:914
  159.3 1.1 copy-done.8
  160.4 23.8 %shard_map.407 = (bf16[320,5632]{1,0:T(8,128)(2,1)}, bf16[320,5632]{1,0:T(8,128)(2,1)}, bf16[320,128]{1,0:T(8,128)(2,1)}, bf16[320,128]{1,0:T(8,128)(2,1)}) custom-call(bf16[320,2176]{1,0:T(8,128)(2,1)} %bitcast.154, bf16[320,128]{1,0:T(8,128)(2,1)} %compare_convert_fusion.mask, bf16[128,2048]{1,0:T(8,128)(2,1)} %bitcast.172, bf16[128,2048]{1,0:T(8,128)(2,1)} %bitcast.170, ...), custom_call_target="tpu_custom_call" | custom-call | flops 59055800320 | bytes 184549376 | tf_op jit(solution)/shard_map/pallas_call | solution.py:1031
  184.3 33.5 %shard_map.408 = (bf16[320,2176]{1,0:T(8,128)(2,1)}, bf16[320,5632]{1,0:T(8,128)(2,1)}, bf16[320,5632]{1,0:T(8,128)(2,1)}, bf16[320,128]{1,0:T(8,128)(2,1)}, bf1...) custom-call(bf16[320,2048]{1,0:T(8,128)(2,1)} %bitcast.159, ...), custom_call_target="tpu_custom_call" | custom-call | flops 59055800320 | bytes 92274688 | tf_op jit(solution)/shard_map/pallas_call | solution.py:1059
  217.9 4.0 all-to-all-start.2
  221.9 26.0 %shard_map.410 = bf16[320,2176]{1,0:T(8,128)(2,1)} custom-call(bf16[320,5632]{1,0:T(8,128)(2,1)} %get-tuple-element.135.dg_far, bf16[320,5632]{1,0:T(8,128)(2,1)} %get-tuple-element.136.du_far, bf16[320,128]{1,0:T(8,128)(2,1)} %get-tuple-element.137.dlg, bf16[320,128]{1,0:T(8,128)(2,1)} %get-tuple-element.138.dlu, bf16[2048,5632]{1,0:T(8,128)(2,1)} %gate_far.3, ...), custom_call_target="tpu_custom_call" | custom-call | flops 59055800320 | bytes 184549376 | tf_op jit(solution)/shard_map/pallas_call | solution.py:1091
  247.9 4.1 all-to-all-start.3
  252.8 3.8 shard_map.409
  256.6 14.5 %all-to-all-done.3 = bf16[8,40,2176]{2,1,0:T(8,128)(2,1)S(1)} async-done(((bf16[8,40,2176]{2,1,0:T(8,128)(2,1)}), bf16[8,40,2176]{2,1,0:T(8,128)(2,1)S(1)}, u32[]{:S(2)}, u32[]{:S(2)}) %all-to-all-start.3) | async-done | bytes 1392672 | tf_op jit(solution)/shard_map/all_to_all | solution.py:997
  272.2 3.9 shard_map.411
  276.3 2.3 collective-permute-start.8
  278.6 1.7 collective-permute-start.6
  280.4 1.2 slice.147.refs_7_
  282.7 4.0 shard_map.412
  286.7 1.2 collective-permute-done.8.refs_5_
  287.9 28.7 %collective-permute-done.7.refs_4_ = bf16[128,1024]{1,0:T(8,128)(2,1)S(1)} collective-permute-done((bf16[128,1024]{1,0:T(8,128)(2,1)}, bf16[128,1024]{1,0:T(8,128)(2,1)S(1)}, u32[]{:S(2)}, u32[]{:S(2)}) %collective-permute-start.7) | collective-permute-done | bytes 262176 | tf_op jit(solution)/shard_map/ppermute | solution.py:855
  316.6 4.0 all-gather.5.cloned.1.call-done.refs_1_
  320.7 40.7 %shard_map.413 = (bf16[512,2048]{1,0:T(8,128)(2,1)}, bf16[272,128]{1,0:T(8,128)(2,1)}, bf16[128,512]{1,0:T(8,128)(2,1)}, bf16[128,512]{1,0:T(8,128)(2,1)}, bf16[256,512]{1,0:T(8,128)(2,1)}) custom-call(s32[4]{0:T(128)} %copy-done.42, bf16[512,1152]{1,0:T(8,128)(2,1)} %all-gather.5.cloned.1.call-done.refs_1_, bf16[128,1024]{1,0:T(8,128)(2,1)} %get-tuple-element.185.refs_2_, ...), custom_call_target="tpu_custom_call" | custom-call | flops 68719476736 | bytes 134217728 | tf_op jit(solution)/shard_map/pallas_call | solution.py:1154
  362.5 2.2 collective-permute-start.10
  364.6 1.6 collective-permute-start.9
  367.6 3.4 collective-permute-done.9
  371.0 5.4 %shard_map.415 = (bf16[384,512]{1,0:T(8,128)(2,1)}, bf16[128,512]{1,0:T(8,128)(2,1)}) custom-call(s32[5]{0:T(128)} %pad_add_fusion.refs_0_, bf16[512,1152]{1,0:T(8,128)(2,1)} %all-gather.5.cloned.1.call-done.refs_1_, bf16[128,1024]{1,0:T(8,128)(2,1)} %get-tuple-element.185.refs_2_, bf16[128,1024]{1,0:T(8,128)(2,1)} %copy-done.24, ...), custom_call_target="tpu_custom_call" | custom-call | tf_op jit(solution)/shard_map/pallas_call | solution.py:1206
  381.2 1.1 copy.164
  382.3 4.6 %all-to-all-start.4 = ((bf16[8,480,128]{2,1,0:T(8,128)(2,1)}), bf16[8,480,128]{2,1,0:T(8,128)(2,1)S(1)}, u32[]{:S(2)}, u32[]{:S(2)}) async-start(bf16[8,480,128]{2,1,0:T(8,128)(2,1)} %copy.164), calls=%async_computation.8 | async-start | bytes 1966080 | tf_op jit(solution)/shard_map/all_to_all | solution.py:1265
  387.1 1.4 fusion.39
  389.3 12.4 %all-to-all-done.4 = bf16[8,480,128]{2,1,0:T(8,128)(2,1)S(1)} async-done(((bf16[8,480,128]{2,1,0:T(8,128)(2,1)}), bf16[8,480,128]{2,1,0:T(8,128)(2,1)S(1)}, u32[]{:S(2)}, u32[]{:S(2)}) %all-to-all-start.4) | async-done | bytes 983072 | tf_op jit(solution)/shard_map/all_to_all | solution.py:1265
  409.6 1.2 fusion.42
  410.8 3.4 shard_map.414
  (239 shorter events, 38.4 us)
Async XLA Ops:
  7.2 19.2 %copy-start = (bf16[8,8,16,512]{3,2,1,0:T(8,128)(2,1)S(1)}, bf16[8,8,16,512]{3,2,1,0:T(8,128)(2,1)}, u32[]{:S(2)}) copy-start(bf16[8,8,16,512]{3,2,1,0:T(8,128)(2,1)} %param.44) | copy-start | bytes 3145732
  7.2 10.3 %copy-start.34 = (s32[128,2]{0,1:T(2,128)S(1)}, s32[128,2]{0,1:T(2,128)}, u32[]{:S(2)}) copy-start(s32[128,2]{0,1:T(2,128)} %param.59) | copy-start | bytes 3076
  7.2 10.9 %copy-start.4 = (bf16[128,2048]{1,0:T(8,128)(2,1)S(1)}, bf16[128,2048]{1,0:T(8,128)(2,1)}, u32[]{:S(2)}) copy-start(bf16[128,2048]{1,0:T(8,128)(2,1)} %cot.1) | copy-start | bytes 1572868
  7.2 47.3 %all-gather.3.cloned.1.call-start = ((), (), s32[]{:S(2)}) async-start(), calls=%async_computation.9 | async-start | bytes 1474560 | tf_op jit(solution)/shard_map/all_gather | solution.py:858
  10.6 9.1 %copy-start.11 = (bf16[128,896]{1,0:T(8,128)(2,1)}, bf16[128,896]{1,0:T(8,128)(2,1)S(1)}, u32[]{:S(2)}) copy-start(bf16[128,896]{1,0:T(8,128)(2,1)S(1)} %slice.140.refs_2_) | copy-start | bytes 688132
  10.6 37.6 %collective-permute-start.2 = (bf16[128,896]{1,0:T(8,128)(2,1)S(1)}, bf16[128,896]{1,0:T(8,128)(2,1)S(1)}, u32[]{:S(2)}, u32[]{:S(2)}) collective-permute-start(bf16[128,896]{1,0:T(8,128)(2,1)S(1)} %slice.140.refs_2_), channel_id=1, source_target_pairs={{0,3},{1,0},{2,1},{3,2},{4,7},{5,4},{6,5},{7,6},{8,11},{9,8},{10,9... | collective-permute-start | bytes 688136 | tf_op jit(solution)/shard_map/ppermute | solution.py:855
  15.7 32.7 %collective-permute-start.1 = (bf16[128,896]{1,0:T(8,128)(2,1)S(1)}, bf16[128,896]{1,0:T(8,128)(2,1)}, u32[]{:S(2)}, u32[]{:S(2)}) collective-permute-start(bf16[128,896]{1,0:T(8,128)(2,1)S(1)} %slice.140.refs_2_), channel_id=1, source_target_pairs={{0,2},{1,3},{2,0},{3,1},{4,6},{5,7},{6,4},{7,5},{8,10},{9,11},{10,... | collective-permute-start | bytes 688136 | tf_op jit(solution)/shard_map/ppermute | solution.py:855
  15.7 32.7 %collective-permute-start = (bf16[128,896]{1,0:T(8,128)(2,1)S(1)}, bf16[128,896]{1,0:T(8,128)(2,1)}, u32[]{:S(2)}, u32[]{:S(2)}) collective-permute-start(bf16[128,896]{1,0:T(8,128)(2,1)S(1)} %slice.140.refs_2_), channel_id=1, source_target_pairs={{0,1},{1,2},{2,3},{3,0},{4,5},{5,6},{6,7},{7,4},{8,9},{9,10},{10,1... | collective-permute-start | bytes 688136 | tf_op jit(solution)/shard_map/ppermute | solution.py:855
  17.9 70.0 %copy-start.6 = (s32[128,2]{1,0:T(8,128)}, s32[128,2]{1,0:T(8,128)S(1)}, u32[]{:S(2)}) copy-start(s32[128,2]{1,0:T(8,128)S(1)} %add.130.refs_5_.mcol) | copy-start | bytes 3076
  19.7 8.9 %copy-start.32 = (s32[512,2]{0,1:T(2,128)S(1)}, s32[512,2]{0,1:T(2,128)}, u32[]{:S(2)}) copy-start(s32[512,2]{0,1:T(2,128)} %param.58) | copy-start | bytes 12292
  19.7 28.7 %all-to-all-start = ((bf16[8,40,2048]{2,1,0:T(8,128)(2,1)}), bf16[8,40,2048]{2,1,0:T(8,128)(2,1)S(1)}, u32[]{:S(2)}, u32[]{:S(2)}) async-start(bf16[8,40,2048]{2,1,0:T(8,128)(2,1)} %bitcast.9), calls=%async_computation | async-start | bytes 2621440 | tf_op jit(solution)/shard_map/all_to_all | solution.py:914
  23.5 109.7 %reduce-scatter.5.cloned.1.call-start = ((), (), s32[]{:S(2)}) async-start(), calls=%async_computation.10 | async-start | bytes 2621440 | tf_op jit(solution)/shard_map/reduce_scatter | solution.py:979
  28.8 9.6 %copy-start.15 = (s32[512,2]{1,0:T(8,128)}, s32[512,2]{1,0:T(8,128)S(1)}, u32[]{:S(2)}) copy-start(s32[512,2]{1,0:T(8,128)S(1)} %copy.138.refs_16_.refs_17_) | copy-start | bytes 12292
  36.5 6.1 %copy-start.26 = (bf16[2048,8]{0,1:T(8,128)(2,1)S(1)}, bf16[2048,8]{0,1:T(8,128)(2,1)}, u32[]{:S(2)}) copy-start(bf16[2048,8]{0,1:T(8,128)(2,1)} %param.34) | copy-start | bytes 98308
  38.4 5.8 %copy-start.36 = (bf16[2048]{0:T(1024)(128)(2,1)S(1)}, bf16[2048]{0:T(1024)(128)(2,1)}, u32[]{:S(2)}) copy-start(bf16[2048]{0:T(1024)(128)(2,1)} %param.32) | copy-start | bytes 12292
  38.4 7.1 %copy-start.37 = (bf16[2048]{0:T(1024)(128)(2,1)S(1)}, bf16[2048]{0:T(1024)(128)(2,1)}, u32[]{:S(2)}) copy-start(bf16[2048]{0:T(1024)(128)(2,1)} %param.33) | copy-start | bytes 12292
  38.4 7.7 %copy-start.31 = (bf16[2048,8]{0,1:T(8,128)(2,1)S(1)}, bf16[2048,8]{0,1:T(8,128)(2,1)}, u32[]{:S(2)}) copy-start(bf16[2048,8]{0,1:T(8,128)(2,1)} %param.35) | copy-start | bytes 98308
  38.4 8.4 %copy-start.30 = (bf16[16,512]{1,0:T(8,128)(2,1)S(1)}, bf16[16,512]{1,0:T(8,128)(2,1)}, u32[]{:S(2)}) copy-start(bf16[16,512]{1,0:T(8,128)(2,1)} %get-tuple-element.242) | copy-start | bytes 49156
  40.3 14.3 %copy-start.42 = (s32[4]{0:T(128)}, s32[4]{0:T(128)S(1)}, u32[]{:S(2)}) copy-start(s32[4]{0:T(128)S(1)} %compare_select_fusion.refs_0_) | copy-start | bytes 52
  48.2 6.4 %copy-start.25 = (bf16[128,896]{1,0:T(8,128)(2,1)}, bf16[128,896]{1,0:T(8,128)(2,1)S(1)}, u32[]{:S(2)}) copy-start(bf16[128,896]{1,0:T(8,128)(2,1)S(1)} %collective-permute-done.2.refs_5_) | copy-start | bytes 688132
  48.3 39.6 %copy-start.10 = (bf16[8,40,2048]{2,1,0:T(8,128)(2,1)}, bf16[8,40,2048]{2,1,0:T(8,128)(2,1)S(1)}, u32[]{:S(2)}) copy-start(bf16[8,40,2048]{2,1,0:T(8,128)(2,1)S(1)} %all-to-all-done) | copy-start | bytes 3932164
  136.6 22.8 %all-to-all-start.1 = ((bf16[8,40,2176]{2,1,0:T(8,128)(2,1)}), bf16[8,40,2176]{2,1,0:T(8,128)(2,1)S(1)}, u32[]{:S(2)}, u32[]{:S(2)}) async-start(bf16[8,40,2176]{2,1,0:T(8,128)(2,1)} %bitcast.156), calls=%async_computation.2 | async-start | bytes 2785280 | tf_op jit(solution)/shard_map/all_to_all | solution.py:914
  140.2 131.3 %reduce-scatter.7.cloned.1.call-start = ((), (), s32[]{:S(2)}) async-start(), calls=%async_computation.11 | async-start | bytes 3440640 | tf_op jit(solution)/shard_map/reduce_scatter | solution.py:1083
  146.5 37.7 %collective-permute-start.5 = (bf16[128,1536]{1,0:T(8,128)(2,1)}, bf16[128,1536]{1,0:T(8,128)(2,1)S(1)}, u32[]{:S(2)}, u32[]{:S(2)}) collective-permute-start(bf16[128,1536]{1,0:T(8,128)(2,1)} %get-tuple-element.224), channel_id=1, source_target_pairs={{0,3},{1,0},{2,1},{3,2},{4,7},{5,4},{6,5},{7,6},{8,11},{9,8},{10,9... | collective-permute-start | bytes 1179656 | tf_op jit(solution)/shard_map/ppermute | solution.py:855
  148.1 36.1 %collective-permute-start.3 = (bf16[128,1536]{1,0:T(8,128)(2,1)}, bf16[128,1536]{1,0:T(8,128)(2,1)S(1)}, u32[]{:S(2)}, u32[]{:S(2)}) collective-permute-start(bf16[128,1536]{1,0:T(8,128)(2,1)} %get-tuple-element.225), channel_id=1, source_target_pairs={{0,1},{1,2},{2,3},{3,0},{4,5},{5,6},{6,7},{7,4},{8,9},{9,10},{10,1... | collective-permute-start | bytes 1179656 | tf_op jit(solution)/shard_map/ppermute | solution.py:855
  148.5 35.7 %collective-permute-start.4 = (bf16[128,1536]{1,0:T(8,128)(2,1)}, bf16[128,1536]{1,0:T(8,128)(2,1)S(1)}, u32[]{:S(2)}, u32[]{:S(2)}) collective-permute-start(bf16[128,1536]{1,0:T(8,128)(2,1)} %get-tuple-element.226), channel_id=1, source_target_pairs={{0,2},{1,3},{2,0},{3,1},{4,6},{5,7},{6,4},{7,5},{8,10},{9,11},{10,... | collective-permute-start | bytes 1179656 | tf_op jit(solution)/shard_map/ppermute | solution.py:855
  184.2 33.6 %copy-start.19 = (bf16[128,1536]{1,0:T(8,128)(2,1)}, bf16[128,1536]{1,0:T(8,128)(2,1)S(1)}, u32[]{:S(2)}) copy-start(bf16[128,1536]{1,0:T(8,128)(2,1)S(1)} %collective-permute-done.3) | copy-start | bytes 1179652
  184.3 33.6 %copy-start.17 = (bf16[128,1536]{1,0:T(8,128)(2,1)}, bf16[128,1536]{1,0:T(8,128)(2,1)S(1)}, u32[]{:S(2)}) copy-start(bf16[128,1536]{1,0:T(8,128)(2,1)S(1)} %collective-permute-done.4) | copy-start | bytes 1179652
  217.9 30.0 %all-to-all-start.2 = ((bf16[8,40,2176]{2,1,0:T(8,128)(2,1)}), bf16[8,40,2176]{2,1,0:T(8,128)(2,1)S(1)}, u32[]{:S(2)}, u32[]{:S(2)}) async-start(bf16[8,40,2176]{2,1,0:T(8,128)(2,1)} %bitcast.42), calls=%async_computation.3 | async-start | bytes 2785280 | tf_op jit(solution)/shard_map/all_to_all | solution.py:997
  247.9 23.2 %all-to-all-start.3 = ((bf16[8,40,2176]{2,1,0:T(8,128)(2,1)}), bf16[8,40,2176]{2,1,0:T(8,128)(2,1)S(1)}, u32[]{:S(2)}, u32[]{:S(2)}) async-start(bf16[8,40,2176]{2,1,0:T(8,128)(2,1)} %bitcast.158), calls=%async_computation.4 | async-start | bytes 2785280 | tf_op jit(solution)/shard_map/all_to_all | solution.py:997
  252.0 68.6 %all-gather.5.cloned.1.call-start = ((), (), s32[]{:S(2)}) async-start(), calls=%async_computation.12 | async-start | bytes 1474560 | tf_op jit(solution)/shard_map/all_gather | solution.py:858
  256.6 19.6 %copy-start.33 = (s32[512,2]{0,1:T(2,128)S(1)}, s32[512,2]{0,1:T(2,128)}, u32[]{:S(2)}) copy-start(s32[512,2]{0,1:T(2,128)} %param.58) | copy-start | bytes 12292
  256.6 19.6 %copy-start.7 = (bf16[128,1536]{1,0:T(8,128)(2,1)S(1)}, bf16[128,1536]{1,0:T(8,128)(2,1)}, u32[]{:S(2)}) copy-start(bf16[128,1536]{1,0:T(8,128)(2,1)} %get-tuple-element.189) | copy-start | bytes 1179652
  272.2 8.1 %copy-start.18 = (bf16[128,1536]{1,0:T(8,128)(2,1)S(1)}, bf16[128,1536]{1,0:T(8,128)(2,1)}, u32[]{:S(2)}) copy-start(bf16[128,1536]{1,0:T(8,128)(2,1)} %copy-done.17) | copy-start | bytes 1179652
  276.1 85.4 %reduce-scatter.9.cloned.1.call-start = ((), (), s32[]{:S(2)}) async-start(), calls=%async_computation.13 | async-start | bytes 1966080 | tf_op jit(solution)/shard_map/reduce_scatter | solution.py:1083
  276.3 11.6 %collective-permute-start.8 = (bf16[128,1024]{1,0:T(8,128)(2,1)}, bf16[128,1024]{1,0:T(8,128)(2,1)S(1)}, u32[]{:S(2)}, u32[]{:S(2)}) collective-permute-start(bf16[128,1024]{1,0:T(8,128)(2,1)} %get-tuple-element.185.refs_2_), channel_id=1, source_target_pairs={{0,3},{1,0},{2,1},{3,2},{4,7},{5,4},{6,5},{7,6},{8,11},{9,8},{10,9... | collective-permute-start | bytes 786440 | tf_op jit(solution)/shard_map/ppermute | solution.py:855
  278.6 38.0 %collective-permute-start.7 = (bf16[128,1024]{1,0:T(8,128)(2,1)}, bf16[128,1024]{1,0:T(8,128)(2,1)S(1)}, u32[]{:S(2)}, u32[]{:S(2)}) collective-permute-start(bf16[128,1024]{1,0:T(8,128)(2,1)} %get-tuple-element.185.refs_2_), channel_id=1, source_target_pairs={{0,2},{1,3},{2,0},{3,1},{4,6},{5,7},{6,4},{7,5},{8,10},{9,11},{10,... | collective-permute-start | bytes 786440 | tf_op jit(solution)/shard_map/ppermute | solution.py:855
  278.6 38.0 %collective-permute-start.6 = (bf16[128,1024]{1,0:T(8,128)(2,1)}, bf16[128,1024]{1,0:T(8,128)(2,1)S(1)}, u32[]{:S(2)}, u32[]{:S(2)}) collective-permute-start(bf16[128,1024]{1,0:T(8,128)(2,1)} %get-tuple-element.185.refs_2_), channel_id=1, source_target_pairs={{0,1},{1,2},{2,3},{3,0},{4,5},{5,6},{6,7},{7,4},{8,9},{9,10},{10,1... | collective-permute-start | bytes 786440 | tf_op jit(solution)/shard_map/ppermute | solution.py:855
  287.9 32.8 %copy-start.22 = (bf16[128,1024]{1,0:T(8,128)(2,1)}, bf16[128,1024]{1,0:T(8,128)(2,1)S(1)}, u32[]{:S(2)}) copy-start(bf16[128,1024]{1,0:T(8,128)(2,1)S(1)} %collective-permute-done.8.refs_5_) | copy-start | bytes 786436
  320.7 90.1 %reduce-scatter.11.cloned.1.call-start = ((), (), s32[]{:S(2)}) async-start(), calls=%async_computation.14 | async-start | bytes 2621440 | tf_op jit(solution)/shard_map/reduce_scatter | solution.py:1225
  361.5 5.8 %copy-start.27 = (bf16[128,512]{1,0:T(8,128)(2,1)S(1)}, bf16[128,512]{1,0:T(8,128)(2,1)}, u32[]{:S(2)}) copy-start(bf16[128,512]{1,0:T(8,128)(2,1)} %get-tuple-element.195) | copy-start | bytes 393220
  361.5 15.9 %collective-permute-start.11 = (bf16[272,128]{1,0:T(8,128)(2,1)}, bf16[272,128]{1,0:T(8,128)(2,1)S(1)}, u32[]{:S(2)}, u32[]{:S(2)}) collective-permute-start(bf16[272,128]{1,0:T(8,128)(2,1)} %get-tuple-element.171), channel_id=1, source_target_pairs={{0,3},{1,0},{2,1},{3,2},{4,7},{5,4},{6,5},{7,6},{8,11},{9,8},{10,9... | collective-permute-start | bytes 208904 | tf_op jit(solution)/shard_map/ppermute | solution.py:855
  362.5 14.9 %collective-permute-start.10 = (bf16[272,128]{1,0:T(8,128)(2,1)}, bf16[272,128]{1,0:T(8,128)(2,1)S(1)}, u32[]{:S(2)}, u32[]{:S(2)}) collective-permute-start(bf16[272,128]{1,0:T(8,128)(2,1)} %get-tuple-element.171), channel_id=1, source_target_pairs={{0,2},{1,3},{2,0},{3,1},{4,6},{5,7},{6,4},{7,5},{8,10},{9,11},{10,... | collective-permute-start | bytes 208904 | tf_op jit(solution)/shard_map/ppermute | solution.py:855
  364.6 6.3 %collective-permute-start.9 = (bf16[272,128]{1,0:T(8,128)(2,1)}, bf16[272,128]{1,0:T(8,128)(2,1)S(1)}, u32[]{:S(2)}, u32[]{:S(2)}) collective-permute-start(bf16[272,128]{1,0:T(8,128)(2,1)} %get-tuple-element.171), channel_id=1, source_target_pairs={{0,1},{1,2},{2,3},{3,0},{4,5},{5,6},{6,7},{7,4},{8,9},{9,10},{10,1... | collective-permute-start | bytes 208904 | tf_op jit(solution)/shard_map/ppermute | solution.py:855
  367.5 9.9 %copy-start.29 = (bf16[272,128]{1,0:T(8,128)(2,1)S(1)}, bf16[272,128]{1,0:T(8,128)(2,1)}, u32[]{:S(2)}) copy-start(bf16[272,128]{1,0:T(8,128)(2,1)} %get-tuple-element.171) | copy-start | bytes 208900
  371.0 6.6 %copy-start.5 = (bf16[512,512]{1,0:T(8,128)(2,1)S(1)}, bf16[512,512]{1,0:T(8,128)(2,1)}, u32[]{:S(2)}) copy-start(bf16[512,512]{1,0:T(8,128)(2,1)} %shard_map.412) | copy-start | bytes 1572868
  382.3 19.3 %all-to-all-start.4 = ((bf16[8,480,128]{2,1,0:T(8,128)(2,1)}), bf16[8,480,128]{2,1,0:T(8,128)(2,1)S(1)}, u32[]{:S(2)}, u32[]{:S(2)}) async-start(bf16[8,480,128]{2,1,0:T(8,128)(2,1)} %copy.164), calls=%async_computation.8 | async-start | bytes 1966080 | tf_op jit(solution)/shard_map/all_to_all | solution.py:1265
  387.1 14.5 %copy-start.41 = (s32[8]{0:T(128)S(1)}, s32[8]{0:T(128)}, u32[]{:S(2)}) copy-start(s32[8]{0:T(128)} %param.57) | copy-start | bytes 100
  (19 other events, 69.3 us)
Sparse Core Ops, SparseCore 0:
  17.6 36.9 all-gather.2
  88.1 45.1 reduce-scatter.4
  218.0 53.4 reduce-scatter.6
  276.3 44.3 all-gather.4
  322.9 35.6 reduce-scatter.8
  366.4 44.1 reduce-scatter.10

commit v6 on v5

--- a/solution.py
+++ b/solution.py
@@ -89,7 +89,7 @@
     return jax.ShapeDtypeStruct(shape, dtype)
 
 
-def call(kernel, grid, in_specs, out_specs, out_shape, scratch, flops, moved):
+def call(kernel, grid, in_specs, out_specs, out_shape, scratch, flops, moved, grant=60):
     return pl.pallas_call(
         kernel,
         grid=grid,
@@ -98,7 +98,7 @@
         out_shape=out_shape,
         scratch_shapes=scratch,
         compiler_params=pltpu.CompilerParams(
-            vmem_limit_bytes=60 * 1024 * 1024,
+            vmem_limit_bytes=grant * 1024 * 1024,
             dimension_semantics=("arbitrary",) * len(grid) if grid else None,
         ),
         cost_estimate=pl.CostEstimate(
@@ -1233,6 +1233,7 @@
         [],
         2 * rows * LOW * D,
         24 * rows * D,
+        20,
     )(dx, own_rows(slopes), ga_own, tokens, gain1, router_first, dh1, routes_own)
 
     lane = jnp.arange(LOW, dtype=jnp.int32)

time: 426 us -> 426 us (level)
  transfers between devices with their start and end apart: 23 -> 23, of which waited for: 11 -> 10; matrix products, arithmetic and copies ran while one was open for 12% -> 11% of each run, Pallas kernels for 25% -> 24%
where the time goes in v6:
time: 426 us; the launch traced here: 422 us
  Pallas kernels  179 us (42%)
  waiting for transfers between devices  127 us (30%)
  local copies, waits for them, and re-layouts  42.1 us (10%)
  starting transfers between devices  41.9 us (10%)
  between operations  17.4 us (4%)
  other arithmetic  9.86 us (2%)
  matrix products  4.33 us (1%)
    reduce_scatter x1, waiting for transfers between devices, on_device(): attn = lax.psum_scatter(attn_part, 'shard', scatter_dimension=0, tiled=True)  44.7 us
    pallas_call x1, Pallas kernels, on_device(): call(lambda *refs: attention_back_kernel(shards, *refs), (steps_attn,), [...  40.7 us
    ppermute x12, waiting for transfers between devices, shifted(): return lax.ppermute(part, 'shard', pairs) if step else part  36 us
    pallas_call x1, Pallas kernels, on_device(): call(lambda *refs: attention_kernel(shards, *refs), (steps_attn,), [pl.Bl...  33.4 us
    pallas_call x1, Pallas kernels, on_device(): call(expert_down_kernel, (steps,), [whole()] * 6 + [kept, kept, far, tabl...  33.1 us
    pallas_call x1, Pallas kernels, on_device(): call(expert_rows_kernel, (parts,), [far, far, whole(), whole(), far, far,...  25.8 us
    pallas_call x1, Pallas kernels, on_device(): call(expert_up_kernel, (steps,), [whole()] * 4 + [far, far, table, table]...  23.8 us
    ppermute x12, starting transfers between devices, shifted(): return lax.ppermute(part, 'shard', pairs) if step else part  18.7 us
  transfers between devices with their start and end apart: 23, of which 10 were waited for; matrix products, arithmetic and copies ran while one was open for 11% of the time, Pallas kernels for 24%

profile of v6, /device:TPU:0, one launch (start us, length us, event | category | flops | bytes accessed | tf_op | source)
XLA Modules:
  0.0 421.6 jit_solution(4576457314277067207)
XLA Ops:
  7.3 1.3 fusion.2
  9.3 1.2 fusion.4
  10.6 5.1 %collective-permute-start.2 = (bf16[128,896]{1,0:T(8,128)(2,1)S(1)}, bf16[128,896]{1,0:T(8,128)(2,1)S(1)}, u32[]{:S(2)}, u32[]{:S(2)}) collective-permute-start(bf16[128,896]{1,0:T(8,128)(2,1)S(1)} %slice.140.refs_2_), channel_id=1, source_target_pairs={{0,3},{1,0},{2,1},{3,2},{4,7},{5,4},{6,5},{7,6},{8,11},{9,8},{10,9... | collective-permute-start | bytes 688136 | tf_op jit(solution)/shard_map/ppermute | solution.py:855
  18.1 1.6 convolution_convert_fusion
  19.7 4.4 %all-to-all-start = ((bf16[8,40,2048]{2,1,0:T(8,128)(2,1)}), bf16[8,40,2048]{2,1,0:T(8,128)(2,1)}, u32[]{:S(2)}, u32[]{:S(2)}) async-start(bf16[8,40,2048]{2,1,0:T(8,128)(2,1)} %bitcast.9), calls=%async_computation | async-start | bytes 2621440 | tf_op jit(solution)/shard_map/all_to_all | solution.py:914
  27.6 1.6 constant_dynamic-slice_fusion.2
  29.3 2.0 constant_dynamic-slice_fusion.4
  35.8 1.9 constant_dynamic-slice_fusion.5
  37.7 1.9 constant_dynamic-slice_fusion.6
  39.6 2.3 constant_dynamic-slice_fusion.7
  46.3 2.0 collective-permute-done.1.refs_4_
  48.3 6.3 %all-gather.3.cloned.1.call-done.refs_1_ = bf16[512,1152]{1,0:T(8,128)(2,1)} async-done(((bf16[128,1152]{1,0:T(8,128)(2,1)}), bf16[512,1152]{1,0:T(8,128)(2,1)}) %all-gather.3.cloned.1.call-update) | async-done | bytes 1179664 | tf_op jit(solution)/shard_map/all_gather | solution.py:858
  54.6 33.4 %shard_map.405 = (bf16[512,2048]{1,0:T(8,128)(2,1)}, bf16[512,128]{1,0:T(8,128)(2,1)}, bf16[1024,512]{1,0:T(8,128)(2,1)}, bf16[512,512]{1,0:T(8,128)(2,1)}, bf16...) custom-call(s32[4]{0:T(128)} %copy-done.41, ...), custom_call_target="tpu_custom_call" | custom-call | flops 68719476736 | bytes 134217728 | tf_op jit(solution)/shard_map/pallas_call | solution.py:945
  88.7 44.7 %reduce-scatter.5.cloned.1.call-done.refs_0_.refs_1_.attn = bf16[128,2048]{1,0:T(8,128)(2,1)} async-done(((bf16[512,2048]{1,0:T(8,128)(2,1)}), bf16[128,2048]{1,0:T(8,128)(2,1)}) %reduce-scatter.5.cloned.1.call-update) | async-done | bytes 524304 | tf_op jit(solution)/shard_map/reduce_scatter | solution.py:979
  133.3 3.3 shard_map.406
  136.6 4.4 %all-to-all-start.1 = ((bf16[8,40,2176]{2,1,0:T(8,128)(2,1)}), bf16[8,40,2176]{2,1,0:T(8,128)(2,1)}, u32[]{:S(2)}, u32[]{:S(2)}) async-start(bf16[8,40,2176]{2,1,0:T(8,128)(2,1)} %bitcast.155), calls=%async_computation.2 | async-start | bytes 2785280 | tf_op jit(solution)/shard_map/all_to_all | solution.py:914
  144.6 1.5 collective-permute-start.5
  146.6 1.8 collective-permute-start.4
  148.4 11.8 %all-to-all-done.1 = bf16[8,40,2176]{2,1,0:T(8,128)(2,1)} async-done(((bf16[8,40,2176]{2,1,0:T(8,128)(2,1)}), bf16[8,40,2176]{2,1,0:T(8,128)(2,1)}, u32[]{:S(2)}, u32[]{:S(2)}) %all-to-all-start.1) | async-done | bytes 1392672 | tf_op jit(solution)/shard_map/all_to_all | solution.py:914
  160.2 23.8 %shard_map.407 = (bf16[320,5632]{1,0:T(8,128)(2,1)}, bf16[320,5632]{1,0:T(8,128)(2,1)}, bf16[320,128]{1,0:T(8,128)(2,1)}, bf16[320,128]{1,0:T(8,128)(2,1)}) custom-call(bf16[320,2176]{1,0:T(8,128)(2,1)} %bitcast.25.x, bf16[320,128]{1,0:T(8,128)(2,1)} %compare_convert_fusion.mask, bf16[128,2048]{1,0:T(8,128)(2,1)} %bitcast.170, bf16[128,2048]{1,0:T(8,128)(2,1)} %bitcast.168, ...), custom_call_target="tpu_custom_call" | custom-call | flops 59055800320 | bytes 184549376 | tf_op jit(solution)/shard_map/pallas_call | solution.py:1031
  184.0 33.1 %shard_map.408 = (bf16[320,2176]{1,0:T(8,128)(2,1)}, bf16[320,5632]{1,0:T(8,128)(2,1)}, bf16[320,5632]{1,0:T(8,128)(2,1)}, bf16[320,128]{1,0:T(8,128)(2,1)}, bf1...) custom-call(bf16[320,2048]{1,0:T(8,128)(2,1)} %bitcast.10.grads, ...), custom_call_target="tpu_custom_call" | custom-call | flops 59055800320 | bytes 92274688 | tf_op jit(solution)/shard_map/pallas_call | solution.py:1059
  217.1 4.0 all-to-all-start.2
  221.1 25.8 %shard_map.410 = bf16[320,2176]{1,0:T(8,128)(2,1)} custom-call(bf16[320,5632]{1,0:T(8,128)(2,1)} %get-tuple-element.135.dg_far, bf16[320,5632]{1,0:T(8,128)(2,1)} %get-tuple-element.136.du_far, bf16[320,128]{1,0:T(8,128)(2,1)} %get-tuple-element.137.dlg, bf16[320,128]{1,0:T(8,128)(2,1)} %get-tuple-element.138.dlu, bf16[2048,5632]{1,0:T(8,128)(2,1)} %gate_far.3, ...), custom_call_target="tpu_custom_call" | custom-call | flops 59055800320 | bytes 184549376 | tf_op jit(solution)/shard_map/pallas_call | solution.py:1091
  246.9 1.1 copy-done.12
  248.0 4.2 all-to-all-start.3
  253.0 3.8 shard_map.409
  256.8 14.5 %all-to-all-done.3 = bf16[8,40,2176]{2,1,0:T(8,128)(2,1)S(1)} async-done(((bf16[8,40,2176]{2,1,0:T(8,128)(2,1)}), bf16[8,40,2176]{2,1,0:T(8,128)(2,1)S(1)}, u32[]{:S(2)}, u32[]{:S(2)}) %all-to-all-start.3) | async-done | bytes 1392672 | tf_op jit(solution)/shard_map/all_to_all | solution.py:997
  271.3 1.1 copy-done.6
  272.4 3.8 shard_map.411
  276.4 1.8 collective-permute-start.8
  278.5 1.9 collective-permute-start.6
  280.5 1.2 slice.147.refs_7_
  282.8 3.9 shard_map.412
  286.7 1.5 collective-permute-done.8.refs_5_
  288.2 29.1 %collective-permute-done.7.refs_4_ = bf16[128,1024]{1,0:T(8,128)(2,1)S(1)} collective-permute-done((bf16[128,1024]{1,0:T(8,128)(2,1)}, bf16[128,1024]{1,0:T(8,128)(2,1)S(1)}, u32[]{:S(2)}, u32[]{:S(2)}) %collective-permute-start.7) | collective-permute-done | bytes 262176 | tf_op jit(solution)/shard_map/ppermute | solution.py:855
  318.4 40.7 %shard_map.413 = (bf16[512,2048]{1,0:T(8,128)(2,1)}, bf16[272,128]{1,0:T(8,128)(2,1)}, bf16[128,512]{1,0:T(8,128)(2,1)}, bf16[128,512]{1,0:T(8,128)(2,1)}, bf16[256,512]{1,0:T(8,128)(2,1)}) custom-call(s32[4]{0:T(128)} %copy-done.41, bf16[512,1152]{1,0:T(8,128)(2,1)} %all-gather.5.cloned.1.call-done.refs_1_, bf16[128,1024]{1,0:T(8,128)(2,1)} %get-tuple-element.185.refs_2_, ...), custom_call_target="tpu_custom_call" | custom-call | flops 68719476736 | bytes 134217728 | tf_op jit(solution)/shard_map/pallas_call | solution.py:1154
  359.2 1.9 collective-permute-start.11
  362.1 1.9 collective-permute-start.9
  365.4 3.3 collective-permute-done.9
  368.7 5.3 %shard_map.415 = (bf16[384,512]{1,0:T(8,128)(2,1)}, bf16[128,512]{1,0:T(8,128)(2,1)}) custom-call(s32[5]{0:T(128)} %pad_add_fusion.refs_0_, bf16[512,1152]{1,0:T(8,128)(2,1)} %all-gather.5.cloned.1.call-done.refs_1_, bf16[128,1024]{1,0:T(8,128)(2,1)} %get-tuple-element.185.refs_2_, bf16[128,1024]{1,0:T(8,128)(2,1)} %copy-done.21, ...), custom_call_target="tpu_custom_call" | custom-call | tf_op jit(solution)/shard_map/pallas_call | solution.py:1206
  378.9 1.1 copy.164
  380.0 5.7 %all-to-all-start.4 = ((bf16[8,480,128]{2,1,0:T(8,128)(2,1)}), bf16[8,480,128]{2,1,0:T(8,128)(2,1)S(1)}, u32[]{:S(2)}, u32[]{:S(2)}) async-start(bf16[8,480,128]{2,1,0:T(8,128)(2,1)} %copy.164), calls=%async_computation.8 | async-start | bytes 1966080 | tf_op jit(solution)/shard_map/all_to_all | solution.py:1266
  385.9 1.4 fusion.39
  387.4 13.0 %all-to-all-done.4 = bf16[8,480,128]{2,1,0:T(8,128)(2,1)S(1)} async-done(((bf16[8,480,128]{2,1,0:T(8,128)(2,1)}), bf16[8,480,128]{2,1,0:T(8,128)(2,1)S(1)}, u32[]{:S(2)}, u32[]{:S(2)}) %all-to-all-start.4) | async-done | bytes 983072 | tf_op jit(solution)/shard_map/all_to_all | solution.py:1266
  401.4 1.8 fusion.5
  403.4 1.0 copy-done.5
  410.5 1.2 fusion.42
  412.8 1.7 shard_map.414
  (237 shorter events, 37.1 us)
Async XLA Ops:
  7.2 19.8 %copy-start = (bf16[8,8,16,512]{3,2,1,0:T(8,128)(2,1)S(1)}, bf16[8,8,16,512]{3,2,1,0:T(8,128)(2,1)}, u32[]{:S(2)}) copy-start(bf16[8,8,16,512]{3,2,1,0:T(8,128)(2,1)} %param.44) | copy-start | bytes 3145732
  7.2 10.3 %copy-start.33 = (s32[128,2]{0,1:T(2,128)S(1)}, s32[128,2]{0,1:T(2,128)}, u32[]{:S(2)}) copy-start(s32[128,2]{0,1:T(2,128)} %param.59) | copy-start | bytes 3076
  7.2 10.9 %copy-start.7 = (bf16[128,2048]{1,0:T(8,128)(2,1)S(1)}, bf16[128,2048]{1,0:T(8,128)(2,1)}, u32[]{:S(2)}) copy-start(bf16[128,2048]{1,0:T(8,128)(2,1)} %cot.1) | copy-start | bytes 1572868
  7.2 47.3 %all-gather.3.cloned.1.call-start = ((), (), s32[]{:S(2)}) async-start(), calls=%async_computation.9 | async-start | bytes 1474560 | tf_op jit(solution)/shard_map/all_gather | solution.py:858
  10.6 9.1 %copy-start.13 = (bf16[128,896]{1,0:T(8,128)(2,1)}, bf16[128,896]{1,0:T(8,128)(2,1)S(1)}, u32[]{:S(2)}) copy-start(bf16[128,896]{1,0:T(8,128)(2,1)S(1)} %slice.140.refs_2_) | copy-start | bytes 688132
  10.6 35.7 %collective-permute-start.2 = (bf16[128,896]{1,0:T(8,128)(2,1)S(1)}, bf16[128,896]{1,0:T(8,128)(2,1)S(1)}, u32[]{:S(2)}, u32[]{:S(2)}) collective-permute-start(bf16[128,896]{1,0:T(8,128)(2,1)S(1)} %slice.140.refs_2_), channel_id=1, source_target_pairs={{0,3},{1,0},{2,1},{3,2},{4,7},{5,4},{6,5},{7,6},{8,11},{9,8},{10,9... | collective-permute-start | bytes 688136 | tf_op jit(solution)/shard_map/ppermute | solution.py:855
  15.7 32.6 %collective-permute-start.1 = (bf16[128,896]{1,0:T(8,128)(2,1)S(1)}, bf16[128,896]{1,0:T(8,128)(2,1)S(1)}, u32[]{:S(2)}, u32[]{:S(2)}) collective-permute-start(bf16[128,896]{1,0:T(8,128)(2,1)S(1)} %slice.140.refs_2_), channel_id=1, source_target_pairs={{0,2},{1,3},{2,0},{3,1},{4,6},{5,7},{6,4},{7,5},{8,10},{9,11},{10,... | collective-permute-start | bytes 688136 | tf_op jit(solution)/shard_map/ppermute | solution.py:855
  15.7 32.6 %collective-permute-start = (bf16[128,896]{1,0:T(8,128)(2,1)S(1)}, bf16[128,896]{1,0:T(8,128)(2,1)S(1)}, u32[]{:S(2)}, u32[]{:S(2)}) collective-permute-start(bf16[128,896]{1,0:T(8,128)(2,1)S(1)} %slice.140.refs_2_), channel_id=1, source_target_pairs={{0,1},{1,2},{2,3},{3,0},{4,5},{5,6},{6,7},{7,4},{8,9},{9,10},{10,1... | collective-permute-start | bytes 688136 | tf_op jit(solution)/shard_map/ppermute | solution.py:855
  17.9 70.1 %copy-start.10 = (s32[128,2]{1,0:T(8,128)}, s32[128,2]{1,0:T(8,128)S(1)}, u32[]{:S(2)}) copy-start(s32[128,2]{1,0:T(8,128)S(1)} %add.130.refs_5_.mcol) | copy-start | bytes 3076
  18.1 6.1 %copy-start.39 = (s32[8]{0:T(128)S(1)}, s32[8]{0:T(128)}, u32[]{:S(2)}) copy-start(s32[8]{0:T(128)} %param.57) | copy-start | bytes 100
  19.7 9.5 %copy-start.31 = (s32[512,2]{0,1:T(2,128)S(1)}, s32[512,2]{0,1:T(2,128)}, u32[]{:S(2)}) copy-start(s32[512,2]{0,1:T(2,128)} %param.58) | copy-start | bytes 12292
  19.7 28.6 %all-to-all-start = ((bf16[8,40,2048]{2,1,0:T(8,128)(2,1)}), bf16[8,40,2048]{2,1,0:T(8,128)(2,1)}, u32[]{:S(2)}, u32[]{:S(2)}) async-start(bf16[8,40,2048]{2,1,0:T(8,128)(2,1)} %bitcast.9), calls=%async_computation | async-start | bytes 2621440 | tf_op jit(solution)/shard_map/all_to_all | solution.py:914
  24.1 109.2 %reduce-scatter.5.cloned.1.call-start = ((), (), s32[]{:S(2)}) async-start(), calls=%async_computation.10 | async-start | bytes 2621440 | tf_op jit(solution)/shard_map/reduce_scatter | solution.py:979
  29.3 8.4 %copy-start.16 = (s32[512,2]{1,0:T(8,128)}, s32[512,2]{1,0:T(8,128)S(1)}, u32[]{:S(2)}) copy-start(s32[512,2]{1,0:T(8,128)S(1)} %copy.138.refs_16_.refs_17_) | copy-start | bytes 12292
  35.8 6.1 %copy-start.25 = (bf16[2048,8]{0,1:T(8,128)(2,1)S(1)}, bf16[2048,8]{0,1:T(8,128)(2,1)}, u32[]{:S(2)}) copy-start(bf16[2048,8]{0,1:T(8,128)(2,1)} %param.34) | copy-start | bytes 98308
  37.7 5.8 %copy-start.35 = (bf16[2048]{0:T(1024)(128)(2,1)S(1)}, bf16[2048]{0:T(1024)(128)(2,1)}, u32[]{:S(2)}) copy-start(bf16[2048]{0:T(1024)(128)(2,1)} %param.32) | copy-start | bytes 12292
  37.7 5.9 %copy-start.36 = (bf16[2048]{0:T(1024)(128)(2,1)S(1)}, bf16[2048]{0:T(1024)(128)(2,1)}, u32[]{:S(2)}) copy-start(bf16[2048]{0:T(1024)(128)(2,1)} %param.33) | copy-start | bytes 12292
  37.7 6.5 %copy-start.30 = (bf16[2048,8]{0,1:T(8,128)(2,1)S(1)}, bf16[2048,8]{0,1:T(8,128)(2,1)}, u32[]{:S(2)}) copy-start(bf16[2048,8]{0,1:T(8,128)(2,1)} %param.35) | copy-start | bytes 98308
  39.6 14.9 %copy-start.41 = (s32[4]{0:T(128)}, s32[4]{0:T(128)S(1)}, u32[]{:S(2)}) copy-start(s32[4]{0:T(128)S(1)} %compare_select_fusion.refs_0_) | copy-start | bytes 52
  46.3 8.3 %copy-start.22 = (bf16[128,896]{1,0:T(8,128)(2,1)}, bf16[128,896]{1,0:T(8,128)(2,1)S(1)}, u32[]{:S(2)}) copy-start(bf16[128,896]{1,0:T(8,128)(2,1)S(1)} %collective-permute-done.2.refs_5_) | copy-start | bytes 688132
  48.3 6.3 %copy-start.23 = (bf16[128,896]{1,0:T(8,128)(2,1)}, bf16[128,896]{1,0:T(8,128)(2,1)S(1)}, u32[]{:S(2)}) copy-start(bf16[128,896]{1,0:T(8,128)(2,1)S(1)} %collective-permute-done.1.refs_4_) | copy-start | bytes 688132
  48.3 6.3 %copy-start.24 = (bf16[128,896]{1,0:T(8,128)(2,1)}, bf16[128,896]{1,0:T(8,128)(2,1)S(1)}, u32[]{:S(2)}) copy-start(bf16[128,896]{1,0:T(8,128)(2,1)S(1)} %collective-permute-done.refs_3_) | copy-start | bytes 688132
  136.6 23.5 %all-to-all-start.1 = ((bf16[8,40,2176]{2,1,0:T(8,128)(2,1)}), bf16[8,40,2176]{2,1,0:T(8,128)(2,1)}, u32[]{:S(2)}, u32[]{:S(2)}) async-start(bf16[8,40,2176]{2,1,0:T(8,128)(2,1)} %bitcast.155), calls=%async_computation.2 | async-start | bytes 2785280 | tf_op jit(solution)/shard_map/all_to_all | solution.py:914
  141.1 130.3 %reduce-scatter.7.cloned.1.call-start = ((), (), s32[]{:S(2)}) async-start(), calls=%async_computation.11 | async-start | bytes 3440640 | tf_op jit(solution)/shard_map/reduce_scatter | solution.py:1083
  144.6 39.3 %collective-permute-start.5 = (bf16[128,1536]{1,0:T(8,128)(2,1)S(1)}, bf16[128,1536]{1,0:T(8,128)(2,1)S(1)}, u32[]{:S(2)}, u32[]{:S(2)}) collective-permute-start(bf16[128,1536]{1,0:T(8,128)(2,1)S(1)} %get-tuple-element.224), channel_id=1, source_target_pairs={{0,3},{1,0},{2,1},{3,2},{4,7},{5,4},{6,5},{7,6},{8,11},{9,8},{10,9... | collective-permute-start | bytes 1179656 | tf_op jit(solution)/shard_map/ppermute | solution.py:855
  146.1 37.8 %collective-permute-start.3 = (bf16[128,1536]{1,0:T(8,128)(2,1)S(1)}, bf16[128,1536]{1,0:T(8,128)(2,1)S(1)}, u32[]{:S(2)}, u32[]{:S(2)}) collective-permute-start(bf16[128,1536]{1,0:T(8,128)(2,1)S(1)} %get-tuple-element.225), channel_id=1, source_target_pairs={{0,1},{1,2},{2,3},{3,0},{4,5},{5,6},{6,7},{7,4},{8,9},{9,10},{10,1... | collective-permute-start | bytes 1179656 | tf_op jit(solution)/shard_map/ppermute | solution.py:855
  146.6 37.3 %collective-permute-start.4 = (bf16[128,1536]{1,0:T(8,128)(2,1)S(1)}, bf16[128,1536]{1,0:T(8,128)(2,1)S(1)}, u32[]{:S(2)}, u32[]{:S(2)}) collective-permute-start(bf16[128,1536]{1,0:T(8,128)(2,1)S(1)} %get-tuple-element.226), channel_id=1, source_target_pairs={{0,2},{1,3},{2,0},{3,1},{4,6},{5,7},{6,4},{7,5},{8,10},{9,11},{10,... | collective-permute-start | bytes 1179656 | tf_op jit(solution)/shard_map/ppermute | solution.py:855
  217.1 29.8 %all-to-all-start.2 = ((bf16[8,40,2176]{2,1,0:T(8,128)(2,1)}), bf16[8,40,2176]{2,1,0:T(8,128)(2,1)S(1)}, u32[]{:S(2)}, u32[]{:S(2)}) async-start(bf16[8,40,2176]{2,1,0:T(8,128)(2,1)} %bitcast.42), calls=%async_computation.3 | async-start | bytes 2785280 | tf_op jit(solution)/shard_map/all_to_all | solution.py:997
  248.0 23.3 %all-to-all-start.3 = ((bf16[8,40,2176]{2,1,0:T(8,128)(2,1)}), bf16[8,40,2176]{2,1,0:T(8,128)(2,1)S(1)}, u32[]{:S(2)}, u32[]{:S(2)}) async-start(bf16[8,40,2176]{2,1,0:T(8,128)(2,1)} %bitcast.157), calls=%async_computation.4 | async-start | bytes 2785280 | tf_op jit(solution)/shard_map/all_to_all | solution.py:997
  252.2 66.1 %all-gather.5.cloned.1.call-start = ((), (), s32[]{:S(2)}) async-start(), calls=%async_computation.12 | async-start | bytes 1474560 | tf_op jit(solution)/shard_map/all_gather | solution.py:858
  256.8 19.5 %copy-start.32 = (s32[512,2]{0,1:T(2,128)S(1)}, s32[512,2]{0,1:T(2,128)}, u32[]{:S(2)}) copy-start(s32[512,2]{0,1:T(2,128)} %param.58) | copy-start | bytes 12292
  256.8 19.6 %copy-start.11 = (bf16[128,1536]{1,0:T(8,128)(2,1)S(1)}, bf16[128,1536]{1,0:T(8,128)(2,1)}, u32[]{:S(2)}) copy-start(bf16[128,1536]{1,0:T(8,128)(2,1)} %get-tuple-element.189) | copy-start | bytes 1179652
  276.3 82.9 %reduce-scatter.9.cloned.1.call-start = ((), (), s32[]{:S(2)}) async-start(), calls=%async_computation.13 | async-start | bytes 1966080 | tf_op jit(solution)/shard_map/reduce_scatter | solution.py:1083
  276.4 11.8 %collective-permute-start.8 = (bf16[128,1024]{1,0:T(8,128)(2,1)}, bf16[128,1024]{1,0:T(8,128)(2,1)S(1)}, u32[]{:S(2)}, u32[]{:S(2)}) collective-permute-start(bf16[128,1024]{1,0:T(8,128)(2,1)} %get-tuple-element.185.refs_2_), channel_id=1, source_target_pairs={{0,3},{1,0},{2,1},{3,2},{4,7},{5,4},{6,5},{7,6},{8,11},{9,8},{10,9... | collective-permute-start | bytes 786440 | tf_op jit(solution)/shard_map/ppermute | solution.py:855
  278.2 39.1 %collective-permute-start.7 = (bf16[128,1024]{1,0:T(8,128)(2,1)}, bf16[128,1024]{1,0:T(8,128)(2,1)S(1)}, u32[]{:S(2)}, u32[]{:S(2)}) collective-permute-start(bf16[128,1024]{1,0:T(8,128)(2,1)} %get-tuple-element.185.refs_2_), channel_id=1, source_target_pairs={{0,2},{1,3},{2,0},{3,1},{4,6},{5,7},{6,4},{7,5},{8,10},{9,11},{10,... | collective-permute-start | bytes 786440 | tf_op jit(solution)/shard_map/ppermute | solution.py:855
  278.5 38.9 %collective-permute-start.6 = (bf16[128,1024]{1,0:T(8,128)(2,1)}, bf16[128,1024]{1,0:T(8,128)(2,1)S(1)}, u32[]{:S(2)}, u32[]{:S(2)}) collective-permute-start(bf16[128,1024]{1,0:T(8,128)(2,1)} %get-tuple-element.185.refs_2_), channel_id=1, source_target_pairs={{0,1},{1,2},{2,3},{3,0},{4,5},{5,6},{6,7},{7,4},{8,9},{9,10},{10,1... | collective-permute-start | bytes 786440 | tf_op jit(solution)/shard_map/ppermute | solution.py:855
  288.2 30.2 %copy-start.19 = (bf16[128,1024]{1,0:T(8,128)(2,1)}, bf16[128,1024]{1,0:T(8,128)(2,1)S(1)}, u32[]{:S(2)}) copy-start(bf16[128,1024]{1,0:T(8,128)(2,1)S(1)} %collective-permute-done.8.refs_5_) | copy-start | bytes 786436
  318.3 93.4 %reduce-scatter.11.cloned.1.call-start = ((), (), s32[]{:S(2)}) async-start(), calls=%async_computation.14 | async-start | bytes 2621440 | tf_op jit(solution)/shard_map/reduce_scatter | solution.py:1225
  359.1 5.7 %copy-start.28 = (bf16[128,512]{1,0:T(8,128)(2,1)S(1)}, bf16[128,512]{1,0:T(8,128)(2,1)}, u32[]{:S(2)}) copy-start(bf16[128,512]{1,0:T(8,128)(2,1)} %get-tuple-element.194) | copy-start | bytes 393220
  359.1 6.0 %copy-start.27 = (bf16[128,512]{1,0:T(8,128)(2,1)S(1)}, bf16[128,512]{1,0:T(8,128)(2,1)}, u32[]{:S(2)}) copy-start(bf16[128,512]{1,0:T(8,128)(2,1)} %get-tuple-element.195) | copy-start | bytes 393220
  359.2 15.9 %collective-permute-start.11 = (bf16[272,128]{1,0:T(8,128)(2,1)}, bf16[272,128]{1,0:T(8,128)(2,1)S(1)}, u32[]{:S(2)}, u32[]{:S(2)}) collective-permute-start(bf16[272,128]{1,0:T(8,128)(2,1)} %get-tuple-element.171), channel_id=1, source_target_pairs={{0,3},{1,0},{2,1},{3,2},{4,7},{5,4},{6,5},{7,6},{8,11},{9,8},{10,9... | collective-permute-start | bytes 208904 | tf_op jit(solution)/shard_map/ppermute | solution.py:855
  361.1 14.0 %collective-permute-start.10 = (bf16[272,128]{1,0:T(8,128)(2,1)}, bf16[272,128]{1,0:T(8,128)(2,1)S(1)}, u32[]{:S(2)}, u32[]{:S(2)}) collective-permute-start(bf16[272,128]{1,0:T(8,128)(2,1)} %get-tuple-element.171), channel_id=1, source_target_pairs={{0,2},{1,3},{2,0},{3,1},{4,6},{5,7},{6,4},{7,5},{8,10},{9,11},{10,... | collective-permute-start | bytes 208904 | tf_op jit(solution)/shard_map/ppermute | solution.py:855
  362.1 6.7 %collective-permute-start.9 = (bf16[272,128]{1,0:T(8,128)(2,1)}, bf16[272,128]{1,0:T(8,128)(2,1)S(1)}, u32[]{:S(2)}, u32[]{:S(2)}) collective-permute-start(bf16[272,128]{1,0:T(8,128)(2,1)} %get-tuple-element.171), channel_id=1, source_target_pairs={{0,1},{1,2},{2,3},{3,0},{4,5},{5,6},{6,7},{7,4},{8,9},{9,10},{10,1... | collective-permute-start | bytes 208904 | tf_op jit(solution)/shard_map/ppermute | solution.py:855
  365.3 9.8 %copy-start.29 = (bf16[272,128]{1,0:T(8,128)(2,1)S(1)}, bf16[272,128]{1,0:T(8,128)(2,1)}, u32[]{:S(2)}) copy-start(bf16[272,128]{1,0:T(8,128)(2,1)} %get-tuple-element.171) | copy-start | bytes 208900
  368.7 6.5 %copy-start.8 = (bf16[512,512]{1,0:T(8,128)(2,1)S(1)}, bf16[512,512]{1,0:T(8,128)(2,1)}, u32[]{:S(2)}) copy-start(bf16[512,512]{1,0:T(8,128)(2,1)} %shard_map.412) | copy-start | bytes 1572868
  378.9 6.8 %copy-start.17 = (bf16[384,512]{1,0:T(8,128)(2,1)S(1)}, bf16[384,512]{1,0:T(8,128)(2,1)}, u32[]{:S(2)}) copy-start(bf16[384,512]{1,0:T(8,128)(2,1)} %reduce-scatter.9.cloned.1.call-done) | copy-start | bytes 1179652
  380.0 20.4 %all-to-all-start.4 = ((bf16[8,480,128]{2,1,0:T(8,128)(2,1)}), bf16[8,480,128]{2,1,0:T(8,128)(2,1)S(1)}, u32[]{:S(2)}, u32[]{:S(2)}) async-start(bf16[8,480,128]{2,1,0:T(8,128)(2,1)} %copy.164), calls=%async_computation.8 | async-start | bytes 1966080 | tf_op jit(solution)/shard_map/all_to_all | solution.py:1266
  385.9 15.5 %copy-start.40 = (s32[8]{0:T(128)S(1)}, s32[8]{0:T(128)}, u32[]{:S(2)}) copy-start(s32[8]{0:T(128)} %param.57) | copy-start | bytes 100
  (18 other events, 46.9 us)
Sparse Core Ops, SparseCore 0:
  17.6 36.9 all-gather.2
  88.1 45.1 reduce-scatter.4
  217.3 51.9 reduce-scatter.6
  276.4 41.8 all-gather.4
  320.6 36.7 reduce-scatter.8
  364.2 45.3 reduce-scatter.10
